TPU v7x, 512 devices: a whole 4x4x16 slice. The times are simulated.
512 devices in a mesh: group: 16 (over x, y_hi, core), blk: 32 (over y_lo, z).
Axes of the slice: x: 4, y: 4 (y_hi: 2, y_lo: 2; y = y_hi * 2 + y_lo), z: 16, core: 2. Of those that a mesh axis runs over, the one named last changes fastest.
Arguments:
- tokens: bfloat16 [16384, 2048], P(('group', 'blk')), may hold values from -6 to 6
- expert_ids: int32 [16384, 4], P(('group', 'blk')), may hold values from 0 to 127, all different within a row; in each aligned block of 32 rows (0 to 31, 32 to 63, ...) at most 2 rows name the same one
- grad_hidden: bfloat16 [16384, 4, 768], P(('group', 'blk')), may hold values from -6 to 6
- gate_blocks: bfloat16 [512, 192, 2048], P(('group', 'blk')), may hold values from -0.125 to 0.125
- up_blocks: bfloat16 [512, 192, 2048], P(('group', 'blk')), may hold values from -0.125 to 0.125
Outputs:
- hidden_out: bfloat16 [16384, 4, 768], P(('group', 'blk'))
- grad_tokens: bfloat16 [16384, 2048], P(('group', 'blk'))
- grad_gate: bfloat16 [512, 192, 2048], P(('group', 'blk'))
- grad_up: bfloat16 [512, 192, 2048], P(('group', 'blk'))
Inputs may be any that keep to these rules, and one draw needn't show every extreme that they name: `expert_ids`: each row names 4 different experts. Among the rows of one device no expert is named by more than 2 rows, and in every draw some expert is named by exactly 2 rows of some device.
All inputs are finite; a program needn't handle non-finite values.
Results may differ from a plain program's by a relative error of at most 0.0058.
Values may be sent and summed in bfloat16 or wider, within the bound.
No kernel may reach another device: no remote copies, remote signals or barrier semaphores. Data moves between devices by JAX's collectives and lax.ppermute only.
A program may use at most 64 MiB of HBM per device.

v0:
```python
import jax
import jax.numpy as jnp
from jax import lax
from jax.sharding import PartitionSpec as P

D = 2048
FF = 768
TOPK = 4
SUB = 4


def partner_2(block, axis, bit):
    count = lax.axis_size(axis)
    route = []
    for low in range(count):
        high = low | 1 << bit
        if high != low and high < count:
            route += [(low, high), (high, low)]
    return lax.ppermute(block, axis, route)


def contract_rows(left, right):
    return lax.dot_general(
        left, right, (((0,), (0,)), ((), ())), preferred_element_type=jnp.float32
    )


def contract_last(left, right):
    return lax.dot_general(
        left, right, (((1,), (1,)), ((), ())), preferred_element_type=jnp.float32
    )


def upper_half(level):
    return lax.axis_index("blk") >> level & 1 == 1


def over_groups(payload):
    return (
        lax.all_to_all(payload[0], "group", split_axis=0, concat_axis=0, tiled=True),
        lax.all_to_all(payload[1], "group", split_axis=0, concat_axis=0, tiled=True),
    )


def over_blocks(payload):
    return (
        lax.all_to_all(payload[0], "blk", split_axis=0, concat_axis=0, tiled=True),
        lax.all_to_all(payload[1], "blk", split_axis=0, concat_axis=0, tiled=True),
    )


def to_blocks(values, group_count, local_experts, capacity):
    last_width = values.shape[-1]
    values = values.reshape(group_count, local_experts, capacity, last_width).transpose(1, 0, 2, 3)
    return values.reshape(local_experts * SUB, group_count * capacity // SUB, last_width)


def from_blocks(values, group_count, local_experts, capacity):
    last_width = values.shape[-1]
    values = values.reshape(local_experts, group_count, capacity, last_width).transpose(1, 0, 2, 3)
    return values.reshape(group_count, local_experts * capacity, last_width)


def gather_members(rows_local):
    gathered = rows_local
    for level in range(SUB.bit_length() - 1):
        partner = partner_2(gathered, "blk", level)
        gathered = jnp.where(
            upper_half(level),
            jnp.concatenate([partner, gathered], 0),
            jnp.concatenate([gathered, partner], 0),
        )
    return gathered


def spread_members(holding, sender):
    layout = holding.shape
    for level in range(SUB.bit_length() - 1):
        halves = holding.reshape((SUB >> level + 1, 2, 1 << level) + layout[1:])
        lower = halves[:, 0]
        higher = halves[:, 1]
        upper_side = upper_half(level)
        incoming = sender(jnp.where(upper_side, lower, higher), level)
        kept_half = jnp.where(upper_side, higher, lower)
        new_lower = jnp.where(upper_side, incoming, kept_half)
        new_higher = jnp.where(upper_side, kept_half, incoming)
        holding = jnp.stack([new_lower, new_higher], axis=1).reshape(layout)
    return holding


def swiglu_pieces(x_rows, dh_rows, w_gate, w_up):
    gate_pre = contract_last(x_rows, w_gate)
    up_pre = contract_last(x_rows, w_up)
    sigmoid_gate = jax.nn.sigmoid(gate_pre)
    active = gate_pre * sigmoid_gate
    hidden = (active * up_pre).astype(jnp.bfloat16)
    upstream = dh_rows.astype(jnp.float32)
    d_gate = (upstream * up_pre * sigmoid_gate * (1.0 + gate_pre * (1.0 - sigmoid_gate))).astype(
        jnp.bfloat16
    )
    d_up = (upstream * active).astype(jnp.bfloat16)
    return (hidden, d_gate, d_up)


def on_device(tokens, expert_ids, grad_hidden, gate_blocks, up_blocks):
    tokens_here = tokens.shape[0]
    group_count = lax.axis_size("group")
    block_count = lax.axis_size("blk")
    local_experts = block_count // SUB
    expert_count = group_count * local_experts
    capacity = max(2, (4 * tokens_here * TOPK + 3 * expert_count - 1) // (3 * expert_count))
    pair_count = tokens_here * TOPK
    slot_count = expert_count * capacity
    flat_ids = expert_ids.reshape(pair_count)
    onehot = (flat_ids[:, None] == jnp.arange(expert_count, dtype=jnp.int32)[None, :]).astype(
        jnp.int32
    )
    rank_pair = jnp.sum((jnp.cumsum(onehot, axis=0) - onehot) * onehot, axis=1)
    slot_index = flat_ids * capacity + rank_pair
    placing = (slot_index[None, :] == jnp.arange(slot_count, dtype=jnp.int32)[:, None]).astype(
        jnp.bfloat16
    )
    token_picks = placing.reshape(slot_count, tokens_here, TOPK).sum(axis=2)
    x_send = jnp.dot(token_picks, tokens, preferred_element_type=jnp.float32).astype(jnp.bfloat16)
    dh_send = jnp.dot(
        placing, grad_hidden.reshape(pair_count, FF), preferred_element_type=jnp.float32
    ).astype(jnp.bfloat16)
    x_group, dh_group = over_groups(
        (
            x_send.reshape(group_count, local_experts * capacity, D),
            dh_send.reshape(group_count, local_experts * capacity, FF),
        )
    )
    x_mine, dh_mine = over_blocks(
        (
            to_blocks(x_group, group_count, local_experts, capacity),
            to_blocks(dh_group, group_count, local_experts, capacity),
        )
    )
    row_count = x_mine.shape[0] * x_mine.shape[1]
    x_mine = x_mine.reshape(row_count, D)
    dh_mine = dh_mine.reshape(row_count, FF)
    x_all = gather_members(x_mine)
    w_gate = gate_blocks[0]
    w_up = up_blocks[0]
    ff_block = w_gate.shape[0]

    def swap_blocks(outgoing, level):
        return partner_2(outgoing, "blk", level)

    dh_parts = dh_mine.reshape(row_count, SUB, ff_block).transpose(1, 0, 2)
    dh_all = spread_members(dh_parts, swap_blocks).reshape(SUB * row_count, ff_block)
    hidden, d_gate, d_up = swiglu_pieces(x_all, dh_all, w_gate, w_up)
    h_parts = spread_members(hidden.reshape(SUB, row_count, ff_block), swap_blocks)
    h_mine = h_parts.transpose(1, 0, 2).reshape(row_count, FF)
    partial_value = jnp.dot(d_gate, w_gate, preferred_element_type=jnp.float32) + jnp.dot(
        d_up, w_up, preferred_element_type=jnp.float32
    )
    fold_partial_value = partial_value.reshape(SUB, row_count, D)
    holding = fold_partial_value
    for level in reversed(range(SUB.bit_length() - 1)):
        middle = holding.shape[0] // 2
        upper_side = upper_half(level)
        outgoing = jnp.where(upper_side, holding[:middle], holding[middle:])
        kept_half = jnp.where(upper_side, holding[middle:], holding[:middle])
        holding = kept_half + partner_2(outgoing, "blk", level)
    dx_mine = holding[0].astype(jnp.bfloat16)
    grad_gate = contract_rows(d_gate, x_all).astype(jnp.bfloat16)
    grad_up = contract_rows(d_up, x_all).astype(jnp.bfloat16)
    dx_back, h_back = over_blocks(
        (dx_mine.reshape(block_count, -1, D), h_mine.reshape(block_count, -1, FF))
    )
    dx_slots, h_slots = over_groups(
        (
            from_blocks(dx_back, group_count, local_experts, capacity),
            from_blocks(h_back, group_count, local_experts, capacity),
        )
    )
    h_pairs = contract_rows(placing, h_slots.reshape(slot_count, FF)).astype(jnp.bfloat16)
    grad_tokens = contract_rows(token_picks, dx_slots.reshape(slot_count, D)).astype(jnp.bfloat16)
    return (h_pairs.reshape(tokens_here, TOPK, FF), grad_tokens, grad_gate[None], grad_up[None])


def solution(mesh):
    in_specs = (
        P(("group", "blk"), None),
        P(("group", "blk"), None),
        P(("group", "blk"), None, None),
        P(("group", "blk"), None, None),
        P(("group", "blk"), None, None),
    )
    out_specs = (
        P(("group", "blk"), None, None),
        P(("group", "blk"), None),
        P(("group", "blk"), None, None),
        P(("group", "blk"), None, None),
    )
    return jax.shard_map(
        on_device, mesh=mesh, in_specs=in_specs, out_specs=out_specs, check_vma=False
    )
```

profile of v0, /device:TPU:1, one launch (start us, length us, event | category | flops | bytes accessed | tf_op | source)
XLA Modules:
  0.0 638.6 jit_solution(11495828700784589863)
XLA Ops:
  4.4 26.1 %all_to_all.40 = bf16[16,16,2048]{2,1,0:T(8,128)(2,1)S(1)} all-to-all(bf16[16,16,2048]{2,1,0:T(8,128)(2,1)S(1)} %bitcast.148), channel_id=1, replica_groups=mesh['group'=16,'blk'=32] {'group'}, dimensions={0} | all-to-all | bytes 2097152 | tf_op jit(solution)/shard_map/all_to_all | solution.py:40
  33.4 14.2 %all-to-all-start.1 = ((bf16[32,8,2048]{2,1,0:T(8,128)(2,1)}), bf16[32,8,2048]{2,1,0:T(8,128)(2,1)S(1)}, u32[]{:S(2)}, u32[]{:S(2)}) async-start(bf16[32,8,2048]{2,1,0:T(8,128)(2,1)} %reshape.272), calls=%async_computation.1 | async-start | bytes 2097152 | tf_op jit(solution)/shard_map/all_to_all | solution.py:47
  48.7 49.1 %all-to-all-done.1 = bf16[32,8,2048]{2,1,0:T(8,128)(2,1)S(1)} async-done(((bf16[32,8,2048]{2,1,0:T(8,128)(2,1)}), bf16[32,8,2048]{2,1,0:T(8,128)(2,1)S(1)}, u32[]{:S(2)}, u32[]{:S(2)}) %all-to-all-start.1) | async-done | bytes 1048608 | tf_op jit(solution)/shard_map/all_to_all | solution.py:47
  97.8 5.7 all-to-all-start.4
  103.4 7.1 %collective-permute-start = (bf16[256,2048]{1,0:T(8,128)(2,1)S(1)}, bf16[256,2048]{1,0:T(8,128)(2,1)S(1)}, u32[]{:S(2)}, u32[]{:S(2)}) collective-permute-start(bf16[256,2048]{1,0:T(8,128)(2,1)S(1)} %bitcast.142), channel_id=1, source_target_pairs={{0,1},{1,0},{2,3},{3,2},{4,5},{5,4},{6,7},{7,6},{8,9},{9,8},{10,11... | collective-permute-start | bytes 3145736 | tf_op jit(solution)/shard_map/ppermute | solution.py:19
  110.5 3.0 all-to-all-done.4
  114.9 7.8 %all-to-all-start.5 = ((bf16[32,8,768]{2,1,0:T(8,128)(2,1)}), bf16[32,8,768]{2,1,0:T(8,128)(2,1)S(1)}, u32[]{:S(2)}, u32[]{:S(2)}) async-start(bf16[32,8,768]{2,1,0:T(8,128)(2,1)} %reshape.282), calls=%async_computation.5 | async-start | bytes 786432 | tf_op jit(solution)/shard_map/all_to_all | solution.py:48
  122.7 20.4 %collective-permute-done = bf16[256,2048]{1,0:T(8,128)(2,1)S(1)} collective-permute-done((bf16[256,2048]{1,0:T(8,128)(2,1)S(1)}, bf16[256,2048]{1,0:T(8,128)(2,1)S(1)}, u32[]{:S(2)}, u32[]{:S(2)}) %collective-permute-start) | collective-permute-done | bytes 1048608 | tf_op jit(solution)/shard_map/ppermute | solution.py:19
  150.4 3.8 collective-permute-start.4
  154.2 44.8 %collective-permute-done.4 = bf16[2,1,256,192]{2,3,0,1:T(8,128)(2,1)S(1)} collective-permute-done((bf16[2,1,256,192]{2,3,0,1:T(8,128)(2,1)S(1)}, bf16[2,1,256,192]{2,3,0,1:T(8,128)(2,1)S(1)}, u32[]{:S(2)}, u32[]{:S(2)}) %collective-permute-start.4) | collective-permute-done | bytes 196640 | tf_op jit(solution)/shard_map/ppermute | solution.py:19
  199.1 3.7 collective-permute-start.5
  202.8 46.0 %collective-permute-done.5 = bf16[1,2,256,192]{2,3,1,0:T(8,128)(2,1)S(1)} collective-permute-done((bf16[1,2,256,192]{2,3,1,0:T(8,128)(2,1)S(1)}, bf16[1,2,256,192]{2,3,1,0:T(8,128)(2,1)S(1)}, u32[]{:S(2)}, u32[]{:S(2)}) %collective-permute-start.5) | collective-permute-done | bytes 196640 | tf_op jit(solution)/shard_map/ppermute | solution.py:19
  250.1 4.4 fusion.4
  254.5 4.4 fusion.8
  262.1 4.1 slice_select_fusion
  269.1 5.0 collective-permute-start.2
  274.1 87.0 %collective-permute-done.2 = bf16[2,1,256,192]{2,3,0,1:T(8,128)(2,1)S(1)} collective-permute-done((bf16[2,1,256,192]{2,3,0,1:T(8,128)(2,1)S(1)}, bf16[2,1,256,192]{2,3,0,1:T(8,128)(2,1)S(1)}, u32[]{:S(2)}, u32[]{:S(2)}) %collective-permute-start.2) | collective-permute-done | bytes 196640 | tf_op jit(solution)/shard_map/ppermute | solution.py:19
  361.1 90.0 %collective-permute-done.6 = f32[2,256,2048]{2,1,0:T(8,128)} collective-permute-done((f32[2,256,2048]{2,1,0:T(8,128)}, f32[2,256,2048]{2,1,0:T(8,128)}, u32[]{:S(2)}, u32[]{:S(2)}) %collective-permute-start.6) | collective-permute-done | bytes 4194336 | tf_op jit(solution)/shard_map/ppermute | solution.py:19
  451.1 4.2 add.30
  457.7 3.7 collective-permute-start.3
  461.3 44.6 %collective-permute-done.3 = bf16[1,2,256,192]{2,3,1,0:T(8,128)(2,1)S(1)} collective-permute-done((bf16[1,2,256,192]{2,3,1,0:T(8,128)(2,1)S(1)}, bf16[1,2,256,192]{2,3,1,0:T(8,128)(2,1)S(1)}, u32[]{:S(2)}, u32[]{:S(2)}) %collective-permute-start.3) | collective-permute-done | bytes 196640 | tf_op jit(solution)/shard_map/ppermute | solution.py:19
  509.3 6.3 all-to-all-start.2
  515.6 4.3 fusion.2
  519.8 20.3 %all-to-all-done.2 = bf16[32,8,768]{2,1,0:T(8,128)(2,1)S(1)} async-done(((bf16[32,8,768]{2,1,0:T(8,128)(2,1)}), bf16[32,8,768]{2,1,0:T(8,128)(2,1)S(1)}, u32[]{:S(2)}, u32[]{:S(2)}) %all-to-all-start.2) | async-done | bytes 393248 | tf_op jit(solution)/shard_map/all_to_all | solution.py:48
  540.1 6.3 all-to-all-start.6
  547.5 48.7 %all-to-all-done.6 = bf16[32,8,2048]{2,1,0:T(8,128)(2,1)S(1)} async-done(((bf16[32,8,2048]{2,1,0:T(8,128)(2,1)}), bf16[32,8,2048]{2,1,0:T(8,128)(2,1)S(1)}, u32[]{:S(2)}, u32[]{:S(2)}) %all-to-all-start.6) | async-done | bytes 1048608 | tf_op jit(solution)/shard_map/all_to_all | solution.py:47
  596.2 9.2 %all-to-all-start.3 = ((bf16[16,16,768]{2,1,0:T(8,128)(2,1)}), bf16[16,16,768]{2,1,0:T(8,128)(2,1)S(1)}, u32[]{:S(2)}, u32[]{:S(2)}) async-start(bf16[16,16,768]{2,1,0:T(8,128)(2,1)} %copy.131), calls=%async_computation.3 | async-start | bytes 786432 | tf_op jit(solution)/shard_map/all_to_all | solution.py:41
  608.0 7.4 %all-to-all-done.3 = bf16[16,16,768]{2,1,0:T(8,128)(2,1)S(1)} async-done(((bf16[16,16,768]{2,1,0:T(8,128)(2,1)}), bf16[16,16,768]{2,1,0:T(8,128)(2,1)S(1)}, u32[]{:S(2)}, u32[]{:S(2)}) %all-to-all-start.3) | async-done | bytes 393248 | tf_op jit(solution)/shard_map/all_to_all | solution.py:41
  616.2 4.2 all-to-all-start.7
  620.4 5.6 fusion.1
  626.0 5.7 fusion
  632.7 4.9 all-to-all-done.7
  (78 shorter events, 35.6 us)
Async XLA Ops:
  0.6 253.9 %copy-start = (bf16[1,192,2048]{2,1,0:T(8,128)(2,1)S(1)}, bf16[1,192,2048]{2,1,0:T(8,128)(2,1)}, u32[]{:S(2)}) copy-start(bf16[1,192,2048]{2,1,0:T(8,128)(2,1)} %param.8) | copy-start | bytes 2359300
  30.5 17.1 %copy-start.8 = (bf16[32,4,768]{2,1,0:T(4,128)(2,1)S(1)}, bf16[32,4,768]{2,1,0:T(4,128)(2,1)}, u32[]{:S(2)}) copy-start(bf16[32,4,768]{2,1,0:T(4,128)(2,1)} %param.7) | copy-start | bytes 589828
  33.4 64.3 %all-to-all-start.1 = ((bf16[32,8,2048]{2,1,0:T(8,128)(2,1)}), bf16[32,8,2048]{2,1,0:T(8,128)(2,1)S(1)}, u32[]{:S(2)}, u32[]{:S(2)}) async-start(bf16[32,8,2048]{2,1,0:T(8,128)(2,1)} %reshape.272), calls=%async_computation.1 | async-start | bytes 2097152 | tf_op jit(solution)/shard_map/all_to_all | solution.py:47
  97.8 15.8 %all-to-all-start.4 = ((bf16[16,16,768]{2,1,0:T(8,128)(2,1)}), bf16[16,16,768]{2,1,0:T(8,128)(2,1)S(1)}, u32[]{:S(2)}, u32[]{:S(2)}) async-start(bf16[16,16,768]{2,1,0:T(8,128)(2,1)} %bitcast.21), calls=%async_computation.4 | async-start | bytes 786432 | tf_op jit(solution)/shard_map/all_to_all | solution.py:41
  103.4 39.7 %collective-permute-start = (bf16[256,2048]{1,0:T(8,128)(2,1)S(1)}, bf16[256,2048]{1,0:T(8,128)(2,1)S(1)}, u32[]{:S(2)}, u32[]{:S(2)}) collective-permute-start(bf16[256,2048]{1,0:T(8,128)(2,1)S(1)} %bitcast.142), channel_id=1, source_target_pairs={{0,1},{1,0},{2,3},{3,2},{4,5},{5,4},{6,7},{7,6},{8,9},{9,8},{10,11... | collective-permute-start | bytes 3145736 | tf_op jit(solution)/shard_map/ppermute | solution.py:19
  114.9 34.6 %all-to-all-start.5 = ((bf16[32,8,768]{2,1,0:T(8,128)(2,1)}), bf16[32,8,768]{2,1,0:T(8,128)(2,1)S(1)}, u32[]{:S(2)}, u32[]{:S(2)}) async-start(bf16[32,8,768]{2,1,0:T(8,128)(2,1)} %reshape.282), calls=%async_computation.5 | async-start | bytes 786432 | tf_op jit(solution)/shard_map/all_to_all | solution.py:48
  145.4 104.7 %collective-permute-start.1 = (bf16[512,2048]{1,0:T(8,128)(2,1)}, bf16[512,2048]{1,0:T(8,128)(2,1)}, u32[]{:S(2)}, u32[]{:S(2)}) collective-permute-start(bf16[512,2048]{1,0:T(8,128)(2,1)} %maximum_select_fusion.1), channel_id=1, source_target_pairs={{0,2},{2,0},{1,3},{3,1},{4,6},{6,4},{5,7},{7,5},{8,10},{10,8},{9,1... | collective-permute-start | bytes 6291464 | tf_op jit(solution)/shard_map/ppermute | solution.py:19
  150.3 99.8 %copy-start.7 = (bf16[1,192,2048]{2,1,0:T(8,128)(2,1)S(1)}, bf16[1,192,2048]{2,1,0:T(8,128)(2,1)}, u32[]{:S(2)}) copy-start(bf16[1,192,2048]{2,1,0:T(8,128)(2,1)} %param.9) | copy-start | bytes 2359300
  150.4 48.6 %collective-permute-start.4 = (bf16[2,1,256,192]{2,3,0,1:T(8,128)(2,1)S(1)}, bf16[2,1,256,192]{2,3,0,1:T(8,128)(2,1)S(1)}, u32[]{:S(2)}, u32[]{:S(2)}) collective-permute-start(bf16[2,1,256,192]{2,3,0,1:T(8,128)(2,1)S(1)} %fusion.14), channel_id=1, source_target_pairs={{0,1},{1,0},{2,3},{3,2},{4,5},{5,4},{6,7},{7,6},{8,9},{9,8},{10,11... | collective-permute-start | bytes 589832 | tf_op jit(solution)/shard_map/ppermute | solution.py:19
  199.1 49.6 %collective-permute-start.5 = (bf16[1,2,256,192]{2,3,1,0:T(8,128)(2,1)S(1)}, bf16[1,2,256,192]{2,3,1,0:T(8,128)(2,1)S(1)}, u32[]{:S(2)}, u32[]{:S(2)}) collective-permute-start(bf16[1,2,256,192]{2,3,1,0:T(8,128)(2,1)S(1)} %fusion.13), channel_id=1, source_target_pairs={{0,2},{2,0},{1,3},{3,1},{4,6},{6,4},{5,7},{7,5},{8,10},{10,8},{9,1... | collective-permute-start | bytes 589832 | tf_op jit(solution)/shard_map/ppermute | solution.py:19
  259.5 1.3 copy-start.5
  266.2 184.9 %collective-permute-start.6 = (f32[2,256,2048]{2,1,0:T(8,128)}, f32[2,256,2048]{2,1,0:T(8,128)}, u32[]{:S(2)}, u32[]{:S(2)}) collective-permute-start(f32[2,256,2048]{2,1,0:T(8,128)} %bitcast.43), channel_id=1, source_target_pairs={{0,2},{2,0},{1,3},{3,1},{4,6},{6,4},{5,7},{7,5},{8,10},{10,8},{9,1... | collective-permute-start | bytes 12582920 | tf_op jit(solution)/shard_map/ppermute | solution.py:19
  269.1 92.0 %collective-permute-start.2 = (bf16[2,1,256,192]{2,3,0,1:T(8,128)(2,1)S(1)}, bf16[2,1,256,192]{2,3,0,1:T(8,128)(2,1)S(1)}, u32[]{:S(2)}, u32[]{:S(2)}) collective-permute-start(bf16[2,1,256,192]{2,3,0,1:T(8,128)(2,1)S(1)} %select_bitcast_fusion.5), channel_id=1, source_target_pairs={{0,1},{1,0},{2,3},{3,2},{4,5},{5,4},{6,7},{7,6},{8,9},{9,8},{10,11... | collective-permute-start | bytes 589832 | tf_op jit(solution)/shard_map/ppermute | solution.py:19
  455.4 50.6 %copy-start.2 = (f32[2,256,2048]{2,1,0:T(8,128)}, f32[2,256,2048]{2,1,0:T(8,128)S(1)}, u32[]{:S(2)}) copy-start(f32[2,256,2048]{2,1,0:T(8,128)S(1)} %add.30) | copy-start | bytes 12582916
  455.6 59.9 %collective-permute-start.7 = (f32[1,256,2048]{2,1,0:T(8,128)S(1)}, f32[1,256,2048]{2,1,0:T(8,128)}, u32[]{:S(2)}, u32[]{:S(2)}) collective-permute-start(f32[1,256,2048]{2,1,0:T(8,128)S(1)} %slice_select_fusion.2), channel_id=1, source_target_pairs={{0,1},{1,0},{2,3},{3,2},{4,5},{5,4},{6,7},{7,6},{8,9},{9,8},{10,11... | collective-permute-start | bytes 6291464 | tf_op jit(solution)/shard_map/ppermute | solution.py:19
  457.7 48.3 %collective-permute-start.3 = (bf16[1,2,256,192]{2,3,1,0:T(8,128)(2,1)S(1)}, bf16[1,2,256,192]{2,3,1,0:T(8,128)(2,1)S(1)}, u32[]{:S(2)}, u32[]{:S(2)}) collective-permute-start(bf16[1,2,256,192]{2,3,1,0:T(8,128)(2,1)S(1)} %select_bitcast_fusion.4), channel_id=1, source_target_pairs={{0,2},{2,0},{1,3},{3,1},{4,6},{6,4},{5,7},{7,5},{8,10},{10,8},{9,1... | collective-permute-start | bytes 589832 | tf_op jit(solution)/shard_map/ppermute | solution.py:19
  509.3 30.9 %all-to-all-start.2 = ((bf16[32,8,768]{2,1,0:T(8,128)(2,1)}), bf16[32,8,768]{2,1,0:T(8,128)(2,1)S(1)}, u32[]{:S(2)}, u32[]{:S(2)}) async-start(bf16[32,8,768]{2,1,0:T(8,128)(2,1)} %reshape_reshape.18), calls=%async_computation.2 | async-start | bytes 786432 | tf_op jit(solution)/shard_map/all_to_all | solution.py:48
  540.1 56.0 %all-to-all-start.6 = ((bf16[32,8,2048]{2,1,0:T(8,128)(2,1)}), bf16[32,8,2048]{2,1,0:T(8,128)(2,1)S(1)}, u32[]{:S(2)}, u32[]{:S(2)}) async-start(bf16[32,8,2048]{2,1,0:T(8,128)(2,1)} %fusion.2), calls=%async_computation.6 | async-start | bytes 2097152 | tf_op jit(solution)/shard_map/all_to_all | solution.py:47
  596.2 19.3 %all-to-all-start.3 = ((bf16[16,16,768]{2,1,0:T(8,128)(2,1)}), bf16[16,16,768]{2,1,0:T(8,128)(2,1)S(1)}, u32[]{:S(2)}, u32[]{:S(2)}) async-start(bf16[16,16,768]{2,1,0:T(8,128)(2,1)} %copy.131), calls=%async_computation.3 | async-start | bytes 786432 | tf_op jit(solution)/shard_map/all_to_all | solution.py:41
  605.4 15.0 %copy-start.6 = (bf16[1024,192]{0,1:T(8,128)(2,1)S(1)}, bf16[1024,192]{0,1:T(8,128)(2,1)}, u32[]{:S(2)}) copy-start(bf16[1024,192]{0,1:T(8,128)(2,1)} %copy-done.5) | copy-start | bytes 1179652
  615.5 0.7 copy-start.3
  616.2 21.5 %all-to-all-start.7 = ((bf16[16,16,2048]{2,1,0:T(8,128)(2,1)}), bf16[16,16,2048]{2,1,0:T(8,128)(2,1)S(1)}, u32[]{:S(2)}, u32[]{:S(2)}) async-start(bf16[16,16,2048]{2,1,0:T(8,128)(2,1)} %copy.146), calls=%async_computation.7 | async-start | bytes 2097152 | tf_op jit(solution)/shard_map/all_to_all | solution.py:40
  626.0 5.7 copy-start.4
  626.0 12.6 %copy-start.1 = (bf16[1,192,2048]{2,1,0:T(8,128)(2,1)S(1)}, bf16[1,192,2048]{2,1,0:T(8,128)(2,1)}, u32[]{:S(2)}) copy-start(bf16[1,192,2048]{2,1,0:T(8,128)(2,1)} %param.8) | copy-start | bytes 2359300
where the time goes:
time: 643 us; the launch traced here: 639 us
  waiting for transfers between devices  468 us (73%)
  starting transfers between devices  82.5 us (13%)
  matrix products  26.3 us (4%)
  blocking collectives  26.1 us (4%)
  other arithmetic  18.2 us (3%)
  local copies, waits for them, and re-layouts  16 us (2%)
    ppermute x8, waiting for transfers between devices, partner_2(): return lax.ppermute(block, axis, route)  333 us
    all_to_all x2, waiting for transfers between devices, over_blocks(): lax.all_to_all(payload[0], 'blk', split_axis=0, concat_axis=0, tiled=True)  97.8 us
    ppermute x8, starting transfers between devices, partner_2(): return lax.ppermute(block, axis, route)  29 us
    all_to_all x1, blocking collectives, over_groups(): lax.all_to_all(payload[0], 'group', split_axis=0, concat_axis=0, tiled=True)  26.1 us
    all_to_all x2, waiting for transfers between devices, over_blocks(): lax.all_to_all(payload[1], 'blk', split_axis=0, concat_axis=0, tiled=True)  22.5 us
    all_to_all x2, starting transfers between devices, over_blocks(): lax.all_to_all(payload[0], 'blk', split_axis=0, concat_axis=0, tiled=True)  20.5 us
    all_to_all x2, starting transfers between devices, over_groups(): lax.all_to_all(payload[1], 'group', split_axis=0, concat_axis=0, tiled=True)  14.8 us
    all_to_all x2, starting transfers between devices, over_blocks(): lax.all_to_all(payload[1], 'blk', split_axis=0, concat_axis=0, tiled=True)  14 us
  transfers between devices with their start and end apart: 15, of which 13 were waited for; matrix products, arithmetic and copies ran while one was open for 5% of the time, Pallas kernels for 0%

commit v1 on v0

v1 whole, which is shorter than its diff:
```python
import functools

import jax
import jax.numpy as jnp
from jax import lax
from jax.experimental import pallas as pl
from jax.experimental.pallas import tpu as pltpu
from jax.sharding import Mesh
from jax.sharding import PartitionSpec as P

D = 2048
FF = 768
TOPK = 4
SUB = 4
BLK = 192
TOK = 32
PAIRS = TOK * TOPK
NZ = 16
NQ = 32
CAP = 2
ROWS = NQ * NZ * CAP
NTOK = NZ * TOK
AXES = ("x", "yh", "core", "yl", "z")
PLANE = ("x", "yh", "core", "yl")
F32 = jnp.float32
BF16 = jnp.bfloat16
VMEM_LIMIT = 56 * 1024 * 1024
STEPS = (0, -4, 4, 8)


def dot(a, b):
    return lax.dot_general(a, b, (((1,), (0,)), ((), ())), preferred_element_type=F32)


def dot_last(a, b):
    return lax.dot_general(a, b, (((1,), (1,)), ((), ())), preferred_element_type=F32)


def dot_first(a, b):
    return lax.dot_general(a, b, (((0,), (0,)), ((), ())), preferred_element_type=F32)


def ones_where(mask):
    return jnp.where(mask, 1.0, 0.0).astype(BF16)


def iota(shape, dim):
    return lax.broadcasted_iota(jnp.int32, shape, dim)


def shift(block, offset):
    return lax.ppermute(block, "z", [(i, (i + offset) % NZ) for i in range(NZ)])


def turn(block, offset):
    return lax.ppermute(
        block, "z", [(i, i // SUB * SUB + (i + offset) % SUB) for i in range(NZ)]
    )


def params():
    return pltpu.CompilerParams(vmem_limit_bytes=VMEM_LIMIT)


def vmem():
    return pl.BlockSpec(memory_space=pltpu.VMEM)


def smem():
    return pl.BlockSpec(memory_space=pltpu.SMEM)


def pack_kernel(place, row_of, rank_of, gh, out):
    s = place[1]
    pairs = gh[...]
    rows = iota((PAIRS, PAIRS), 0)
    hit = rows == row_of[...]
    placed = [
        dot(ones_where(hit & (rank_of[...] == r)), pairs).astype(BF16) for r in range(CAP)
    ]
    source = iota((FF, CAP * BLK), 0)
    target = iota((FF, CAP * BLK), 1)
    for step in range(SUB):
        base = ((s + step) & 3) * BLK
        total = None
        for r in range(CAP):
            unit = target - r * BLK
            pick = ones_where((unit >= 0) & (unit < BLK) & (source == unit + base))
            part = dot(placed[r], pick)
            total = part if total is None else total + part
        out[:, step * CAP * BLK : (step + 1) * CAP * BLK] = total.astype(BF16)


def unpack_kernel(place, row_of, rank_of, slots, out):
    s = place[1]
    rows = iota((PAIRS, PAIRS), 1)
    hit = rows == row_of[...]
    source = iota((CAP * BLK, FF), 0)
    target = iota((CAP * BLK, FF), 1)
    total = jnp.zeros((PAIRS, FF), F32)
    for r in range(CAP):
        spread = jnp.zeros((PAIRS, FF), F32)
        unit = source - r * BLK
        for step in range(SUB):
            base = ((s + step) & 3) * BLK
            pick = ones_where((unit >= 0) & (unit < BLK) & (target == unit + base))
            spread += dot(slots[:, step * CAP * BLK : (step + 1) * CAP * BLK], pick)
        total += dot(ones_where(hit & (rank_of[...] == r)), spread.astype(BF16))
    out[...] = total.astype(BF16)


def slot_of(codes, place_z, quarter):
    expert = codes >> 1
    slot = (expert >> 2) * (NZ * CAP) + place_z * CAP + (codes & 1)
    return jnp.where((expert & 3) == quarter, slot, -1)


def select_kernel(place, tokens, out):
    tile = out.shape[0]
    first = pl.program_id(0) * tile
    codes = jnp.transpose(tokens[:, D:].astype(F32)).astype(jnp.int32)
    origin = codes[TOPK : TOPK + 1, :]
    slots = iota((tile, NTOK), 0) + first
    hit = None
    for k in range(TOPK):
        same = slots == slot_of(codes[k : k + 1, :], origin, place[0])
        hit = same if hit is None else hit | same
    out[...] = dot(ones_where(hit), tokens[:, :D]).astype(BF16)


def combine_kernel(place, codes, slots, out):
    tile = out.shape[0]
    marks = codes[...].astype(F32).astype(jnp.int32)
    origin = marks[:, TOPK : TOPK + 1]
    index = iota((tile, ROWS), 1)
    hit = None
    for k in range(TOPK):
        same = index == slot_of(marks[:, k : k + 1], origin, place[0])
        hit = same if hit is None else hit | same
    out[...] = dot(ones_where(hit), slots[...]).astype(BF16)


def row_of_block(m, place):
    source = m & (NQ - 1)
    quarter = (place[0] - ((m >> 5) & 3)) & 3
    member = (place[1] - (m >> 7)) & 3
    return source * (NZ * CAP) + (quarter * SUB + member) * CAP


def expert_kernel(place, x, dh_in, w_gate, w_up, h_out, d_gate_out, d_up_out, dx, h_sum):
    step = pl.program_id(0)
    tile = x.shape[0]
    first = step * tile
    rows = x[...]
    spread_at = iota((BLK, CAP * BLK), 1) - iota((BLK, CAP * BLK), 0)
    pick_at = iota((CAP * BLK, BLK), 0) - iota((CAP * BLK, BLK), 1)
    upstream = jnp.zeros((tile, BLK), F32)
    home = row_of_block(iota((tile, NTOK), 1), place)
    here = iota((tile, NTOK), 0) + first
    for r in range(CAP):
        part = dot(dh_in[...], ones_where(pick_at == r * BLK)).astype(BF16)
        upstream += dot(ones_where(here == home + r), part)
    gate = dot_last(rows, w_gate[...])
    up = dot_last(rows, w_up[...])
    sigmoid = jax.nn.sigmoid(gate)
    active = gate * sigmoid
    hidden = (active * up).astype(BF16)
    d_gate = (upstream * up * sigmoid * (1.0 + gate * (1.0 - sigmoid))).astype(BF16)
    d_up = (upstream * active).astype(BF16)
    d_gate_out[...] = d_gate
    d_up_out[...] = d_up
    dx[...] = (dot(d_gate, w_gate[...]) + dot(d_up, w_up[...])).astype(BF16)

    back_home = row_of_block(iota((NTOK, tile), 0), place)
    back_here = iota((NTOK, tile), 1) + first
    total = None
    for r in range(CAP):
        wide = dot(hidden, ones_where(spread_at == r * BLK)).astype(BF16)
        part = dot(ones_where(back_here == back_home + r), wide)
        total = part if total is None else total + part

    @pl.when(step == 0)
    def _():
        h_sum[...] = total

    @pl.when(step > 0)
    def _():
        h_sum[...] += total

    @pl.when(step == pl.num_programs(0) - 1)
    def _():
        h_out[...] = h_sum[...].astype(BF16)


def weights_kernel(x, d_gate, d_up, grad_gate, grad_up):
    grad_gate[...] = dot_first(d_gate[...], x[...]).astype(BF16)
    grad_up[...] = dot_first(d_up[...], x[...]).astype(BF16)


def on_device(tokens, expert_ids, grad_hidden, gate_blocks, up_blocks):
    z = lax.axis_index("z")
    quarter, member = z // SUB, z % SUB
    place = jnp.stack([quarter, member]).astype(jnp.int32)

    same = expert_ids[:, :, None, None] == expert_ids[None, None, :, :]
    before = (
        jnp.arange(TOK, dtype=jnp.int32)[:, None, None, None]
        > jnp.arange(TOK, dtype=jnp.int32)[None, None, :, None]
    )
    rank = jnp.sum((same & before).astype(jnp.int32), axis=(2, 3))
    codes = jnp.concatenate(
        [expert_ids * 2 + rank, jnp.full((TOK, 1), z, jnp.int32), jnp.zeros((TOK, 123), jnp.int32)],
        axis=1,
    ).astype(BF16)
    block = jnp.concatenate([tokens, codes], axis=1)

    near = jnp.stack([block, shift(block, 4), shift(block, -4), shift(block, 8)])
    column = jnp.concatenate(
        [
            near,
            shift(near, 1),
            shift(near, -1),
            shift(near[0:2], 2),
            shift(jnp.concatenate([near[0:1], near[2:3]]), -2),
        ]
    ).reshape(NTOK, D + 128)

    row_of = (expert_ids >> 2) * SUB + ((expert_ids - quarter) & 3)
    row_line, rank_line = row_of.reshape(1, PAIRS), rank.reshape(1, PAIRS)
    dh_send = pl.pallas_call(
        pack_kernel,
        out_shape=jax.ShapeDtypeStruct((PAIRS, SUB * CAP * BLK), BF16),
        in_specs=[smem(), vmem(), vmem(), vmem()],
        out_specs=vmem(),
        compiler_params=params(),
        name="pack",
    )(place, row_line, rank_line, grad_hidden.reshape(PAIRS, FF))
    dh_plane = lax.all_to_all(
        dh_send.reshape(NQ, SUB, SUB * CAP * BLK), PLANE, split_axis=0, concat_axis=0, tiled=True
    )
    dh_far = dh_plane.transpose(1, 0, 2)
    dh_quarter = jnp.stack([dh_far[0]] + [shift(dh_far[i], 4 * i) for i in range(1, SUB)])
    width = CAP * BLK
    dh_in = jnp.concatenate(
        [dh_quarter[:, :, :width]]
        + [turn(dh_quarter[:, :, i * width : (i + 1) * width], i) for i in range(1, SUB)]
    ).reshape(NTOK, width)

    tile = 256
    x_send = pl.pallas_call(
        select_kernel,
        out_shape=jax.ShapeDtypeStruct((ROWS, D), BF16),
        grid=(ROWS // tile,),
        in_specs=[smem(), pl.BlockSpec((NTOK, D + 128), lambda i: (0, 0))],
        out_specs=pl.BlockSpec((tile, D), lambda i: (i, 0)),
        compiler_params=params(),
        name="select",
    )(place, column)
    x_all = lax.all_to_all(
        x_send.reshape(NQ, NZ * CAP, D), PLANE, split_axis=0, concat_axis=0, tiled=True
    ).reshape(ROWS, D)

    w_gate, w_up = gate_blocks[0], up_blocks[0]
    whole = lambda i: (0, 0)
    h_all, d_gate, d_up, dx = pl.pallas_call(
        expert_kernel,
        out_shape=(
            jax.ShapeDtypeStruct((NTOK, width), BF16),
            jax.ShapeDtypeStruct((ROWS, BLK), BF16),
            jax.ShapeDtypeStruct((ROWS, BLK), BF16),
            jax.ShapeDtypeStruct((ROWS, D), BF16),
        ),
        grid=(ROWS // tile,),
        in_specs=[
            smem(),
            pl.BlockSpec((tile, D), lambda i: (i, 0)),
            pl.BlockSpec((NTOK, width), whole),
            pl.BlockSpec((BLK, D), whole),
            pl.BlockSpec((BLK, D), whole),
        ],
        out_specs=(
            pl.BlockSpec((NTOK, width), whole),
            pl.BlockSpec((tile, BLK), lambda i: (i, 0)),
            pl.BlockSpec((tile, BLK), lambda i: (i, 0)),
            pl.BlockSpec((tile, D), lambda i: (i, 0)),
        ),
        scratch_shapes=[pltpu.VMEM((NTOK, width), F32)],
        compiler_params=params(),
        name="expert",
    )(place, x_all, dh_in, w_gate, w_up)

    dx_back = lax.all_to_all(
        dx.reshape(NQ, NZ * CAP, D), PLANE, split_axis=0, concat_axis=0, tiled=True
    ).reshape(ROWS, D)

    h_turn = h_all.reshape(SUB, SUB, NQ, width)
    h_quarter = jnp.concatenate(
        [h_turn[0]] + [turn(h_turn[i], -i) for i in range(1, SUB)], axis=2
    )
    h_plane = jnp.stack([h_quarter[0]] + [shift(h_quarter[i], -4 * i) for i in range(1, SUB)])

    cols = D // 4
    grad_gate, grad_up = pl.pallas_call(
        weights_kernel,
        out_shape=(jax.ShapeDtypeStruct((BLK, D), BF16), jax.ShapeDtypeStruct((BLK, D), BF16)),
        grid=(4,),
        in_specs=[
            pl.BlockSpec((ROWS, cols), lambda i: (0, i)),
            pl.BlockSpec((ROWS, BLK), whole),
            pl.BlockSpec((ROWS, BLK), whole),
        ],
        out_specs=(pl.BlockSpec((BLK, cols), lambda i: (0, i)),) * 2,
        compiler_params=params(),
        cost_estimate=pl.CostEstimate(flops=4 * ROWS * BLK * D, bytes_accessed=6 << 20, transcendentals=0),
        name="weights",
    )(x_all, d_gate, d_up)

    part = pl.pallas_call(
        combine_kernel,
        out_shape=jax.ShapeDtypeStruct((NTOK, D), BF16),
        grid=(NTOK // 128,),
        in_specs=[
            smem(),
            pl.BlockSpec((128, 128), lambda i: (i, 0)),
            pl.BlockSpec((ROWS, D), whole),
        ],
        out_specs=pl.BlockSpec((128, D), lambda i: (i, 0)),
        compiler_params=params(),
        name="combine",
    )(place, column[:, D:], dx_back).reshape(NZ, TOK, D)

    from_up = shift(part[4:8], -1)
    from_down = shift(part[8:12], 1)
    far_up = shift(part[12:14], -2)
    far_down = shift(part[14:16], 2)
    held = [part[i].astype(F32) + from_up[i].astype(F32) + from_down[i].astype(F32) for i in range(4)]
    held[0] = held[0] + far_up[0].astype(F32) + far_down[0].astype(F32)
    held[1] = held[1] + far_up[1].astype(F32)
    held[2] = held[2] + far_down[1].astype(F32)
    grad_tokens = (
        held[0]
        + shift(held[1].astype(BF16), -4).astype(F32)
        + shift(held[2].astype(BF16), 4).astype(F32)
        + shift(held[3].astype(BF16), 8).astype(F32)
    ).astype(BF16)

    h_slots = lax.all_to_all(
        h_plane.transpose(1, 0, 2), PLANE, split_axis=0, concat_axis=0, tiled=True
    ).reshape(PAIRS, SUB * width)
    hidden = pl.pallas_call(
        unpack_kernel,
        out_shape=jax.ShapeDtypeStruct((PAIRS, FF), BF16),
        in_specs=[smem(), vmem(), vmem(), vmem()],
        out_specs=vmem(),
        compiler_params=params(),
        name="unpack",
    )(place, row_of.reshape(PAIRS, 1), rank.reshape(PAIRS, 1), h_slots)
    return hidden.reshape(TOK, TOPK, FF), grad_tokens, grad_gate[None], grad_up[None]


def solution(mesh):
    fine = Mesh(mesh.devices.reshape(4, 2, 2, 2, NZ), AXES)
    return jax.shard_map(
        on_device, mesh=fine, in_specs=(P(AXES),) * 5, out_specs=(P(AXES),) * 4, check_vma=False
    )
```

time: 643 us -> 310 us (0.48)
  the two profiles are of different devices: /device:TPU:1 before, /device:TPU:105 now
where the time goes in v1:
time: 310 us; the launch traced here: 308 us
  starting transfers between devices  150 us (48%)
  waiting for transfers between devices  92.6 us (30%)
  Pallas kernels  38 us (12%)
  local copies, waits for them, and re-layouts  18.3 us (6%)
  other arithmetic  8.17 us (3%)
    ppermute x20, starting transfers between devices, shift(): return lax.ppermute(block, 'z', [(i, (i + offset) % NZ) for i in range(NZ)])  98.3 us
    ppermute x20, waiting for transfers between devices, shift(): return lax.ppermute(block, 'z', [(i, (i + offset) % NZ) for i in range(NZ)])  47.9 us
    all_to_all x1, waiting for transfers between devices, on_device(): lax.all_to_all(dx.reshape(NQ, NZ * CAP, D), PLANE, split_axis=0, concat_a...  25.7 us
    ppermute x6, starting transfers between devices, turn(): lax.ppermute(block, 'z', [(i, i // SUB * SUB + (i + offset) % SUB) for i...  20.5 us
    pallas_call x1, Pallas kernels, on_device(): pl.pallas_call(expert_kernel, out_shape=(jax.ShapeDtypeStruct((NTOK, widt...  13.2 us
    all_to_all x1, waiting for transfers between devices, on_device(): lax.all_to_all(x_send.reshape(NQ, NZ * CAP, D), PLANE, split_axis=0, conc...  12.9 us
    all_to_all x1, starting transfers between devices, on_device(): lax.all_to_all(dh_send.reshape(NQ, SUB, SUB * CAP * BLK), PLANE, split_ax...  8.72 us
    all_to_all x1, starting transfers between devices, on_device(): lax.all_to_all(x_send.reshape(NQ, NZ * CAP, D), PLANE, split_axis=0, conc...  8.58 us
  transfers between devices with their start and end apart: 30, of which 14 were waited for; matrix products, arithmetic and copies ran while one was open for 7% of the time, Pallas kernels for 8%

profile of v1, /device:TPU:105, one launch (start us, length us, event | category | flops | bytes accessed | tf_op | source)
XLA Modules:
  0.0 308.2 jit_solution(15932763049567310391)
XLA Ops:
  3.5 12.7 %collective-permute-start.2 = (bf16[32,2176]{1,0:T(8,128)(2,1)S(1)}, bf16[32,2176]{1,0:T(8,128)(2,1)S(1)}, u32[]{:S(2)}, u32[]{:S(2)}) collective-permute-start(bf16[32,2176]{1,0:T(8,128)(2,1)S(1)} %concatenate.20), channel_id=1, source_target_pairs={{0,8},{1,9},{2,10},{3,11},{4,12},{5,13},{6,14},{7,15},{8,0},{9,1},... | collective-permute-start | bytes 417800 | tf_op jit(solution)/shard_map/ppermute | solution.py:52
  19.3 6.1 %collective-permute-start = (bf16[32,2176]{1,0:T(8,128)(2,1)S(1)}, bf16[32,2176]{1,0:T(8,128)(2,1)S(1)}, u32[]{:S(2)}, u32[]{:S(2)}) collective-permute-start(bf16[32,2176]{1,0:T(8,128)(2,1)S(1)} %concatenate.20), channel_id=1, source_target_pairs={{0,4},{1,5},{2,6},{3,7},{4,8},{5,9},{6,10},{7,11},{8,12},{9,13},{1... | collective-permute-start | bytes 417800 | tf_op jit(solution)/shard_map/ppermute | solution.py:52
  33.9 8.7 %all-to-all-start.1 = ((bf16[32,4,1536]{2,1,0:T(4,128)(2,1)}), bf16[32,4,1536]{2,1,0:T(4,128)(2,1)S(1)}, u32[]{:S(2)}, u32[]{:S(2)}) async-start(bf16[32,4,1536]{2,1,0:T(4,128)(2,1)} %reshape.121), calls=%async_computation.1 | async-start | bytes 786432 | tf_op jit(solution)/shard_map/all_to_all | solution.py:238
  45.5 3.9 %collective-permute-start.3 = (bf16[4,32,2176]{2,1,0:T(8,128)(2,1)S(1)}, bf16[4,32,2176]{2,1,0:T(8,128)(2,1)S(1)}, u32[]{:S(2)}, u32[]{:S(2)}) collective-permute-start(bf16[4,32,2176]{2,1,0:T(8,128)(2,1)S(1)} %pad_maximum_fusion), channel_id=1, source_target_pairs={{0,1},{1,2},{2,3},{3,4},{4,5},{5,6},{6,7},{7,8},{8,9},{9,10},{10,1... | collective-permute-start | bytes 1671176 | tf_op jit(solution)/shard_map/ppermute | solution.py:52
  51.3 5.5 %collective-permute-start.5 = (bf16[2,32,2176]{2,1,0:T(8,128)(2,1)S(1)}, bf16[2,32,2176]{2,1,0:T(8,128)(2,1)S(1)}, u32[]{:S(2)}, u32[]{:S(2)}) collective-permute-start(bf16[2,32,2176]{2,1,0:T(8,128)(2,1)S(1)} %get-tuple-element.40), channel_id=1, source_target_pairs={{0,2},{1,3},{2,4},{3,5},{4,6},{5,7},{6,8},{7,9},{8,10},{9,11},{10,... | collective-permute-start | bytes 835592 | tf_op jit(solution)/shard_map/ppermute | solution.py:52
  56.8 4.1 %collective-permute-done.3 = bf16[4,32,2176]{2,1,0:T(8,128)(2,1)S(1)} collective-permute-done((bf16[4,32,2176]{2,1,0:T(8,128)(2,1)S(1)}, bf16[4,32,2176]{2,1,0:T(8,128)(2,1)S(1)}, u32[]{:S(2)}, u32[]{:S(2)}) %collective-permute-start.3) | collective-permute-done | bytes 557088 | tf_op jit(solution)/shard_map/ppermute | solution.py:52
  61.0 12.2 %collective-permute-done.5 = bf16[2,32,2176]{2,1,0:T(8,128)(2,1)S(1)} collective-permute-done((bf16[2,32,2176]{2,1,0:T(8,128)(2,1)S(1)}, bf16[2,32,2176]{2,1,0:T(8,128)(2,1)S(1)}, u32[]{:S(2)}, u32[]{:S(2)}) %collective-permute-start.5) | collective-permute-done | bytes 278560 | tf_op jit(solution)/shard_map/ppermute | solution.py:52
  74.7 6.3 %select.7 = bf16[1024,2048]{1,0:T(8,128)(2,1)} custom-call(s32[2]{0:T(128)} %pad_add_fusion.place, bf16[512,2176]{1,0:T(8,128)(2,1)} %bitcast.113), custom_call_target="tpu_custom_call" | custom-call | tf_op jit(solution)/shard_map/select/pallas_call | solution.py:250
  81.0 8.6 %all-to-all-start = ((bf16[32,32,2048]{2,1,0:T(8,128)(2,1)}), bf16[32,32,2048]{2,1,0:T(8,128)(2,1)}, u32[]{:S(2)}, u32[]{:S(2)}) async-start(bf16[32,32,2048]{2,1,0:T(8,128)(2,1)} %bitcast.111), calls=%async_computation | async-start | bytes 8388608 | tf_op jit(solution)/shard_map/all_to_all | solution.py:259
  89.7 5.6 %collective-permute-start.9 = (bf16[32,1536]{1,0:T(8,128)(2,1)S(1)}, bf16[32,1536]{1,0:T(8,128)(2,1)S(1)}, u32[]{:S(2)}, u32[]{:S(2)}) collective-permute-start(bf16[32,1536]{1,0:T(8,128)(2,1)S(1)} %get-tuple-element.36), channel_id=1, source_target_pairs={{0,12},{1,13},{2,14},{3,15},{4,0},{5,1},{6,2},{7,3},{8,4},{9,5},{1... | collective-permute-start | bytes 294920 | tf_op jit(solution)/shard_map/ppermute | solution.py:52
  95.3 6.2 %collective-permute-start.8 = (bf16[32,1536]{1,0:T(8,128)(2,1)S(1)}, bf16[32,1536]{1,0:T(8,128)(2,1)S(1)}, u32[]{:S(2)}, u32[]{:S(2)}) collective-permute-start(bf16[32,1536]{1,0:T(8,128)(2,1)S(1)} %get-tuple-element.37), channel_id=1, source_target_pairs={{0,8},{1,9},{2,10},{3,11},{4,12},{5,13},{6,14},{7,15},{8,0},{9,1},... | collective-permute-start | bytes 294920 | tf_op jit(solution)/shard_map/ppermute | solution.py:52
  101.5 5.0 %collective-permute-start.7 = (bf16[32,1536]{1,0:T(8,128)(2,1)S(1)}, bf16[32,1536]{1,0:T(8,128)(2,1)S(1)}, u32[]{:S(2)}, u32[]{:S(2)}) collective-permute-start(bf16[32,1536]{1,0:T(8,128)(2,1)S(1)} %get-tuple-element.38), channel_id=1, source_target_pairs={{0,4},{1,5},{2,6},{3,7},{4,8},{5,9},{6,10},{7,11},{8,12},{9,13},{1... | collective-permute-start | bytes 294920 | tf_op jit(solution)/shard_map/ppermute | solution.py:52
  106.5 7.1 %collective-permute-done.8 = bf16[32,1536]{1,0:T(8,128)(2,1)S(1)} collective-permute-done((bf16[32,1536]{1,0:T(8,128)(2,1)S(1)}, bf16[32,1536]{1,0:T(8,128)(2,1)S(1)}, u32[]{:S(2)}, u32[]{:S(2)}) %collective-permute-start.8) | collective-permute-done | bytes 98336 | tf_op jit(solution)/shard_map/ppermute | solution.py:52
  113.6 7.0 %collective-permute-done.7 = bf16[32,1536]{1,0:T(8,128)(2,1)S(1)} collective-permute-done((bf16[32,1536]{1,0:T(8,128)(2,1)S(1)}, bf16[32,1536]{1,0:T(8,128)(2,1)S(1)}, u32[]{:S(2)}, u32[]{:S(2)}) %collective-permute-start.7) | collective-permute-done | bytes 98336 | tf_op jit(solution)/shard_map/ppermute | solution.py:52
  122.6 3.6 %collective-permute-start.11 = (bf16[4,32,384]{2,1,0:T(8,128)(2,1)S(1)}, bf16[4,32,384]{2,1,0:T(8,128)(2,1)S(1)}, u32[]{:S(2)}, u32[]{:S(2)}) collective-permute-start(bf16[4,32,384]{2,1,0:T(8,128)(2,1)S(1)} %get-tuple-element.33), channel_id=1, source_target_pairs={{0,2},{1,3},{2,0},{3,1},{4,6},{5,7},{6,4},{7,5},{8,10},{9,11},{10,... | collective-permute-start | bytes 294920 | tf_op jit(solution)/shard_map/ppermute | solution.py:56
  126.2 4.3 %collective-permute-start.10 = (bf16[4,32,384]{2,1,0:T(8,128)(2,1)S(1)}, bf16[4,32,384]{2,1,0:T(8,128)(2,1)S(1)}, u32[]{:S(2)}, u32[]{:S(2)}) collective-permute-start(bf16[4,32,384]{2,1,0:T(8,128)(2,1)S(1)} %get-tuple-element.34), channel_id=1, source_target_pairs={{0,1},{1,2},{2,3},{3,0},{4,5},{5,6},{6,7},{7,4},{8,9},{9,10},{10,1... | collective-permute-start | bytes 294920 | tf_op jit(solution)/shard_map/ppermute | solution.py:56
  134.7 12.9 %all-to-all-done = bf16[32,32,2048]{2,1,0:T(8,128)(2,1)} async-done(((bf16[32,32,2048]{2,1,0:T(8,128)(2,1)}), bf16[32,32,2048]{2,1,0:T(8,128)(2,1)}, u32[]{:S(2)}, u32[]{:S(2)}) %all-to-all-start) | async-done | bytes 4194336 | tf_op jit(solution)/shard_map/all_to_all | solution.py:259
  147.6 13.2 %expert.1 = (bf16[512,384]{1,0:T(8,128)(2,1)}, bf16[1024,192]{1,0:T(8,128)(2,1)}, bf16[1024,192]{1,0:T(8,128)(2,1)}, bf16[1024,2048]{1,0:T(8,128)(2,1)}) custom-call(s32[2]{0:T(128)} %pad_add_fusion.place, bf16[1024,2048]{1,0:T(8,128)(2,1)} %bitcast.8.x, bf16[512,384]{1,0:T(8,128)(2,1)} %bitcast.117, bf16[192,2048]{1,0:T(8,128)(2,1)} %bitcast.123, ...), custom_call_target="tpu_custom_call" | custom-call | tf_op jit(solution)/shard_map/expert/pallas_call | solution.py:265
  160.8 6.6 %all-to-all-start.3 = ((bf16[32,32,2048]{2,1,0:T(8,128)(2,1)}), bf16[32,32,2048]{2,1,0:T(8,128)(2,1)}, u32[]{:S(2)}, u32[]{:S(2)}) async-start(bf16[32,32,2048]{2,1,0:T(8,128)(2,1)} %bitcast.112), calls=%async_computation.3 | async-start | bytes 8388608 | tf_op jit(solution)/shard_map/all_to_all | solution.py:292
  169.4 5.5 %collective-permute-start.14 = (bf16[4,32,384]{2,1,0:T(8,128)(2,1)S(1)}, bf16[4,32,384]{2,1,0:T(8,128)(2,1)S(1)}, u32[]{:S(2)}, u32[]{:S(2)}) collective-permute-start(bf16[4,32,384]{2,1,0:T(8,128)(2,1)S(1)} %bitcast.130), channel_id=1, source_target_pairs={{0,2},{1,3},{2,0},{3,1},{4,6},{5,7},{6,4},{7,5},{8,10},{9,11},{10,... | collective-permute-start | bytes 294920 | tf_op jit(solution)/shard_map/ppermute | solution.py:56
  183.2 4.0 %collective-permute-start.18 = (bf16[32,1536]{1,0:T(8,128)(2,1)}, bf16[32,1536]{1,0:T(8,128)(2,1)S(1)}, u32[]{:S(2)}, u32[]{:S(2)}) collective-permute-start(bf16[32,1536]{1,0:T(8,128)(2,1)} %get-tuple-element.24), channel_id=1, source_target_pairs={{0,4},{1,5},{2,6},{3,7},{4,8},{5,9},{6,10},{7,11},{8,12},{9,13},{1... | collective-permute-start | bytes 294920 | tf_op jit(solution)/shard_map/ppermute | solution.py:52
  187.2 8.3 %collective-permute-start.17 = (bf16[32,1536]{1,0:T(8,128)(2,1)}, bf16[32,1536]{1,0:T(8,128)(2,1)}, u32[]{:S(2)}, u32[]{:S(2)}) collective-permute-start(bf16[32,1536]{1,0:T(8,128)(2,1)} %get-tuple-element.25), channel_id=1, source_target_pairs={{0,8},{1,9},{2,10},{3,11},{4,12},{5,13},{6,14},{7,15},{8,0},{9,1},... | collective-permute-start | bytes 294920 | tf_op jit(solution)/shard_map/ppermute | solution.py:52
  195.5 4.2 %collective-permute-start.16 = (bf16[32,1536]{1,0:T(8,128)(2,1)S(1)}, bf16[32,1536]{1,0:T(8,128)(2,1)}, u32[]{:S(2)}, u32[]{:S(2)}) collective-permute-start(bf16[32,1536]{1,0:T(8,128)(2,1)S(1)} %get-tuple-element.26), channel_id=1, source_target_pairs={{0,12},{1,13},{2,14},{3,15},{4,0},{5,1},{6,2},{7,3},{8,4},{9,5},{1... | collective-permute-start | bytes 294920 | tf_op jit(solution)/shard_map/ppermute | solution.py:52
  199.7 25.7 %all-to-all-done.3 = bf16[32,32,2048]{2,1,0:T(8,128)(2,1)} async-done(((bf16[32,32,2048]{2,1,0:T(8,128)(2,1)}), bf16[32,32,2048]{2,1,0:T(8,128)(2,1)}, u32[]{:S(2)}, u32[]{:S(2)}) %all-to-all-start.3) | async-done | bytes 4194336 | tf_op jit(solution)/shard_map/all_to_all | solution.py:292
  225.5 7.1 %combine.1 = bf16[512,2048]{1,0:T(8,128)(2,1)} custom-call(s32[2]{0:T(128)} %pad_add_fusion.place, bf16[512,128]{1,0:T(8,128)(2,1)} %slice.186.codes, bf16[1024,2048]{1,0:T(8,128)(2,1)} %bitcast.31.slots), custom_call_target="tpu_custom_call" | custom-call | tf_op jit(solution)/shard_map/combine/pallas_call | solution.py:318
  241.1 5.5 %collective-permute-start.22 = (bf16[2,32,2048]{2,1,0:T(8,128)(2,1)}, bf16[2,32,2048]{2,1,0:T(8,128)(2,1)}, u32[]{:S(2)}, u32[]{:S(2)}) collective-permute-start(bf16[2,32,2048]{2,1,0:T(8,128)(2,1)} %bitcast.38), channel_id=1, source_target_pairs={{0,2},{1,3},{2,4},{3,5},{4,6},{5,7},{6,8},{7,9},{8,10},{9,11},{10,... | collective-permute-start | bytes 786440 | tf_op jit(solution)/shard_map/ppermute | solution.py:52
  252.1 7.3 %all-to-all-start.2 = ((bf16[32,4,1536]{2,1,0:T(4,128)(2,1)}), bf16[32,4,1536]{2,1,0:T(4,128)(2,1)S(1)}, u32[]{:S(2)}, u32[]{:S(2)}) async-start(bf16[32,4,1536]{2,1,0:T(4,128)(2,1)} %copy.63), calls=%async_computation.2 | async-start | bytes 786432 | tf_op jit(solution)/shard_map/all_to_all | solution.py:347
  264.7 4.6 %collective-permute-start.23 = (bf16[32,2048]{1,0:T(8,128)(2,1)}, bf16[32,2048]{1,0:T(8,128)(2,1)}, u32[]{:S(2)}, u32[]{:S(2)}) collective-permute-start(bf16[32,2048]{1,0:T(8,128)(2,1)} %get-tuple-element.16), channel_id=1, source_target_pairs={{0,12},{1,13},{2,14},{3,15},{4,0},{5,1},{6,2},{7,3},{8,4},{9,5},{1... | collective-permute-start | bytes 393224 | tf_op jit(solution)/shard_map/ppermute | solution.py:52
  269.3 7.3 %collective-permute-start.25 = (bf16[32,2048]{1,0:T(8,128)(2,1)}, bf16[32,2048]{1,0:T(8,128)(2,1)}, u32[]{:S(2)}, u32[]{:S(2)}) collective-permute-start(bf16[32,2048]{1,0:T(8,128)(2,1)} %get-tuple-element.17), channel_id=1, source_target_pairs={{0,8},{1,9},{2,10},{3,11},{4,12},{5,13},{6,14},{7,15},{8,0},{9,1},... | collective-permute-start | bytes 393224 | tf_op jit(solution)/shard_map/ppermute | solution.py:52
  276.5 4.6 %collective-permute-start.24 = (bf16[32,2048]{1,0:T(8,128)(2,1)}, bf16[32,2048]{1,0:T(8,128)(2,1)}, u32[]{:S(2)}, u32[]{:S(2)}) collective-permute-start(bf16[32,2048]{1,0:T(8,128)(2,1)} %get-tuple-element.18), channel_id=1, source_target_pairs={{0,4},{1,5},{2,6},{3,7},{4,8},{5,9},{6,10},{7,11},{8,12},{9,13},{1... | collective-permute-start | bytes 393224 | tf_op jit(solution)/shard_map/ppermute | solution.py:52
  281.2 5.5 %weights.1 = (bf16[192,2048]{1,0:T(8,128)(2,1)}, bf16[192,2048]{1,0:T(8,128)(2,1)}) custom-call(bf16[1024,2048]{1,0:T(8,128)(2,1)} %bitcast.8.x, bf16[1024,192]{1,0:T(8,128)(2,1)} %get-tuple-element.12.d_gate, bf16[1024,192]{1,0:T(8,128)(2,1)} %get-tuple-element.13.d_up), custom_call_target="tpu_custom_call" | custom-call | flops 1610612736 | bytes 6291456 | tf_op jit(solution)/shard_map/weights/pallas_call | solution.py:303
  295.3 10.9 %collective-permute-done.24 = bf16[32,2048]{1,0:T(8,128)(2,1)} collective-permute-done((bf16[32,2048]{1,0:T(8,128)(2,1)}, bf16[32,2048]{1,0:T(8,128)(2,1)}, u32[]{:S(2)}, u32[]{:S(2)}) %collective-permute-start.24) | collective-permute-done | bytes 131104 | tf_op jit(solution)/shard_map/ppermute | solution.py:52
  (83 shorter events, 67.1 us)
Async XLA Ops:
  3.5 39.2 %collective-permute-start.2 = (bf16[32,2176]{1,0:T(8,128)(2,1)S(1)}, bf16[32,2176]{1,0:T(8,128)(2,1)S(1)}, u32[]{:S(2)}, u32[]{:S(2)}) collective-permute-start(bf16[32,2176]{1,0:T(8,128)(2,1)S(1)} %concatenate.20), channel_id=1, source_target_pairs={{0,8},{1,9},{2,10},{3,11},{4,12},{5,13},{6,14},{7,15},{8,0},{9,1},... | collective-permute-start | bytes 417800 | tf_op jit(solution)/shard_map/ppermute | solution.py:52
  16.2 26.4 %collective-permute-start.1 = (bf16[32,2176]{1,0:T(8,128)(2,1)S(1)}, bf16[32,2176]{1,0:T(8,128)(2,1)S(1)}, u32[]{:S(2)}, u32[]{:S(2)}) collective-permute-start(bf16[32,2176]{1,0:T(8,128)(2,1)S(1)} %concatenate.20), channel_id=1, source_target_pairs={{0,12},{1,13},{2,14},{3,15},{4,0},{5,1},{6,2},{7,3},{8,4},{9,5},{1... | collective-permute-start | bytes 417800 | tf_op jit(solution)/shard_map/ppermute | solution.py:52
  19.3 23.3 %collective-permute-start = (bf16[32,2176]{1,0:T(8,128)(2,1)S(1)}, bf16[32,2176]{1,0:T(8,128)(2,1)S(1)}, u32[]{:S(2)}, u32[]{:S(2)}) collective-permute-start(bf16[32,2176]{1,0:T(8,128)(2,1)S(1)} %concatenate.20), channel_id=1, source_target_pairs={{0,4},{1,5},{2,6},{3,7},{4,8},{5,9},{6,10},{7,11},{8,12},{9,13},{1... | collective-permute-start | bytes 417800 | tf_op jit(solution)/shard_map/ppermute | solution.py:52
  33.9 47.1 %all-to-all-start.1 = ((bf16[32,4,1536]{2,1,0:T(4,128)(2,1)}), bf16[32,4,1536]{2,1,0:T(4,128)(2,1)S(1)}, u32[]{:S(2)}, u32[]{:S(2)}) async-start(bf16[32,4,1536]{2,1,0:T(4,128)(2,1)} %reshape.121), calls=%async_computation.1 | async-start | bytes 786432 | tf_op jit(solution)/shard_map/all_to_all | solution.py:238
  42.8 18.1 %collective-permute-start.4 = (bf16[4,32,2176]{2,1,0:T(8,128)(2,1)S(1)}, bf16[4,32,2176]{2,1,0:T(8,128)(2,1)S(1)}, u32[]{:S(2)}, u32[]{:S(2)}) collective-permute-start(bf16[4,32,2176]{2,1,0:T(8,128)(2,1)S(1)} %pad_maximum_fusion), channel_id=1, source_target_pairs={{0,15},{1,0},{2,1},{3,2},{4,3},{5,4},{6,5},{7,6},{8,7},{9,8},{10,9... | collective-permute-start | bytes 1671176 | tf_op jit(solution)/shard_map/ppermute | solution.py:52
  45.5 15.4 %collective-permute-start.3 = (bf16[4,32,2176]{2,1,0:T(8,128)(2,1)S(1)}, bf16[4,32,2176]{2,1,0:T(8,128)(2,1)S(1)}, u32[]{:S(2)}, u32[]{:S(2)}) collective-permute-start(bf16[4,32,2176]{2,1,0:T(8,128)(2,1)S(1)} %pad_maximum_fusion), channel_id=1, source_target_pairs={{0,1},{1,2},{2,3},{3,4},{4,5},{5,6},{6,7},{7,8},{8,9},{9,10},{10,1... | collective-permute-start | bytes 1671176 | tf_op jit(solution)/shard_map/ppermute | solution.py:52
  49.3 23.9 %collective-permute-start.6 = (bf16[2,32,2176]{2,1,0:T(8,128)(2,1)S(1)}, bf16[2,32,2176]{2,1,0:T(8,128)(2,1)S(1)}, u32[]{:S(2)}, u32[]{:S(2)}) collective-permute-start(bf16[2,32,2176]{2,1,0:T(8,128)(2,1)S(1)} %get-tuple-element.39), channel_id=1, source_target_pairs={{0,14},{1,15},{2,0},{3,1},{4,2},{5,3},{6,4},{7,5},{8,6},{9,7},{10,... | collective-permute-start | bytes 835592 | tf_op jit(solution)/shard_map/ppermute | solution.py:52
  51.3 22.0 %collective-permute-start.5 = (bf16[2,32,2176]{2,1,0:T(8,128)(2,1)S(1)}, bf16[2,32,2176]{2,1,0:T(8,128)(2,1)S(1)}, u32[]{:S(2)}, u32[]{:S(2)}) collective-permute-start(bf16[2,32,2176]{2,1,0:T(8,128)(2,1)S(1)} %get-tuple-element.40), channel_id=1, source_target_pairs={{0,2},{1,3},{2,4},{3,5},{4,6},{5,7},{6,8},{7,9},{8,10},{9,11},{10,... | collective-permute-start | bytes 835592 | tf_op jit(solution)/shard_map/ppermute | solution.py:52
  81.0 66.6 %all-to-all-start = ((bf16[32,32,2048]{2,1,0:T(8,128)(2,1)}), bf16[32,32,2048]{2,1,0:T(8,128)(2,1)}, u32[]{:S(2)}, u32[]{:S(2)}) async-start(bf16[32,32,2048]{2,1,0:T(8,128)(2,1)} %bitcast.111), calls=%async_computation | async-start | bytes 8388608 | tf_op jit(solution)/shard_map/all_to_all | solution.py:259
  89.7 16.8 %collective-permute-start.9 = (bf16[32,1536]{1,0:T(8,128)(2,1)S(1)}, bf16[32,1536]{1,0:T(8,128)(2,1)S(1)}, u32[]{:S(2)}, u32[]{:S(2)}) collective-permute-start(bf16[32,1536]{1,0:T(8,128)(2,1)S(1)} %get-tuple-element.36), channel_id=1, source_target_pairs={{0,12},{1,13},{2,14},{3,15},{4,0},{5,1},{6,2},{7,3},{8,4},{9,5},{1... | collective-permute-start | bytes 294920 | tf_op jit(solution)/shard_map/ppermute | solution.py:52
  95.3 18.3 %collective-permute-start.8 = (bf16[32,1536]{1,0:T(8,128)(2,1)S(1)}, bf16[32,1536]{1,0:T(8,128)(2,1)S(1)}, u32[]{:S(2)}, u32[]{:S(2)}) collective-permute-start(bf16[32,1536]{1,0:T(8,128)(2,1)S(1)} %get-tuple-element.37), channel_id=1, source_target_pairs={{0,8},{1,9},{2,10},{3,11},{4,12},{5,13},{6,14},{7,15},{8,0},{9,1},... | collective-permute-start | bytes 294920 | tf_op jit(solution)/shard_map/ppermute | solution.py:52
  101.5 19.1 %collective-permute-start.7 = (bf16[32,1536]{1,0:T(8,128)(2,1)S(1)}, bf16[32,1536]{1,0:T(8,128)(2,1)S(1)}, u32[]{:S(2)}, u32[]{:S(2)}) collective-permute-start(bf16[32,1536]{1,0:T(8,128)(2,1)S(1)} %get-tuple-element.38), channel_id=1, source_target_pairs={{0,4},{1,5},{2,6},{3,7},{4,8},{5,9},{6,10},{7,11},{8,12},{9,13},{1... | collective-permute-start | bytes 294920 | tf_op jit(solution)/shard_map/ppermute | solution.py:52
  120.7 9.8 %collective-permute-start.12 = (bf16[4,32,384]{2,1,0:T(8,128)(2,1)S(1)}, bf16[4,32,384]{2,1,0:T(8,128)(2,1)S(1)}, u32[]{:S(2)}, u32[]{:S(2)}) collective-permute-start(bf16[4,32,384]{2,1,0:T(8,128)(2,1)S(1)} %get-tuple-element.32), channel_id=1, source_target_pairs={{0,3},{1,0},{2,1},{3,2},{4,7},{5,4},{6,5},{7,6},{8,11},{9,8},{10,9... | collective-permute-start | bytes 294920 | tf_op jit(solution)/shard_map/ppermute | solution.py:56
  122.6 10.8 %collective-permute-start.11 = (bf16[4,32,384]{2,1,0:T(8,128)(2,1)S(1)}, bf16[4,32,384]{2,1,0:T(8,128)(2,1)S(1)}, u32[]{:S(2)}, u32[]{:S(2)}) collective-permute-start(bf16[4,32,384]{2,1,0:T(8,128)(2,1)S(1)} %get-tuple-element.33), channel_id=1, source_target_pairs={{0,2},{1,3},{2,0},{3,1},{4,6},{5,7},{6,4},{7,5},{8,10},{9,11},{10,... | collective-permute-start | bytes 294920 | tf_op jit(solution)/shard_map/ppermute | solution.py:56
  126.2 7.8 %collective-permute-start.10 = (bf16[4,32,384]{2,1,0:T(8,128)(2,1)S(1)}, bf16[4,32,384]{2,1,0:T(8,128)(2,1)S(1)}, u32[]{:S(2)}, u32[]{:S(2)}) collective-permute-start(bf16[4,32,384]{2,1,0:T(8,128)(2,1)S(1)} %get-tuple-element.34), channel_id=1, source_target_pairs={{0,1},{1,2},{2,3},{3,0},{4,5},{5,6},{6,7},{7,4},{8,9},{9,10},{10,1... | collective-permute-start | bytes 294920 | tf_op jit(solution)/shard_map/ppermute | solution.py:56
  160.8 6.6 %copy-start.2 = (bf16[512,384]{1,0:T(8,128)(2,1)S(1)}, bf16[512,384]{1,0:T(8,128)(2,1)}, u32[]{:S(2)}) copy-start(bf16[512,384]{1,0:T(8,128)(2,1)} %get-tuple-element.10) | copy-start | bytes 1179652
  160.8 64.7 %all-to-all-start.3 = ((bf16[32,32,2048]{2,1,0:T(8,128)(2,1)}), bf16[32,32,2048]{2,1,0:T(8,128)(2,1)}, u32[]{:S(2)}, u32[]{:S(2)}) async-start(bf16[32,32,2048]{2,1,0:T(8,128)(2,1)} %bitcast.112), calls=%async_computation.3 | async-start | bytes 8388608 | tf_op jit(solution)/shard_map/all_to_all | solution.py:292
  167.5 12.4 %collective-permute-start.15 = (bf16[4,32,384]{2,1,0:T(8,128)(2,1)S(1)}, bf16[4,32,384]{2,1,0:T(8,128)(2,1)S(1)}, u32[]{:S(2)}, u32[]{:S(2)}) collective-permute-start(bf16[4,32,384]{2,1,0:T(8,128)(2,1)S(1)} %bitcast.132), channel_id=1, source_target_pairs={{0,1},{1,2},{2,3},{3,0},{4,5},{5,6},{6,7},{7,4},{8,9},{9,10},{10,1... | collective-permute-start | bytes 294920 | tf_op jit(solution)/shard_map/ppermute | solution.py:56
  169.4 11.0 %collective-permute-start.14 = (bf16[4,32,384]{2,1,0:T(8,128)(2,1)S(1)}, bf16[4,32,384]{2,1,0:T(8,128)(2,1)S(1)}, u32[]{:S(2)}, u32[]{:S(2)}) collective-permute-start(bf16[4,32,384]{2,1,0:T(8,128)(2,1)S(1)} %bitcast.130), channel_id=1, source_target_pairs={{0,2},{1,3},{2,0},{3,1},{4,6},{5,7},{6,4},{7,5},{8,10},{9,11},{10,... | collective-permute-start | bytes 294920 | tf_op jit(solution)/shard_map/ppermute | solution.py:56
  174.9 7.6 %collective-permute-start.13 = (bf16[4,32,384]{2,1,0:T(8,128)(2,1)S(1)}, bf16[4,32,384]{2,1,0:T(8,128)(2,1)S(1)}, u32[]{:S(2)}, u32[]{:S(2)}) collective-permute-start(bf16[4,32,384]{2,1,0:T(8,128)(2,1)S(1)} %bitcast.128), channel_id=1, source_target_pairs={{0,3},{1,0},{2,1},{3,2},{4,7},{5,4},{6,5},{7,6},{8,11},{9,8},{10,9... | collective-permute-start | bytes 294920 | tf_op jit(solution)/shard_map/ppermute | solution.py:56
  183.2 57.9 %collective-permute-start.18 = (bf16[32,1536]{1,0:T(8,128)(2,1)}, bf16[32,1536]{1,0:T(8,128)(2,1)S(1)}, u32[]{:S(2)}, u32[]{:S(2)}) collective-permute-start(bf16[32,1536]{1,0:T(8,128)(2,1)} %get-tuple-element.24), channel_id=1, source_target_pairs={{0,4},{1,5},{2,6},{3,7},{4,8},{5,9},{6,10},{7,11},{8,12},{9,13},{1... | collective-permute-start | bytes 294920 | tf_op jit(solution)/shard_map/ppermute | solution.py:52
  187.2 59.4 %collective-permute-start.17 = (bf16[32,1536]{1,0:T(8,128)(2,1)}, bf16[32,1536]{1,0:T(8,128)(2,1)}, u32[]{:S(2)}, u32[]{:S(2)}) collective-permute-start(bf16[32,1536]{1,0:T(8,128)(2,1)} %get-tuple-element.25), channel_id=1, source_target_pairs={{0,8},{1,9},{2,10},{3,11},{4,12},{5,13},{6,14},{7,15},{8,0},{9,1},... | collective-permute-start | bytes 294920 | tf_op jit(solution)/shard_map/ppermute | solution.py:52
  195.5 54.5 %collective-permute-start.16 = (bf16[32,1536]{1,0:T(8,128)(2,1)S(1)}, bf16[32,1536]{1,0:T(8,128)(2,1)}, u32[]{:S(2)}, u32[]{:S(2)}) collective-permute-start(bf16[32,1536]{1,0:T(8,128)(2,1)S(1)} %get-tuple-element.26), channel_id=1, source_target_pairs={{0,12},{1,13},{2,14},{3,15},{4,0},{5,1},{6,2},{7,3},{8,4},{9,5},{1... | collective-permute-start | bytes 294920 | tf_op jit(solution)/shard_map/ppermute | solution.py:52
  232.6 7.7 %copy-start = (bf16[512,2048]{1,0:T(8,128)(2,1)S(1)}, bf16[512,2048]{1,0:T(8,128)(2,1)}, u32[]{:S(2)}) copy-start(bf16[512,2048]{1,0:T(8,128)(2,1)} %combine.1) | copy-start | bytes 6291460
  235.0 27.9 %collective-permute-start.20 = (bf16[4,32,2048]{2,1,0:T(8,128)(2,1)}, bf16[4,32,2048]{2,1,0:T(8,128)(2,1)S(1)}, u32[]{:S(2)}, u32[]{:S(2)}) collective-permute-start(bf16[4,32,2048]{2,1,0:T(8,128)(2,1)} %bitcast.34), channel_id=1, source_target_pairs={{0,1},{1,2},{2,3},{3,4},{4,5},{5,6},{6,7},{7,8},{8,9},{9,10},{10,1... | collective-permute-start | bytes 1572872 | tf_op jit(solution)/shard_map/ppermute | solution.py:52
  236.9 25.9 %collective-permute-start.19 = (bf16[4,32,2048]{2,1,0:T(8,128)(2,1)}, bf16[4,32,2048]{2,1,0:T(8,128)(2,1)S(1)}, u32[]{:S(2)}, u32[]{:S(2)}) collective-permute-start(bf16[4,32,2048]{2,1,0:T(8,128)(2,1)} %bitcast.32), channel_id=1, source_target_pairs={{0,15},{1,0},{2,1},{3,2},{4,3},{5,4},{6,5},{7,6},{8,7},{9,8},{10,9... | collective-permute-start | bytes 1572872 | tf_op jit(solution)/shard_map/ppermute | solution.py:52
  241.1 19.8 %collective-permute-start.22 = (bf16[2,32,2048]{2,1,0:T(8,128)(2,1)}, bf16[2,32,2048]{2,1,0:T(8,128)(2,1)}, u32[]{:S(2)}, u32[]{:S(2)}) collective-permute-start(bf16[2,32,2048]{2,1,0:T(8,128)(2,1)} %bitcast.38), channel_id=1, source_target_pairs={{0,2},{1,3},{2,4},{3,5},{4,6},{5,7},{6,8},{7,9},{8,10},{9,11},{10,... | collective-permute-start | bytes 786440 | tf_op jit(solution)/shard_map/ppermute | solution.py:52
  246.7 16.2 %collective-permute-start.21 = (bf16[2,32,2048]{2,1,0:T(8,128)(2,1)}, bf16[2,32,2048]{2,1,0:T(8,128)(2,1)}, u32[]{:S(2)}, u32[]{:S(2)}) collective-permute-start(bf16[2,32,2048]{2,1,0:T(8,128)(2,1)} %bitcast.36), channel_id=1, source_target_pairs={{0,14},{1,15},{2,0},{3,1},{4,2},{5,3},{6,4},{7,5},{8,6},{9,7},{10,... | collective-permute-start | bytes 786440 | tf_op jit(solution)/shard_map/ppermute | solution.py:52
  252.1 34.6 %all-to-all-start.2 = ((bf16[32,4,1536]{2,1,0:T(4,128)(2,1)}), bf16[32,4,1536]{2,1,0:T(4,128)(2,1)S(1)}, u32[]{:S(2)}, u32[]{:S(2)}) async-start(bf16[32,4,1536]{2,1,0:T(4,128)(2,1)} %copy.63), calls=%async_computation.2 | async-start | bytes 786432 | tf_op jit(solution)/shard_map/all_to_all | solution.py:347
  264.7 27.5 %collective-permute-start.23 = (bf16[32,2048]{1,0:T(8,128)(2,1)}, bf16[32,2048]{1,0:T(8,128)(2,1)}, u32[]{:S(2)}, u32[]{:S(2)}) collective-permute-start(bf16[32,2048]{1,0:T(8,128)(2,1)} %get-tuple-element.16), channel_id=1, source_target_pairs={{0,12},{1,13},{2,14},{3,15},{4,0},{5,1},{6,2},{7,3},{8,4},{9,5},{1... | collective-permute-start | bytes 393224 | tf_op jit(solution)/shard_map/ppermute | solution.py:52
  269.3 26.0 %collective-permute-start.25 = (bf16[32,2048]{1,0:T(8,128)(2,1)}, bf16[32,2048]{1,0:T(8,128)(2,1)}, u32[]{:S(2)}, u32[]{:S(2)}) collective-permute-start(bf16[32,2048]{1,0:T(8,128)(2,1)} %get-tuple-element.17), channel_id=1, source_target_pairs={{0,8},{1,9},{2,10},{3,11},{4,12},{5,13},{6,14},{7,15},{8,0},{9,1},... | collective-permute-start | bytes 393224 | tf_op jit(solution)/shard_map/ppermute | solution.py:52
  276.5 29.7 %collective-permute-start.24 = (bf16[32,2048]{1,0:T(8,128)(2,1)}, bf16[32,2048]{1,0:T(8,128)(2,1)}, u32[]{:S(2)}, u32[]{:S(2)}) collective-permute-start(bf16[32,2048]{1,0:T(8,128)(2,1)} %get-tuple-element.18), channel_id=1, source_target_pairs={{0,4},{1,5},{2,6},{3,7},{4,8},{5,9},{6,10},{7,11},{8,12},{9,13},{1... | collective-permute-start | bytes 393224 | tf_op jit(solution)/shard_map/ppermute | solution.py:52
  (1 other events, 1.3 us)

commit v2 on v1

v2 whole, which is shorter than its diff:
```python
import jax
import jax.numpy as jnp
from jax import lax
from jax.experimental import pallas as pl
from jax.experimental.pallas import tpu as pltpu
from jax.sharding import Mesh
from jax.sharding import PartitionSpec as P

D = 2048
FF = 768
TOPK = 4
SUB = 4
BLK = 192
PAIR = 2 * BLK
WIDE = D + PAIR
TOK = 32
PAIRS = TOK * TOPK
NZ = 16
NQ = 32
CAP = 2
HALF = NZ // 2
PER = HALF * CAP
ROWS = NQ * PER
NTOK = HALF * TOK
SENT = NQ * CAP
PLANE = ("x", "yh", "core", "yl")
EVEN = ("zq", "zm")
COLUMN = ("zq", "zm", "zl")
AXES = PLANE + COLUMN
F32 = jnp.float32
BF16 = jnp.bfloat16


def dot(a, b):
    return lax.dot_general(a, b, (((1,), (0,)), ((), ())), preferred_element_type=F32)


def dot_last(a, b):
    return lax.dot_general(a, b, (((1,), (1,)), ((), ())), preferred_element_type=F32)


def dot_first(a, b):
    return lax.dot_general(a, b, (((0,), (0,)), ((), ())), preferred_element_type=F32)


def ones_where(mask):
    return jnp.where(mask, 1.0, 0.0).astype(BF16)


def iota(shape, dim):
    return lax.broadcasted_iota(jnp.int32, shape, dim)


def shift(block, offset):
    return lax.ppermute(block, COLUMN, [(i, (i + offset) % NZ) for i in range(NZ)])


def swap(block):
    return lax.ppermute(block, COLUMN, [(i, i ^ 1) for i in range(NZ)])


def exchange(values, axes):
    return lax.all_to_all(values, axes, split_axis=0, concat_axis=0, tiled=True)


def params():
    return pltpu.CompilerParams(vmem_limit_bytes=56 * 1024 * 1024)


def vmem():
    return pl.BlockSpec(memory_space=pltpu.VMEM)


def smem():
    return pl.BlockSpec(memory_space=pltpu.SMEM)


def whole(i):
    return (0, 0)


def pack_kernel(row_of, gh, out):
    hit = iota((SUB * SENT, PAIRS), 0) == row_of[...]
    slots = dot(ones_where(hit), gh[...]).astype(BF16)
    for q in range(SUB):
        for m in range(2):
            out[q * 2 + m] = slots[q * SENT : (q + 1) * SENT, m * PAIR : (m + 1) * PAIR]


def unpack_kernel(row_of, received, out, slots):
    for q in range(SUB):
        for m in range(2):
            slots[q * SENT : (q + 1) * SENT, m * PAIR : (m + 1) * PAIR] = received[q * 2 + m]
    hit = iota((PAIRS, SUB * SENT), 1) == row_of[...]
    out[...] = dot(ones_where(hit), slots[...]).astype(BF16)


def slot_of(codes, origin, quarter):
    expert = codes >> 1
    slot = (expert >> 2) * PER + (origin >> 1) * CAP + (codes & 1)
    return jnp.where((expert & 3) == quarter, slot, -1)


def select_kernel(place, *refs):
    pieces, dh, out, codes_out, held = refs[:7], refs[7], refs[8], refs[9], refs[10]
    tile = out.shape[0]

    @pl.when(pl.program_id(0) == 0)
    def _():
        at = 0
        for piece in pieces:
            held[at : at + piece.shape[0]] = piece[...]
            at += piece.shape[0]
        codes_out[...] = held[:, D:]

    first = pl.program_id(0) * tile
    codes = jnp.transpose(held[:, D:].astype(F32)).astype(jnp.int32)
    origin = codes[TOPK : TOPK + 1, :]
    slots = iota((tile, NTOK), 0) + first
    hit = None
    for k in range(TOPK):
        same = slots == slot_of(codes[k : k + 1, :], origin, place[0])
        hit = same if hit is None else hit | same
    out[:, :D] = dot(ones_where(hit), held[:, :D]).astype(BF16)
    row = iota((tile, ROWS), 0) + first
    came = ((row >> 1) & (HALF - 1)) * SENT + (row >> 4) * CAP + (row & 1)
    out[:, D:] = dot(ones_where(iota((tile, ROWS), 1) == came), dh[...]).astype(BF16)


def combine_kernel(place, codes, slots, out, h_out):
    tile = out.shape[0]
    marks = codes[...].astype(F32).astype(jnp.int32)
    origin = marks[:, TOPK : TOPK + 1]
    index = iota((tile, ROWS), 1)
    hit = None
    for k in range(TOPK):
        same = index == slot_of(marks[:, k : k + 1], origin, place[0])
        hit = same if hit is None else hit | same
    out[...] = dot(ones_where(hit), slots[:, :D]).astype(BF16)
    tile = h_out.shape[0]
    sent = iota((tile, ROWS), 0) + pl.program_id(0) * tile
    row = ((sent >> 1) & (NQ - 1)) * PER + (sent >> 6) * CAP + (sent & 1)
    h_out[...] = dot(ones_where(iota((tile, ROWS), 1) == row), slots[:, D:]).astype(BF16)


def expert_kernel(
    place, x, gate_own, gate_other, up_own, up_other, back, d_gate_out, d_up_out, w_gate, w_up
):
    for parity in range(2):
        first, second = (gate_own, up_own), (gate_other, up_other)
        if parity:
            first, second = second, first

        @pl.when((pl.program_id(0) == 0) & (place[1] == parity))
        def _(first=first, second=second):
            w_gate[:BLK], w_up[:BLK] = first[0][...], first[1][...]
            w_gate[BLK:], w_up[BLK:] = second[0][...], second[1][...]

    rows = x[:, :D]
    upstream = x[:, D:].astype(F32)
    gate = dot_last(rows, w_gate[...])
    up = dot_last(rows, w_up[...])
    sigmoid = jax.nn.sigmoid(gate)
    active = gate * sigmoid
    back[:, D:] = (active * up).astype(BF16)
    d_gate = (upstream * up * sigmoid * (1.0 + gate * (1.0 - sigmoid))).astype(BF16)
    d_up = (upstream * active).astype(BF16)
    d_gate_out[...] = d_gate
    d_up_out[...] = d_up
    back[:, :D] = (dot(d_gate, w_gate[...]) + dot(d_up, w_up[...])).astype(BF16)


def weights_kernel(place, x, d_gate, d_up, own_gate, own_up, send_gate, send_up):
    even = place[1] == 0
    for d, own, send in ((d_gate, own_gate, send_gate), (d_up, own_up, send_up)):
        total = dot_first(d[...], x[...])
        own[...] = jnp.where(even, total[:BLK], total[BLK:])
        send[...] = jnp.where(even, total[BLK:], total[:BLK]).astype(BF16)


def on_device(tokens, expert_ids, grad_hidden, gate_blocks, up_blocks):
    z = lax.axis_index(COLUMN)
    place = jnp.stack([z // SUB, z % 2]).astype(jnp.int32)

    same = expert_ids[:, :, None, None] == expert_ids[None, None, :, :]
    before = (
        jnp.arange(TOK, dtype=jnp.int32)[:, None, None, None]
        > jnp.arange(TOK, dtype=jnp.int32)[None, None, :, None]
    )
    rank = jnp.sum((same & before).astype(jnp.int32), axis=(2, 3))
    codes = jnp.concatenate(
        [expert_ids * 2 + rank, jnp.full((TOK, 1), z, jnp.int32), jnp.zeros((TOK, 123), jnp.int32)],
        axis=1,
    ).astype(BF16)
    block = jnp.concatenate([tokens, codes], axis=1)

    half = TOK // 2
    below, above = shift(block, 4), shift(block, -4)

    row_of = (expert_ids & 3) * SENT + (expert_ids >> 2) * CAP + rank
    dh_send = pl.pallas_call(
        pack_kernel,
        out_shape=jax.ShapeDtypeStruct((HALF, SENT, PAIR), BF16),
        in_specs=[vmem(), vmem()],
        out_specs=vmem(),
        compiler_params=params(),
        name="pack",
    )(row_of.reshape(1, PAIRS), grad_hidden.reshape(PAIRS, FF))
    dh_send, below, above = lax.optimization_barrier((dh_send, below, above))
    dh = exchange(dh_send, EVEN).reshape(ROWS, PAIR)
    near_below = shift(jnp.concatenate([block, below]), 2)
    near_above = shift(jnp.concatenate([block, above]), -2)
    far_below, far_above = shift(below[:half], 4), shift(above[half:], -4)
    pieces = (block, below, above, far_below, far_above, near_below, near_above)

    tile = 256
    x_send, codes_all = pl.pallas_call(
        select_kernel,
        out_shape=(
            jax.ShapeDtypeStruct((ROWS, WIDE), BF16),
            jax.ShapeDtypeStruct((NTOK, 128), BF16),
        ),
        grid=(ROWS // tile,),
        in_specs=[smem()]
        + [pl.BlockSpec(piece.shape, whole) for piece in pieces]
        + [pl.BlockSpec((ROWS, PAIR), whole)],
        out_specs=(pl.BlockSpec((tile, WIDE), lambda i: (i, 0)), pl.BlockSpec((NTOK, 128), whole)),
        scratch_shapes=[pltpu.VMEM((NTOK, D + 128), BF16)],
        compiler_params=params(),
        name="select",
    )(place, *pieces, dh)

    gate_own, up_own = gate_blocks[0], up_blocks[0]
    x_send, gate_out, up_out = lax.optimization_barrier((x_send, gate_own, up_own))
    gate_other, up_other = swap(gate_out), swap(up_out)
    x_all = exchange(x_send.reshape(NQ, PER, WIDE), PLANE).reshape(ROWS, WIDE)

    by_rows = pl.BlockSpec((tile, WIDE), lambda i: (i, 0))
    by_rows_d = pl.BlockSpec((tile, PAIR), lambda i: (i, 0))
    back, d_gate, d_up = pl.pallas_call(
        expert_kernel,
        out_shape=(
            jax.ShapeDtypeStruct((ROWS, WIDE), BF16),
            jax.ShapeDtypeStruct((ROWS, PAIR), BF16),
            jax.ShapeDtypeStruct((ROWS, PAIR), BF16),
        ),
        grid=(ROWS // tile,),
        in_specs=[smem(), by_rows] + [pl.BlockSpec((BLK, D), whole)] * 4,
        out_specs=(by_rows, by_rows_d, by_rows_d),
        scratch_shapes=[pltpu.VMEM((PAIR, D), BF16)] * 2,
        compiler_params=params(),
        name="expert",
    )(place, x_all, gate_own, gate_other, up_own, up_other)

    returned = exchange(back.reshape(NQ, PER, WIDE), PLANE).reshape(ROWS, WIDE)

    cols = D // 4
    by_cols = pl.BlockSpec((BLK, cols), lambda i: (0, i))
    own_gate, own_up, send_gate, send_up = pl.pallas_call(
        weights_kernel,
        out_shape=(jax.ShapeDtypeStruct((BLK, D), F32),) * 2
        + (jax.ShapeDtypeStruct((BLK, D), BF16),) * 2,
        grid=(4,),
        in_specs=[
            smem(),
            pl.BlockSpec((ROWS, cols), lambda i: (0, i)),
            pl.BlockSpec((ROWS, PAIR), whole),
            pl.BlockSpec((ROWS, PAIR), whole),
        ],
        out_specs=(by_cols,) * 4,
        compiler_params=params(),
        cost_estimate=pl.CostEstimate(
            flops=4 * ROWS * PAIR * D, bytes_accessed=7 << 20, transcendentals=0
        ),
        name="weights",
    )(place, x_all, d_gate, d_up)
    recv_gate, recv_up = swap(send_gate), swap(send_up)

    part, h_send = pl.pallas_call(
        combine_kernel,
        out_shape=(
            jax.ShapeDtypeStruct((NTOK, D), BF16),
            jax.ShapeDtypeStruct((ROWS, PAIR), BF16),
        ),
        grid=(2,),
        in_specs=[
            smem(),
            pl.BlockSpec((NTOK // 2, 128), lambda i: (i, 0)),
            pl.BlockSpec((ROWS, WIDE), whole),
        ],
        out_specs=(
            pl.BlockSpec((NTOK // 2, D), lambda i: (i, 0)),
            pl.BlockSpec((ROWS // 2, PAIR), lambda i: (i, 0)),
        ),
        compiler_params=params(),
        name="combine",
    )(place, codes_all, returned)

    recv_gate, recv_up, part = lax.optimization_barrier((recv_gate, recv_up, part))
    grad_gate = (own_gate + recv_gate.astype(F32)).astype(BF16)
    grad_up = (own_up + recv_up.astype(F32)).astype(BF16)

    own, to_below, to_above = (part[i * TOK : (i + 1) * TOK].astype(F32) for i in range(3))
    at = 3 * TOK
    far_up = shift(part[at : at + half], -4).astype(F32)
    far_down = shift(part[at + half : at + TOK], 4).astype(F32)
    at += TOK
    near_up = shift(part[at : at + 2 * TOK], -2).astype(F32)
    near_down = shift(part[at + 2 * TOK :], 2).astype(F32)
    own = own + near_up[:TOK] + near_down[:TOK]
    to_below = to_below + near_up[TOK:]
    to_above = to_above + near_down[TOK:]
    to_below = jnp.concatenate([to_below[:half] + far_up, to_below[half:]])
    to_above = jnp.concatenate([to_above[:half], to_above[half:] + far_down])
    grad_tokens = (
        own
        + shift(to_below.astype(BF16), -4).astype(F32)
        + shift(to_above.astype(BF16), 4).astype(F32)
    ).astype(BF16)

    h_slots = exchange(h_send.reshape(HALF, SENT, PAIR), EVEN)
    hidden = pl.pallas_call(
        unpack_kernel,
        out_shape=jax.ShapeDtypeStruct((PAIRS, FF), BF16),
        in_specs=[vmem(), vmem()],
        out_specs=vmem(),
        scratch_shapes=[pltpu.VMEM((SUB * SENT, FF), BF16)],
        compiler_params=params(),
        name="unpack",
    )(row_of.reshape(PAIRS, 1), h_slots)
    return hidden.reshape(TOK, TOPK, FF), grad_tokens, grad_gate[None], grad_up[None]


def solution(mesh):
    fine = Mesh(mesh.devices.reshape(4, 2, 2, 2, SUB, 2, 2), AXES)
    return jax.shard_map(
        on_device, mesh=fine, in_specs=(P(AXES),) * 5, out_specs=(P(AXES),) * 4, check_vma=False
    )
```

time: 310 us -> 263 us (0.85)
  the two profiles are of different devices: /device:TPU:105 before, /device:TPU:1 now
where the time goes in v2:
time: 263 us; the launch traced here: 259 us
  starting transfers between devices  118 us (45%)
  waiting for transfers between devices  96 us (37%)
  Pallas kernels  25.8 us (10%)
  local copies, waits for them, and re-layouts  12.4 us (5%)
  other arithmetic  6.16 us (2%)
    ppermute x12, starting transfers between devices, shift(): lax.ppermute(block, COLUMN, [(i, (i + offset) % NZ) for i in range(NZ)])  57.7 us
    ppermute x12, waiting for transfers between devices, shift(): lax.ppermute(block, COLUMN, [(i, (i + offset) % NZ) for i in range(NZ)])  40.1 us
    all_to_all x4, starting transfers between devices, exchange(): return lax.all_to_all(values, axes, split_axis=0, concat_axis=0, tiled=True)  34.5 us
    ppermute x4, waiting for transfers between devices, swap(): return lax.ppermute(block, COLUMN, [(i, i ^ 1) for i in range(NZ)])  31.9 us
    ppermute x4, starting transfers between devices, swap(): return lax.ppermute(block, COLUMN, [(i, i ^ 1) for i in range(NZ)])  25.5 us
    all_to_all x4, waiting for transfers between devices, exchange(): return lax.all_to_all(values, axes, split_axis=0, concat_axis=0, tiled=True)  24 us
    pallas_call x1, Pallas kernels, on_device(): pl.pallas_call(expert_kernel, out_shape=(jax.ShapeDtypeStruct((ROWS, WIDE...  8.34 us
    unnamed x32, local copies, waits for them, and re-layouts  5.47 us
  transfers between devices with their start and end apart: 20, of which 8 were waited for; matrix products, arithmetic and copies ran while one was open for 3% of the time, Pallas kernels for 4%

profile of v2, /device:TPU:1, one launch (start us, length us, event | category | flops | bytes accessed | tf_op | source)
XLA Modules:
  0.0 259.1 jit_solution(7467569574575976371)
XLA Ops:
  3.5 13.3 %collective-permute-start.1 = (bf16[32,2176]{1,0:T(8,128)(2,1)S(1)}, bf16[32,2176]{1,0:T(8,128)(2,1)S(1)}, u32[]{:S(2)}, u32[]{:S(2)}) collective-permute-start(bf16[32,2176]{1,0:T(8,128)(2,1)S(1)} %concatenate.20.refs_0_), channel_id=1, source_target_pairs={{0,12},{1,13},{2,14},{3,15},{4,0},{5,1},{6,2},{7,3},{8,4},{9,5},{1... | collective-permute-start | bytes 417800 | tf_op jit(solution)/shard_map/ppermute | solution.py:55
  21.0 1.9 pack.1
  23.0 5.5 %collective-permute-done.1.refs_2_ = bf16[32,2176]{1,0:T(8,128)(2,1)S(1)} collective-permute-done((bf16[32,2176]{1,0:T(8,128)(2,1)S(1)}, bf16[32,2176]{1,0:T(8,128)(2,1)S(1)}, u32[]{:S(2)}, u32[]{:S(2)}) %collective-permute-start.1) | collective-permute-done | bytes 139296 | tf_op jit(solution)/shard_map/ppermute | solution.py:55
  28.5 10.6 %all-to-all-start = ((bf16[8,64,384]{2,1,0:T(8,128)(2,1)}), bf16[8,64,384]{2,1,0:T(8,128)(2,1)S(1)}, u32[]{:S(2)}, u32[]{:S(2)}) async-start(bf16[8,64,384]{2,1,0:T(8,128)(2,1)} %pack.1), calls=%async_computation | async-start | bytes 786432 | tf_op jit(solution)/shard_map/all_to_all | solution.py:63
  39.1 5.5 %collective-permute-start.5 = (bf16[64,2176]{1,0:T(8,128)(2,1)S(1)}, bf16[64,2176]{1,0:T(8,128)(2,1)S(1)}, u32[]{:S(2)}, u32[]{:S(2)}) collective-permute-start(bf16[64,2176]{1,0:T(8,128)(2,1)S(1)} %get-tuple-element.50), channel_id=1, source_target_pairs={{0,14},{1,15},{2,0},{3,1},{4,2},{5,3},{6,4},{7,5},{8,6},{9,7},{10,... | collective-permute-start | bytes 835592 | tf_op jit(solution)/shard_map/ppermute | solution.py:55
  46.6 7.0 %collective-permute-start.3 = (bf16[16,2176]{1,0:T(8,128)(2,1)S(1)}, bf16[16,2176]{1,0:T(8,128)(2,1)S(1)}, u32[]{:S(2)}, u32[]{:S(2)}) collective-permute-start(bf16[16,2176]{1,0:T(8,128)(2,1)S(1)} %slice.54), channel_id=1, source_target_pairs={{0,12},{1,13},{2,14},{3,15},{4,0},{5,1},{6,2},{7,3},{8,4},{9,5},{1... | collective-permute-start | bytes 208904 | tf_op jit(solution)/shard_map/ppermute | solution.py:55
  53.6 2.2 collective-permute-start.2
  56.5 5.2 %collective-permute-done.3.refs_4_ = bf16[16,2176]{1,0:T(8,128)(2,1)S(1)} collective-permute-done((bf16[16,2176]{1,0:T(8,128)(2,1)S(1)}, bf16[16,2176]{1,0:T(8,128)(2,1)S(1)}, u32[]{:S(2)}, u32[]{:S(2)}) %collective-permute-start.3) | collective-permute-done | bytes 69664 | tf_op jit(solution)/shard_map/ppermute | solution.py:55
  61.7 2.0 collective-permute-done.2.refs_3_
  64.7 4.0 %select.7 = (bf16[512,2432]{1,0:T(8,128)(2,1)}, bf16[256,128]{1,0:T(8,128)(2,1)}) custom-call(s32[2]{0:T(128)} %pad_add_fusion.place, bf16[32,2176]{1,0:T(8,128)(2,1)} %copy-done.6, bf16[32,2176]{1,0:T(8,128)(2,1)} %copy-done.9, bf16[32,2176]{1,0:T(8,128)(2,1)} %copy-done.8, bf16[16,2176]{1,0:T(8,128)(2,1)} %copy-done.15, bf16[16,2176]{1,0:T(8,128)(2,1)} %copy-done.14, ...), custom_call_target="tpu_custom_call" | custom-call | tf_op jit(solution)/shard_map/select/pallas_call | solution.py:217
  68.6 9.3 %all-to-all-start.1 = ((bf16[32,16,2432]{2,1,0:T(8,128)(2,1)}), bf16[32,16,2432]{2,1,0:T(8,128)(2,1)S(1)}, u32[]{:S(2)}, u32[]{:S(2)}) async-start(bf16[32,16,2432]{2,1,0:T(8,128)(2,1)} %bitcast.17), calls=%async_computation.1 | async-start | bytes 4980736 | tf_op jit(solution)/shard_map/all_to_all | solution.py:63
  78.0 18.3 %collective-permute-start.6 = (bf16[192,2048]{1,0:T(8,128)(2,1)S(1)}, bf16[192,2048]{1,0:T(8,128)(2,1)S(1)}, u32[]{:S(2)}, u32[]{:S(2)}) collective-permute-start(bf16[192,2048]{1,0:T(8,128)(2,1)S(1)} %bitcast.21), channel_id=1, source_target_pairs={{0,1},{1,0},{2,3},{3,2},{4,5},{5,4},{6,7},{7,6},{8,9},{9,8},{10,11... | collective-permute-start | bytes 2359304 | tf_op jit(solution)/shard_map/ppermute | solution.py:59
  96.3 1.9 collective-permute-start.7
  98.3 15.8 %collective-permute-done.6.gate_other = bf16[192,2048]{1,0:T(8,128)(2,1)S(1)} collective-permute-done((bf16[192,2048]{1,0:T(8,128)(2,1)S(1)}, bf16[192,2048]{1,0:T(8,128)(2,1)S(1)}, u32[]{:S(2)}, u32[]{:S(2)}) %collective-permute-start.6) | collective-permute-done | bytes 786464 | tf_op jit(solution)/shard_map/ppermute | solution.py:59
  115.0 16.1 %collective-permute-done.7.up_other = bf16[192,2048]{1,0:T(8,128)(2,1)} collective-permute-done((bf16[192,2048]{1,0:T(8,128)(2,1)}, bf16[192,2048]{1,0:T(8,128)(2,1)}, u32[]{:S(2)}, u32[]{:S(2)}) %collective-permute-start.7) | collective-permute-done | bytes 786464 | tf_op jit(solution)/shard_map/ppermute | solution.py:59
  132.5 8.3 %expert.1 = (bf16[512,2432]{1,0:T(8,128)(2,1)}, bf16[512,384]{1,0:T(8,128)(2,1)}, bf16[512,384]{1,0:T(8,128)(2,1)}) custom-call(s32[2]{0:T(128)} %pad_add_fusion.place, bf16[512,2432]{1,0:T(8,128)(2,1)} %bitcast.14, bf16[192,2048]{1,0:T(8,128)(2,1)} %bitcast.20, bf16[192,2048]{1,0:T(8,128)(2,1)} %copy-done.11, bf16[192,2048]{1,0:T(8,128)(2,1)} %bitcast.23, ...), custom_call_target="tpu_custom_call" | custom-call | tf_op jit(solution)/shard_map/expert/pallas_call | solution.py:240
  140.9 7.7 %all-to-all-start.2 = ((bf16[32,16,2432]{2,1,0:T(8,128)(2,1)}), bf16[32,16,2432]{2,1,0:T(8,128)(2,1)S(1)}, u32[]{:S(2)}, u32[]{:S(2)}) async-start(bf16[32,16,2432]{2,1,0:T(8,128)(2,1)} %bitcast.18), calls=%async_computation.2 | async-start | bytes 4980736 | tf_op jit(solution)/shard_map/all_to_all | solution.py:63
  148.6 5.4 %weights.1 = (f32[192,2048]{1,0:T(8,128)}, f32[192,2048]{1,0:T(8,128)}, bf16[192,2048]{1,0:T(8,128)(2,1)}, bf16[192,2048]{1,0:T(8,128)(2,1)}) custom-call(s32[2]{0:T(128)} %pad_add_fusion.place, bf16[512,2432]{1,0:T(8,128)(2,1)} %bitcast.15, bf16[512,384]{1,0:T(8,128)(2,1)} %get-tuple-element.34.d_gate, bf16[512,384]{1,0:T(8,128)(2,1)} %get-tuple-element.35.d_up), custom_call_target="tpu_custom_call" | custom-call | flops 1610612736 | bytes 7340032 | tf_op jit(solution)/shard_map/weights/pallas_call | solution.py:259
  154.1 3.4 %collective-permute-start.8 = (bf16[192,2048]{1,0:T(8,128)(2,1)}, bf16[192,2048]{1,0:T(8,128)(2,1)S(1)}, u32[]{:S(2)}, u32[]{:S(2)}) collective-permute-start(bf16[192,2048]{1,0:T(8,128)(2,1)} %get-tuple-element.36), channel_id=1, source_target_pairs={{0,1},{1,0},{2,3},{3,2},{4,5},{5,4},{6,7},{7,6},{8,9},{9,8},{10,11... | collective-permute-start | bytes 2359304 | tf_op jit(solution)/shard_map/ppermute | solution.py:59
  157.4 1.9 collective-permute-start.9
  160.1 24.0 %all-to-all-done.2 = bf16[32,16,2432]{2,1,0:T(8,128)(2,1)S(1)} async-done(((bf16[32,16,2432]{2,1,0:T(8,128)(2,1)}), bf16[32,16,2432]{2,1,0:T(8,128)(2,1)S(1)}, u32[]{:S(2)}, u32[]{:S(2)}) %all-to-all-start.2) | async-done | bytes 2490400 | tf_op jit(solution)/shard_map/all_to_all | solution.py:63
  185.5 4.2 %combine.1 = (bf16[256,2048]{1,0:T(8,128)(2,1)}, bf16[512,384]{1,0:T(8,128)(2,1)}) custom-call(s32[2]{0:T(128)} %pad_add_fusion.place, bf16[256,128]{1,0:T(8,128)(2,1)} %get-tuple-element.27.codes, bf16[512,2432]{1,0:T(8,128)(2,1)} %bitcast.16), custom_call_target="tpu_custom_call" | custom-call | tf_op jit(solution)/shard_map/combine/pallas_call | solution.py:279
  189.6 6.8 %all-to-all-start.3 = ((bf16[8,64,384]{2,1,0:T(8,128)(2,1)}), bf16[8,64,384]{2,1,0:T(8,128)(2,1)S(1)}, u32[]{:S(2)}, u32[]{:S(2)}) async-start(bf16[8,64,384]{2,1,0:T(8,128)(2,1)} %bitcast.24), calls=%async_computation.3 | async-start | bytes 786432 | tf_op jit(solution)/shard_map/all_to_all | solution.py:63
  197.6 5.5 %collective-permute-start.10 = (bf16[64,2048]{1,0:T(8,128)(2,1)S(1)}, bf16[64,2048]{1,0:T(8,128)(2,1)S(1)}, u32[]{:S(2)}, u32[]{:S(2)}) collective-permute-start(bf16[64,2048]{1,0:T(8,128)(2,1)S(1)} %get-tuple-element.48), channel_id=1, source_target_pairs={{0,14},{1,15},{2,0},{3,1},{4,2},{5,3},{6,4},{7,5},{8,6},{9,7},{10,... | collective-permute-start | bytes 786440 | tf_op jit(solution)/shard_map/ppermute | solution.py:55
  205.0 7.0 %collective-permute-start.12 = (bf16[16,2048]{1,0:T(8,128)(2,1)S(1)}, bf16[16,2048]{1,0:T(8,128)(2,1)S(1)}, u32[]{:S(2)}, u32[]{:S(2)}) collective-permute-start(bf16[16,2048]{1,0:T(8,128)(2,1)S(1)} %get-tuple-element.44), channel_id=1, source_target_pairs={{0,12},{1,13},{2,14},{3,15},{4,0},{5,1},{6,2},{7,3},{8,4},{9,5},{1... | collective-permute-start | bytes 196616 | tf_op jit(solution)/shard_map/ppermute | solution.py:55
  212.0 2.2 collective-permute-start.14
  214.2 16.3 %collective-permute-done.10 = bf16[64,2048]{1,0:T(8,128)(2,1)S(1)} collective-permute-done((bf16[64,2048]{1,0:T(8,128)(2,1)S(1)}, bf16[64,2048]{1,0:T(8,128)(2,1)S(1)}, u32[]{:S(2)}, u32[]{:S(2)}) %collective-permute-start.10) | collective-permute-done | bytes 262176 | tf_op jit(solution)/shard_map/ppermute | solution.py:55
  230.8 7.1 %collective-permute-start.15 = (bf16[32,2048]{1,0:T(8,128)(2,1)S(1)}, bf16[32,2048]{1,0:T(8,128)(2,1)S(1)}, u32[]{:S(2)}, u32[]{:S(2)}) collective-permute-start(bf16[32,2048]{1,0:T(8,128)(2,1)S(1)} %pad_maximum_fusion.3), channel_id=1, source_target_pairs={{0,4},{1,5},{2,6},{3,7},{4,8},{5,9},{6,10},{7,11},{8,12},{9,13},{1... | collective-permute-start | bytes 393224 | tf_op jit(solution)/shard_map/ppermute | solution.py:55
  238.0 2.2 collective-permute-start.13
  240.2 2.8 %fusion = (bf16[1,192,2048]{2,1,0:T(8,128)(2,1)}, bf16[1,192,2048]{2,1,0:T(8,128)(2,1)}) fusion(f32[192,2048]{1,0:T(8,128)S(1)} %copy-done.4, bf16[192,2048]{1,0:T(8,128)(2,1)S(1)} %collective-permute-done.8, f32[192,2048]{1,0:T(8,128)S(1)} %copy-done.5, bf16[192,2048]{1,0:T(8,128)(2,1)} %collective-permute-done.9), kind=kLoop, calls=%fused_computation.2 | loop fusion | flops 2359296 | bytes 6291456 | tf_op jit(solution)/shard_map/broadcast_in_dim | solution.py:331
  243.0 11.0 %collective-permute-done.13 = bf16[32,2048]{1,0:T(8,128)(2,1)S(1)} collective-permute-done((bf16[32,2048]{1,0:T(8,128)(2,1)S(1)}, bf16[32,2048]{1,0:T(8,128)(2,1)S(1)}, u32[]{:S(2)}, u32[]{:S(2)}) %collective-permute-start.13) | collective-permute-done | bytes 131104 | tf_op jit(solution)/shard_map/ppermute | solution.py:55
  255.5 2.0 unpack.1
  (76 shorter events, 21.5 us)
Async XLA Ops:
  3.5 60.3 %copy-start.6 = (bf16[32,2176]{1,0:T(8,128)(2,1)}, bf16[32,2176]{1,0:T(8,128)(2,1)S(1)}, u32[]{:S(2)}) copy-start(bf16[32,2176]{1,0:T(8,128)(2,1)S(1)} %concatenate.20.refs_0_) | copy-start | bytes 417796
  3.5 25.0 %collective-permute-start.1 = (bf16[32,2176]{1,0:T(8,128)(2,1)S(1)}, bf16[32,2176]{1,0:T(8,128)(2,1)S(1)}, u32[]{:S(2)}, u32[]{:S(2)}) collective-permute-start(bf16[32,2176]{1,0:T(8,128)(2,1)S(1)} %concatenate.20.refs_0_), channel_id=1, source_target_pairs={{0,12},{1,13},{2,14},{3,15},{4,0},{5,1},{6,2},{7,3},{8,4},{9,5},{1... | collective-permute-start | bytes 417800 | tf_op jit(solution)/shard_map/ppermute | solution.py:55
  16.8 11.8 %collective-permute-start = (bf16[32,2176]{1,0:T(8,128)(2,1)S(1)}, bf16[32,2176]{1,0:T(8,128)(2,1)S(1)}, u32[]{:S(2)}, u32[]{:S(2)}) collective-permute-start(bf16[32,2176]{1,0:T(8,128)(2,1)S(1)} %concatenate.20.refs_0_), channel_id=1, source_target_pairs={{0,4},{1,5},{2,6},{3,7},{4,8},{5,9},{6,10},{7,11},{8,12},{9,13},{1... | collective-permute-start | bytes 417800 | tf_op jit(solution)/shard_map/ppermute | solution.py:55
  28.5 35.3 %copy-start.8 = (bf16[32,2176]{1,0:T(8,128)(2,1)}, bf16[32,2176]{1,0:T(8,128)(2,1)S(1)}, u32[]{:S(2)}) copy-start(bf16[32,2176]{1,0:T(8,128)(2,1)S(1)} %collective-permute-done.1.refs_2_) | copy-start | bytes 417796
  28.5 35.3 %copy-start.9 = (bf16[32,2176]{1,0:T(8,128)(2,1)}, bf16[32,2176]{1,0:T(8,128)(2,1)S(1)}, u32[]{:S(2)}) copy-start(bf16[32,2176]{1,0:T(8,128)(2,1)S(1)} %collective-permute-done.refs_1_) | copy-start | bytes 417796
  28.5 35.2 %all-to-all-start = ((bf16[8,64,384]{2,1,0:T(8,128)(2,1)}), bf16[8,64,384]{2,1,0:T(8,128)(2,1)S(1)}, u32[]{:S(2)}, u32[]{:S(2)}) async-start(bf16[8,64,384]{2,1,0:T(8,128)(2,1)} %pack.1), calls=%async_computation | async-start | bytes 786432 | tf_op jit(solution)/shard_map/all_to_all | solution.py:63
  39.1 24.6 %collective-permute-start.5 = (bf16[64,2176]{1,0:T(8,128)(2,1)S(1)}, bf16[64,2176]{1,0:T(8,128)(2,1)S(1)}, u32[]{:S(2)}, u32[]{:S(2)}) collective-permute-start(bf16[64,2176]{1,0:T(8,128)(2,1)S(1)} %get-tuple-element.50), channel_id=1, source_target_pairs={{0,14},{1,15},{2,0},{3,1},{4,2},{5,3},{6,4},{7,5},{8,6},{9,7},{10,... | collective-permute-start | bytes 835592 | tf_op jit(solution)/shard_map/ppermute | solution.py:55
  44.6 19.1 %collective-permute-start.4 = (bf16[64,2176]{1,0:T(8,128)(2,1)S(1)}, bf16[64,2176]{1,0:T(8,128)(2,1)S(1)}, u32[]{:S(2)}, u32[]{:S(2)}) collective-permute-start(bf16[64,2176]{1,0:T(8,128)(2,1)S(1)} %get-tuple-element.51), channel_id=1, source_target_pairs={{0,2},{1,3},{2,4},{3,5},{4,6},{5,7},{6,8},{7,9},{8,10},{9,11},{10,... | collective-permute-start | bytes 835592 | tf_op jit(solution)/shard_map/ppermute | solution.py:55
  46.6 15.1 %collective-permute-start.3 = (bf16[16,2176]{1,0:T(8,128)(2,1)S(1)}, bf16[16,2176]{1,0:T(8,128)(2,1)S(1)}, u32[]{:S(2)}, u32[]{:S(2)}) collective-permute-start(bf16[16,2176]{1,0:T(8,128)(2,1)S(1)} %slice.54), channel_id=1, source_target_pairs={{0,12},{1,13},{2,14},{3,15},{4,0},{5,1},{6,2},{7,3},{8,4},{9,5},{1... | collective-permute-start | bytes 208904 | tf_op jit(solution)/shard_map/ppermute | solution.py:55
  53.6 10.1 %collective-permute-start.2 = (bf16[16,2176]{1,0:T(8,128)(2,1)S(1)}, bf16[16,2176]{1,0:T(8,128)(2,1)S(1)}, u32[]{:S(2)}, u32[]{:S(2)}) collective-permute-start(bf16[16,2176]{1,0:T(8,128)(2,1)S(1)} %slice.53), channel_id=1, source_target_pairs={{0,4},{1,5},{2,6},{3,7},{4,8},{5,9},{6,10},{7,11},{8,12},{9,13},{1... | collective-permute-start | bytes 208904 | tf_op jit(solution)/shard_map/ppermute | solution.py:55
  61.7 2.1 copy-start.14
  63.7 0.9 copy-start.3
  68.6 9.4 %copy-start.10 = (bf16[1,192,2048]{2,1,0:T(8,128)(2,1)S(1)}, bf16[1,192,2048]{2,1,0:T(8,128)(2,1)}, u32[]{:S(2)}) copy-start(bf16[1,192,2048]{2,1,0:T(8,128)(2,1)} %param.8) | copy-start | bytes 2359300
  68.6 62.4 %all-to-all-start.1 = ((bf16[32,16,2432]{2,1,0:T(8,128)(2,1)}), bf16[32,16,2432]{2,1,0:T(8,128)(2,1)S(1)}, u32[]{:S(2)}, u32[]{:S(2)}) async-start(bf16[32,16,2432]{2,1,0:T(8,128)(2,1)} %bitcast.17), calls=%async_computation.1 | async-start | bytes 4980736 | tf_op jit(solution)/shard_map/all_to_all | solution.py:63
  78.0 36.1 %collective-permute-start.6 = (bf16[192,2048]{1,0:T(8,128)(2,1)S(1)}, bf16[192,2048]{1,0:T(8,128)(2,1)S(1)}, u32[]{:S(2)}, u32[]{:S(2)}) collective-permute-start(bf16[192,2048]{1,0:T(8,128)(2,1)S(1)} %bitcast.21), channel_id=1, source_target_pairs={{0,1},{1,0},{2,3},{3,2},{4,5},{5,4},{6,7},{7,6},{8,9},{9,8},{10,11... | collective-permute-start | bytes 2359304 | tf_op jit(solution)/shard_map/ppermute | solution.py:59
  96.3 34.7 %collective-permute-start.7 = (bf16[192,2048]{1,0:T(8,128)(2,1)}, bf16[192,2048]{1,0:T(8,128)(2,1)}, u32[]{:S(2)}, u32[]{:S(2)}) collective-permute-start(bf16[192,2048]{1,0:T(8,128)(2,1)} %bitcast.22), channel_id=1, source_target_pairs={{0,1},{1,0},{2,3},{3,2},{4,5},{5,4},{6,7},{7,6},{8,9},{9,8},{10,11... | collective-permute-start | bytes 2359304 | tf_op jit(solution)/shard_map/ppermute | solution.py:59
  114.1 0.9 copy-start.11
  131.1 1.5 copy-start
  140.9 43.1 %all-to-all-start.2 = ((bf16[32,16,2432]{2,1,0:T(8,128)(2,1)}), bf16[32,16,2432]{2,1,0:T(8,128)(2,1)S(1)}, u32[]{:S(2)}, u32[]{:S(2)}) async-start(bf16[32,16,2432]{2,1,0:T(8,128)(2,1)} %bitcast.18), calls=%async_computation.2 | async-start | bytes 4980736 | tf_op jit(solution)/shard_map/all_to_all | solution.py:63
  154.1 42.4 %collective-permute-start.8 = (bf16[192,2048]{1,0:T(8,128)(2,1)}, bf16[192,2048]{1,0:T(8,128)(2,1)S(1)}, u32[]{:S(2)}, u32[]{:S(2)}) collective-permute-start(bf16[192,2048]{1,0:T(8,128)(2,1)} %get-tuple-element.36), channel_id=1, source_target_pairs={{0,1},{1,0},{2,3},{3,2},{4,5},{5,4},{6,7},{7,6},{8,9},{9,8},{10,11... | collective-permute-start | bytes 2359304 | tf_op jit(solution)/shard_map/ppermute | solution.py:59
  157.4 39.1 %collective-permute-start.9 = (bf16[192,2048]{1,0:T(8,128)(2,1)}, bf16[192,2048]{1,0:T(8,128)(2,1)}, u32[]{:S(2)}, u32[]{:S(2)}) collective-permute-start(bf16[192,2048]{1,0:T(8,128)(2,1)} %get-tuple-element.37), channel_id=1, source_target_pairs={{0,1},{1,0},{2,3},{3,2},{4,5},{5,4},{6,7},{7,6},{8,9},{9,8},{10,11... | collective-permute-start | bytes 2359304 | tf_op jit(solution)/shard_map/ppermute | solution.py:59
  184.0 1.4 copy-start.1
  189.6 15.3 %copy-start.7 = (bf16[256,2048]{1,0:T(8,128)(2,1)S(1)}, bf16[256,2048]{1,0:T(8,128)(2,1)}, u32[]{:S(2)}) copy-start(bf16[256,2048]{1,0:T(8,128)(2,1)} %get-tuple-element.39) | copy-start | bytes 3145732
  189.6 65.1 %all-to-all-start.3 = ((bf16[8,64,384]{2,1,0:T(8,128)(2,1)}), bf16[8,64,384]{2,1,0:T(8,128)(2,1)S(1)}, u32[]{:S(2)}, u32[]{:S(2)}) async-start(bf16[8,64,384]{2,1,0:T(8,128)(2,1)} %bitcast.24), calls=%async_computation.3 | async-start | bytes 786432 | tf_op jit(solution)/shard_map/all_to_all | solution.py:63
  197.6 32.9 %collective-permute-start.10 = (bf16[64,2048]{1,0:T(8,128)(2,1)S(1)}, bf16[64,2048]{1,0:T(8,128)(2,1)S(1)}, u32[]{:S(2)}, u32[]{:S(2)}) collective-permute-start(bf16[64,2048]{1,0:T(8,128)(2,1)S(1)} %get-tuple-element.48), channel_id=1, source_target_pairs={{0,14},{1,15},{2,0},{3,1},{4,2},{5,3},{6,4},{7,5},{8,6},{9,7},{10,... | collective-permute-start | bytes 786440 | tf_op jit(solution)/shard_map/ppermute | solution.py:55
  203.1 27.5 %collective-permute-start.11 = (bf16[64,2048]{1,0:T(8,128)(2,1)S(1)}, bf16[64,2048]{1,0:T(8,128)(2,1)S(1)}, u32[]{:S(2)}, u32[]{:S(2)}) collective-permute-start(bf16[64,2048]{1,0:T(8,128)(2,1)S(1)} %get-tuple-element.49), channel_id=1, source_target_pairs={{0,2},{1,3},{2,4},{3,5},{4,6},{5,7},{6,8},{7,9},{8,10},{9,11},{10,... | collective-permute-start | bytes 786440 | tf_op jit(solution)/shard_map/ppermute | solution.py:55
  205.0 32.9 %collective-permute-start.12 = (bf16[16,2048]{1,0:T(8,128)(2,1)S(1)}, bf16[16,2048]{1,0:T(8,128)(2,1)S(1)}, u32[]{:S(2)}, u32[]{:S(2)}) collective-permute-start(bf16[16,2048]{1,0:T(8,128)(2,1)S(1)} %get-tuple-element.44), channel_id=1, source_target_pairs={{0,12},{1,13},{2,14},{3,15},{4,0},{5,1},{6,2},{7,3},{8,4},{9,5},{1... | collective-permute-start | bytes 196616 | tf_op jit(solution)/shard_map/ppermute | solution.py:55
  212.0 18.7 %collective-permute-start.14 = (bf16[16,2048]{1,0:T(8,128)(2,1)S(1)}, bf16[16,2048]{1,0:T(8,128)(2,1)S(1)}, u32[]{:S(2)}, u32[]{:S(2)}) collective-permute-start(bf16[16,2048]{1,0:T(8,128)(2,1)S(1)} %get-tuple-element.45), channel_id=1, source_target_pairs={{0,4},{1,5},{2,6},{3,7},{4,8},{5,9},{6,10},{7,11},{8,12},{9,13},{1... | collective-permute-start | bytes 196616 | tf_op jit(solution)/shard_map/ppermute | solution.py:55
  230.6 9.6 %copy-start.4 = (f32[192,2048]{1,0:T(8,128)S(1)}, f32[192,2048]{1,0:T(8,128)}, u32[]{:S(2)}) copy-start(f32[192,2048]{1,0:T(8,128)} %get-tuple-element.40) | copy-start | bytes 4718596
  230.6 9.6 %copy-start.5 = (f32[192,2048]{1,0:T(8,128)S(1)}, f32[192,2048]{1,0:T(8,128)}, u32[]{:S(2)}) copy-start(f32[192,2048]{1,0:T(8,128)} %get-tuple-element.42) | copy-start | bytes 4718596
  230.8 12.3 %collective-permute-start.15 = (bf16[32,2048]{1,0:T(8,128)(2,1)S(1)}, bf16[32,2048]{1,0:T(8,128)(2,1)S(1)}, u32[]{:S(2)}, u32[]{:S(2)}) collective-permute-start(bf16[32,2048]{1,0:T(8,128)(2,1)S(1)} %pad_maximum_fusion.3), channel_id=1, source_target_pairs={{0,4},{1,5},{2,6},{3,7},{4,8},{5,9},{6,10},{7,11},{8,12},{9,13},{1... | collective-permute-start | bytes 393224 | tf_op jit(solution)/shard_map/ppermute | solution.py:55
  238.0 16.1 %collective-permute-start.13 = (bf16[32,2048]{1,0:T(8,128)(2,1)S(1)}, bf16[32,2048]{1,0:T(8,128)(2,1)S(1)}, u32[]{:S(2)}, u32[]{:S(2)}) collective-permute-start(bf16[32,2048]{1,0:T(8,128)(2,1)S(1)} %pad_maximum_fusion.2), channel_id=1, source_target_pairs={{0,12},{1,13},{2,14},{3,15},{4,0},{5,1},{6,2},{7,3},{8,4},{9,5},{1... | collective-permute-start | bytes 393224 | tf_op jit(solution)/shard_map/ppermute | solution.py:55
  (4 other events, 2.9 us)

commit v3 on v2

--- a/solution.py
+++ b/solution.py
@@ -52,7 +52,10 @@
 
 
 def shift(block, offset):
-    return lax.ppermute(block, COLUMN, [(i, (i + offset) % NZ) for i in range(NZ)])
+    route = []
+    for i in range(NZ):
+        route += [(i, (i + offset) % NZ), (NZ + i, NZ + (i - offset) % NZ)]
+    return lax.ppermute(block, ("core",) + COLUMN, route)
 
 
 def swap(block):
@@ -211,6 +214,12 @@
     near_below = shift(jnp.concatenate([block, below]), 2)
     near_above = shift(jnp.concatenate([block, above]), -2)
     far_below, far_above = shift(below[:half], 4), shift(above[half:], -4)
+
+    gate_own, up_own = gate_blocks[0], up_blocks[0]
+    near_below, near_above, gate_out, up_out = lax.optimization_barrier(
+        (near_below, near_above, gate_own, up_own)
+    )
+    gate_other, up_other = swap(gate_out), swap(up_out)
     pieces = (block, below, above, far_below, far_above, near_below, near_above)
 
     tile = 256
@@ -230,9 +239,6 @@
         name="select",
     )(place, *pieces, dh)
 
-    gate_own, up_own = gate_blocks[0], up_blocks[0]
-    x_send, gate_out, up_out = lax.optimization_barrier((x_send, gate_own, up_own))
-    gate_other, up_other = swap(gate_out), swap(up_out)
     x_all = exchange(x_send.reshape(NQ, PER, WIDE), PLANE).reshape(ROWS, WIDE)
 
     by_rows = pl.BlockSpec((tile, WIDE), lambda i: (i, 0))
@@ -305,19 +311,13 @@
     far_up = shift(part[at : at + half], -4).astype(F32)
     far_down = shift(part[at + half : at + TOK], 4).astype(F32)
     at += TOK
-    near_up = shift(part[at : at + 2 * TOK], -2).astype(F32)
-    near_down = shift(part[at + 2 * TOK :], 2).astype(F32)
+    near_up, near_down = shift(part[at : at + 2 * TOK], -2), shift(part[at + 2 * TOK :], 2)
+    near_up, near_down = near_up.astype(F32), near_down.astype(F32)
     own = own + near_up[:TOK] + near_down[:TOK]
     to_below = to_below + near_up[TOK:]
     to_above = to_above + near_down[TOK:]
     to_below = jnp.concatenate([to_below[:half] + far_up, to_below[half:]])
     to_above = jnp.concatenate([to_above[:half], to_above[half:] + far_down])
-    grad_tokens = (
-        own
-        + shift(to_below.astype(BF16), -4).astype(F32)
-        + shift(to_above.astype(BF16), 4).astype(F32)
-    ).astype(BF16)
-
     h_slots = exchange(h_send.reshape(HALF, SENT, PAIR), EVEN)
     hidden = pl.pallas_call(
         unpack_kernel,
@@ -328,7 +328,11 @@
         compiler_params=params(),
         name="unpack",
     )(row_of.reshape(PAIRS, 1), h_slots)
-    return hidden.reshape(TOK, TOPK, FF), grad_tokens, grad_gate[None], grad_up[None]
+    hidden = hidden.reshape(TOK, TOPK, FF)
+    from_above, from_below = shift(to_below.astype(BF16), -4), shift(to_above.astype(BF16), 4)
+    hidden, from_above, from_below = lax.optimization_barrier((hidden, from_above, from_below))
+    grad_tokens = (own + from_above.astype(F32) + from_below.astype(F32)).astype(BF16)
+    return hidden, grad_tokens, grad_gate[None], grad_up[None]
 
 
 def solution(mesh):

time: 263 us -> 259 us (0.985); the launches traced: 259 us -> 258 us
  starting transfers between devices: 118 us -> 105 us
  waiting for transfers between devices: 96 us -> 107 us
    ppermute x4, starting transfers between devices: 25.5 us -> 10.6 us  [swap(): return lax.ppermute(block, COLUMN, [(i, i ^ 1) for i in range(NZ)])]
    ppermute x12, waiting for transfers between devices: 40.1 us -> 51.6 us  [shift(): return lax.ppermute(block, ('core',) + COLUMN, route)]
  transfers between devices with their start and end apart: 20 -> 20, of which waited for: 8 -> 9; matrix products, arithmetic and copies ran while one was open for 3% -> 4% of each run, Pallas kernels for 4% -> 5%
where the time goes in v3:
time: 259 us; the launch traced here: 258 us
  waiting for transfers between devices  107 us (41%)
  starting transfers between devices  105 us (41%)
  Pallas kernels  25.8 us (10%)
  local copies, waits for them, and re-layouts  12.2 us (5%)
  other arithmetic  7.1 us (3%)
    ppermute x12, starting transfers between devices, shift(): return lax.ppermute(block, ('core',) + COLUMN, route)  57.7 us
    ppermute x12, waiting for transfers between devices, shift(): return lax.ppermute(block, ('core',) + COLUMN, route)  51.6 us
    all_to_all x4, starting transfers between devices, exchange(): return lax.all_to_all(values, axes, split_axis=0, concat_axis=0, tiled=True)  36.3 us
    ppermute x4, waiting for transfers between devices, swap(): return lax.ppermute(block, COLUMN, [(i, i ^ 1) for i in range(NZ)])  31.6 us
    all_to_all x4, waiting for transfers between devices, exchange(): return lax.all_to_all(values, axes, split_axis=0, concat_axis=0, tiled=True)  24 us
    ppermute x4, starting transfers between devices, swap(): return lax.ppermute(block, COLUMN, [(i, i ^ 1) for i in range(NZ)])  10.6 us
    pallas_call x1, Pallas kernels, on_device(): pl.pallas_call(expert_kernel, out_shape=(jax.ShapeDtypeStruct((ROWS, WIDE...  8.34 us
    pallas_call x1, Pallas kernels, on_device(): pl.pallas_call(weights_kernel, out_shape=(jax.ShapeDtypeStruct((BLK, D),...  5.43 us
  transfers between devices with their start and end apart: 20, of which 9 were waited for; matrix products, arithmetic and copies ran while one was open for 4% of the time, Pallas kernels for 5%

profile of v3, /device:TPU:1, one launch (start us, length us, event | category | flops | bytes accessed | tf_op | source)
XLA Modules:
  0.0 257.9 jit_solution(14863607174507394898)
XLA Ops:
  3.5 9.6 %collective-permute-start.1 = (bf16[32,2176]{1,0:T(8,128)(2,1)S(1)}, bf16[32,2176]{1,0:T(8,128)(2,1)S(1)}, u32[]{:S(2)}, u32[]{:S(2)}) collective-permute-start(bf16[32,2176]{1,0:T(8,128)(2,1)S(1)} %concatenate.20.refs_0_), channel_id=1, source_target_pairs={{0,12},{32,36},{1,13},{33,37},{2,14},{34,38},{3,15},{35,39},{4,0},... | collective-permute-start | bytes 417800 | tf_op jit(solution)/shard_map/ppermute | solution.py:58
  13.1 5.6 %collective-permute-start = (bf16[32,2176]{1,0:T(8,128)(2,1)S(1)}, bf16[32,2176]{1,0:T(8,128)(2,1)S(1)}, u32[]{:S(2)}, u32[]{:S(2)}) collective-permute-start(bf16[32,2176]{1,0:T(8,128)(2,1)S(1)} %concatenate.20.refs_0_), channel_id=1, source_target_pairs={{0,4},{32,44},{1,5},{33,45},{2,6},{34,46},{3,7},{35,47},{4,8},{36,... | collective-permute-start | bytes 417800 | tf_op jit(solution)/shard_map/ppermute | solution.py:58
  21.0 1.9 pack.1
  23.0 5.3 %collective-permute-done.refs_1_ = bf16[32,2176]{1,0:T(8,128)(2,1)S(1)} collective-permute-done((bf16[32,2176]{1,0:T(8,128)(2,1)S(1)}, bf16[32,2176]{1,0:T(8,128)(2,1)S(1)}, u32[]{:S(2)}, u32[]{:S(2)}) %collective-permute-start) | collective-permute-done | bytes 139296 | tf_op jit(solution)/shard_map/ppermute | solution.py:58
  28.3 10.8 %all-to-all-start = ((bf16[8,64,384]{2,1,0:T(8,128)(2,1)}), bf16[8,64,384]{2,1,0:T(8,128)(2,1)S(1)}, u32[]{:S(2)}, u32[]{:S(2)}) async-start(bf16[8,64,384]{2,1,0:T(8,128)(2,1)} %pack.1), calls=%async_computation | async-start | bytes 786432 | tf_op jit(solution)/shard_map/all_to_all | solution.py:66
  39.2 4.3 %collective-permute-start.5 = (bf16[64,2176]{1,0:T(8,128)(2,1)S(1)}, bf16[64,2176]{1,0:T(8,128)(2,1)S(1)}, u32[]{:S(2)}, u32[]{:S(2)}) collective-permute-start(bf16[64,2176]{1,0:T(8,128)(2,1)S(1)} %get-tuple-element.58), channel_id=1, source_target_pairs={{0,14},{32,34},{1,15},{33,35},{2,0},{34,36},{3,1},{35,37},{4,2},{3... | collective-permute-start | bytes 835592 | tf_op jit(solution)/shard_map/ppermute | solution.py:58
  43.5 3.1 %collective-permute-start.4 = (bf16[64,2176]{1,0:T(8,128)(2,1)S(1)}, bf16[64,2176]{1,0:T(8,128)(2,1)S(1)}, u32[]{:S(2)}, u32[]{:S(2)}) collective-permute-start(bf16[64,2176]{1,0:T(8,128)(2,1)S(1)} %get-tuple-element.59), channel_id=1, source_target_pairs={{0,2},{32,46},{1,3},{33,47},{2,4},{34,32},{3,5},{35,33},{4,6},{36,... | collective-permute-start | bytes 835592 | tf_op jit(solution)/shard_map/ppermute | solution.py:58
  46.7 7.3 %collective-permute-start.3 = (bf16[16,2176]{1,0:T(8,128)(2,1)S(1)}, bf16[16,2176]{1,0:T(8,128)(2,1)S(1)}, u32[]{:S(2)}, u32[]{:S(2)}) collective-permute-start(bf16[16,2176]{1,0:T(8,128)(2,1)S(1)} %slice.54), channel_id=1, source_target_pairs={{0,12},{32,36},{1,13},{33,37},{2,14},{34,38},{3,15},{35,39},{4,0},... | collective-permute-start | bytes 208904 | tf_op jit(solution)/shard_map/ppermute | solution.py:58
  56.6 4.4 %collective-permute-done.5.refs_6_ = bf16[64,2176]{1,0:T(8,128)(2,1)S(1)} collective-permute-done((bf16[64,2176]{1,0:T(8,128)(2,1)S(1)}, bf16[64,2176]{1,0:T(8,128)(2,1)S(1)}, u32[]{:S(2)}, u32[]{:S(2)}) %collective-permute-start.5) | collective-permute-done | bytes 278560 | tf_op jit(solution)/shard_map/ppermute | solution.py:58
  60.9 12.3 %collective-permute-done.4.refs_5_ = bf16[64,2176]{1,0:T(8,128)(2,1)S(1)} collective-permute-done((bf16[64,2176]{1,0:T(8,128)(2,1)S(1)}, bf16[64,2176]{1,0:T(8,128)(2,1)S(1)}, u32[]{:S(2)}, u32[]{:S(2)}) %collective-permute-start.4) | collective-permute-done | bytes 278560 | tf_op jit(solution)/shard_map/ppermute | solution.py:58
  73.2 5.0 %collective-permute-done.2.refs_3_ = bf16[16,2176]{1,0:T(8,128)(2,1)S(1)} collective-permute-done((bf16[16,2176]{1,0:T(8,128)(2,1)S(1)}, bf16[16,2176]{1,0:T(8,128)(2,1)S(1)}, u32[]{:S(2)}, u32[]{:S(2)}) %collective-permute-start.2) | collective-permute-done | bytes 69664 | tf_op jit(solution)/shard_map/ppermute | solution.py:58
  78.9 4.0 %select.7 = (bf16[512,2432]{1,0:T(8,128)(2,1)}, bf16[256,128]{1,0:T(8,128)(2,1)}) custom-call(s32[2]{0:T(128)} %pad_add_fusion.place, bf16[32,2176]{1,0:T(8,128)(2,1)} %copy-done.6, bf16[32,2176]{1,0:T(8,128)(2,1)} %copy-done.9, bf16[32,2176]{1,0:T(8,128)(2,1)} %copy-done.8, bf16[16,2176]{1,0:T(8,128)(2,1)} %copy-done.15, bf16[16,2176]{1,0:T(8,128)(2,1)} %copy-done.14, ...), custom_call_target="tpu_custom_call" | custom-call | tf_op jit(solution)/shard_map/select/pallas_call | solution.py:226
  82.9 10.1 %all-to-all-start.1 = ((bf16[32,16,2432]{2,1,0:T(8,128)(2,1)}), bf16[32,16,2432]{2,1,0:T(8,128)(2,1)S(1)}, u32[]{:S(2)}, u32[]{:S(2)}) async-start(bf16[32,16,2432]{2,1,0:T(8,128)(2,1)} %bitcast.17), calls=%async_computation.1 | async-start | bytes 4980736 | tf_op jit(solution)/shard_map/all_to_all | solution.py:66
  94.9 3.4 %collective-permute-start.7 = (bf16[192,2048]{1,0:T(8,128)(2,1)}, bf16[192,2048]{1,0:T(8,128)(2,1)}, u32[]{:S(2)}, u32[]{:S(2)}) collective-permute-start(bf16[192,2048]{1,0:T(8,128)(2,1)} %bitcast.22), channel_id=1, source_target_pairs={{0,1},{1,0},{2,3},{3,2},{4,5},{5,4},{6,7},{7,6},{8,9},{9,8},{10,11... | collective-permute-start | bytes 2359304 | tf_op jit(solution)/shard_map/ppermute | solution.py:62
  98.3 15.5 %collective-permute-done.6.gate_other = bf16[192,2048]{1,0:T(8,128)(2,1)S(1)} collective-permute-done((bf16[192,2048]{1,0:T(8,128)(2,1)S(1)}, bf16[192,2048]{1,0:T(8,128)(2,1)S(1)}, u32[]{:S(2)}, u32[]{:S(2)}) %collective-permute-start.6) | collective-permute-done | bytes 786464 | tf_op jit(solution)/shard_map/ppermute | solution.py:62
  114.7 16.1 %collective-permute-done.7.up_other = bf16[192,2048]{1,0:T(8,128)(2,1)} collective-permute-done((bf16[192,2048]{1,0:T(8,128)(2,1)}, bf16[192,2048]{1,0:T(8,128)(2,1)}, u32[]{:S(2)}, u32[]{:S(2)}) %collective-permute-start.7) | collective-permute-done | bytes 786464 | tf_op jit(solution)/shard_map/ppermute | solution.py:62
  132.3 8.3 %expert.1 = (bf16[512,2432]{1,0:T(8,128)(2,1)}, bf16[512,384]{1,0:T(8,128)(2,1)}, bf16[512,384]{1,0:T(8,128)(2,1)}) custom-call(s32[2]{0:T(128)} %pad_add_fusion.place, bf16[512,2432]{1,0:T(8,128)(2,1)} %bitcast.14, bf16[192,2048]{1,0:T(8,128)(2,1)} %bitcast.20, bf16[192,2048]{1,0:T(8,128)(2,1)} %copy-done.11, bf16[192,2048]{1,0:T(8,128)(2,1)} %bitcast.23, ...), custom_call_target="tpu_custom_call" | custom-call | tf_op jit(solution)/shard_map/expert/pallas_call | solution.py:246
  140.6 8.1 %all-to-all-start.2 = ((bf16[32,16,2432]{2,1,0:T(8,128)(2,1)}), bf16[32,16,2432]{2,1,0:T(8,128)(2,1)S(1)}, u32[]{:S(2)}, u32[]{:S(2)}) async-start(bf16[32,16,2432]{2,1,0:T(8,128)(2,1)} %bitcast.18), calls=%async_computation.2 | async-start | bytes 4980736 | tf_op jit(solution)/shard_map/all_to_all | solution.py:66
  148.7 5.4 %weights.1 = (f32[192,2048]{1,0:T(8,128)}, f32[192,2048]{1,0:T(8,128)}, bf16[192,2048]{1,0:T(8,128)(2,1)}, bf16[192,2048]{1,0:T(8,128)(2,1)}) custom-call(s32[2]{0:T(128)} %pad_add_fusion.place, bf16[512,2432]{1,0:T(8,128)(2,1)} %bitcast.15, bf16[512,384]{1,0:T(8,128)(2,1)} %get-tuple-element.39.d_gate, bf16[512,384]{1,0:T(8,128)(2,1)} %get-tuple-element.40.d_up), custom_call_target="tpu_custom_call" | custom-call | flops 1610612736 | bytes 7340032 | tf_op jit(solution)/shard_map/weights/pallas_call | solution.py:265
  156.0 3.4 %collective-permute-start.9 = (bf16[192,2048]{1,0:T(8,128)(2,1)}, bf16[192,2048]{1,0:T(8,128)(2,1)}, u32[]{:S(2)}, u32[]{:S(2)}) collective-permute-start(bf16[192,2048]{1,0:T(8,128)(2,1)} %get-tuple-element.42), channel_id=1, source_target_pairs={{0,1},{1,0},{2,3},{3,2},{4,5},{5,4},{6,7},{7,6},{8,9},{9,8},{10,11... | collective-permute-start | bytes 2359304 | tf_op jit(solution)/shard_map/ppermute | solution.py:62
  160.1 24.0 %all-to-all-done.2 = bf16[32,16,2432]{2,1,0:T(8,128)(2,1)S(1)} async-done(((bf16[32,16,2432]{2,1,0:T(8,128)(2,1)}), bf16[32,16,2432]{2,1,0:T(8,128)(2,1)S(1)}, u32[]{:S(2)}, u32[]{:S(2)}) %all-to-all-start.2) | async-done | bytes 2490400 | tf_op jit(solution)/shard_map/all_to_all | solution.py:66
  185.5 4.1 %combine.1 = (bf16[256,2048]{1,0:T(8,128)(2,1)}, bf16[512,384]{1,0:T(8,128)(2,1)}) custom-call(s32[2]{0:T(128)} %pad_add_fusion.place, bf16[256,128]{1,0:T(8,128)(2,1)} %get-tuple-element.33.codes, bf16[512,2432]{1,0:T(8,128)(2,1)} %bitcast.16), custom_call_target="tpu_custom_call" | custom-call | tf_op jit(solution)/shard_map/combine/pallas_call | solution.py:285
  189.7 7.3 %all-to-all-start.3 = ((bf16[8,64,384]{2,1,0:T(8,128)(2,1)}), bf16[8,64,384]{2,1,0:T(8,128)(2,1)S(1)}, u32[]{:S(2)}, u32[]{:S(2)}) async-start(bf16[8,64,384]{2,1,0:T(8,128)(2,1)} %bitcast.24), calls=%async_computation.3 | async-start | bytes 786432 | tf_op jit(solution)/shard_map/all_to_all | solution.py:66
  198.1 5.5 %collective-permute-start.13 = (bf16[64,2048]{1,0:T(8,128)(2,1)S(1)}, bf16[64,2048]{1,0:T(8,128)(2,1)S(1)}, u32[]{:S(2)}, u32[]{:S(2)}) collective-permute-start(bf16[64,2048]{1,0:T(8,128)(2,1)S(1)} %get-tuple-element.56), channel_id=1, source_target_pairs={{0,2},{32,46},{1,3},{33,47},{2,4},{34,32},{3,5},{35,33},{4,6},{36,... | collective-permute-start | bytes 786440 | tf_op jit(solution)/shard_map/ppermute | solution.py:58
  205.5 7.0 %collective-permute-start.14 = (bf16[16,2048]{1,0:T(8,128)(2,1)S(1)}, bf16[16,2048]{1,0:T(8,128)(2,1)S(1)}, u32[]{:S(2)}, u32[]{:S(2)}) collective-permute-start(bf16[16,2048]{1,0:T(8,128)(2,1)S(1)} %get-tuple-element.52), channel_id=1, source_target_pairs={{0,4},{32,44},{1,5},{33,45},{2,6},{34,46},{3,7},{35,47},{4,8},{36,... | collective-permute-start | bytes 196616 | tf_op jit(solution)/shard_map/ppermute | solution.py:58
  212.5 2.2 collective-permute-start.11
  214.7 16.9 %collective-permute-done.13 = bf16[64,2048]{1,0:T(8,128)(2,1)S(1)} collective-permute-done((bf16[64,2048]{1,0:T(8,128)(2,1)S(1)}, bf16[64,2048]{1,0:T(8,128)(2,1)S(1)}, u32[]{:S(2)}, u32[]{:S(2)}) %collective-permute-start.13) | collective-permute-done | bytes 262176 | tf_op jit(solution)/shard_map/ppermute | solution.py:58
  231.8 7.0 %collective-permute-start.12 = (bf16[32,2048]{1,0:T(8,128)(2,1)S(1)}, bf16[32,2048]{1,0:T(8,128)(2,1)}, u32[]{:S(2)}, u32[]{:S(2)}) collective-permute-start(bf16[32,2048]{1,0:T(8,128)(2,1)S(1)} %pad_maximum_fusion.2), channel_id=1, source_target_pairs={{0,12},{32,36},{1,13},{33,37},{2,14},{34,38},{3,15},{35,39},{4,0},... | collective-permute-start | bytes 393224 | tf_op jit(solution)/shard_map/ppermute | solution.py:58
  238.8 2.4 collective-permute-start.15
  241.2 2.8 %fusion = (bf16[1,192,2048]{2,1,0:T(8,128)(2,1)}, bf16[1,192,2048]{2,1,0:T(8,128)(2,1)}) fusion(f32[192,2048]{1,0:T(8,128)S(1)} %copy-done.4, bf16[192,2048]{1,0:T(8,128)(2,1)S(1)} %collective-permute-done.8, f32[192,2048]{1,0:T(8,128)S(1)} %copy-done.5, bf16[192,2048]{1,0:T(8,128)(2,1)} %collective-permute-done.9), kind=kLoop, calls=%fused_computation.2 | loop fusion | flops 2359296 | bytes 6291456 | tf_op jit(solution)/shard_map/broadcast_in_dim | solution.py:335
  244.8 2.0 unpack.1
  248.4 7.8 %collective-permute-done.15 = bf16[32,2048]{1,0:T(8,128)(2,1)} collective-permute-done((bf16[32,2048]{1,0:T(8,128)(2,1)S(1)}, bf16[32,2048]{1,0:T(8,128)(2,1)}, u32[]{:S(2)}, u32[]{:S(2)}) %collective-permute-start.15) | collective-permute-done | bytes 131104 | tf_op jit(solution)/shard_map/ppermute | solution.py:58
  (76 shorter events, 24.2 us)
Async XLA Ops:
  3.5 74.7 %copy-start.6 = (bf16[32,2176]{1,0:T(8,128)(2,1)}, bf16[32,2176]{1,0:T(8,128)(2,1)S(1)}, u32[]{:S(2)}) copy-start(bf16[32,2176]{1,0:T(8,128)(2,1)S(1)} %concatenate.20.refs_0_) | copy-start | bytes 417796
  3.5 19.5 %collective-permute-start.1 = (bf16[32,2176]{1,0:T(8,128)(2,1)S(1)}, bf16[32,2176]{1,0:T(8,128)(2,1)S(1)}, u32[]{:S(2)}, u32[]{:S(2)}) collective-permute-start(bf16[32,2176]{1,0:T(8,128)(2,1)S(1)} %concatenate.20.refs_0_), channel_id=1, source_target_pairs={{0,12},{32,36},{1,13},{33,37},{2,14},{34,38},{3,15},{35,39},{4,0},... | collective-permute-start | bytes 417800 | tf_op jit(solution)/shard_map/ppermute | solution.py:58
  13.1 15.2 %collective-permute-start = (bf16[32,2176]{1,0:T(8,128)(2,1)S(1)}, bf16[32,2176]{1,0:T(8,128)(2,1)S(1)}, u32[]{:S(2)}, u32[]{:S(2)}) collective-permute-start(bf16[32,2176]{1,0:T(8,128)(2,1)S(1)} %concatenate.20.refs_0_), channel_id=1, source_target_pairs={{0,4},{32,44},{1,5},{33,45},{2,6},{34,46},{3,7},{35,47},{4,8},{36,... | collective-permute-start | bytes 417800 | tf_op jit(solution)/shard_map/ppermute | solution.py:58
  23.0 55.2 %copy-start.8 = (bf16[32,2176]{1,0:T(8,128)(2,1)}, bf16[32,2176]{1,0:T(8,128)(2,1)S(1)}, u32[]{:S(2)}) copy-start(bf16[32,2176]{1,0:T(8,128)(2,1)S(1)} %collective-permute-done.1.refs_2_) | copy-start | bytes 417796
  28.3 49.9 %copy-start.9 = (bf16[32,2176]{1,0:T(8,128)(2,1)}, bf16[32,2176]{1,0:T(8,128)(2,1)S(1)}, u32[]{:S(2)}) copy-start(bf16[32,2176]{1,0:T(8,128)(2,1)S(1)} %collective-permute-done.refs_1_) | copy-start | bytes 417796
  28.3 49.8 %all-to-all-start = ((bf16[8,64,384]{2,1,0:T(8,128)(2,1)}), bf16[8,64,384]{2,1,0:T(8,128)(2,1)S(1)}, u32[]{:S(2)}, u32[]{:S(2)}) async-start(bf16[8,64,384]{2,1,0:T(8,128)(2,1)} %pack.1), calls=%async_computation | async-start | bytes 786432 | tf_op jit(solution)/shard_map/all_to_all | solution.py:66
  39.2 21.7 %collective-permute-start.5 = (bf16[64,2176]{1,0:T(8,128)(2,1)S(1)}, bf16[64,2176]{1,0:T(8,128)(2,1)S(1)}, u32[]{:S(2)}, u32[]{:S(2)}) collective-permute-start(bf16[64,2176]{1,0:T(8,128)(2,1)S(1)} %get-tuple-element.58), channel_id=1, source_target_pairs={{0,14},{32,34},{1,15},{33,35},{2,0},{34,36},{3,1},{35,37},{4,2},{3... | collective-permute-start | bytes 835592 | tf_op jit(solution)/shard_map/ppermute | solution.py:58
  43.5 29.7 %collective-permute-start.4 = (bf16[64,2176]{1,0:T(8,128)(2,1)S(1)}, bf16[64,2176]{1,0:T(8,128)(2,1)S(1)}, u32[]{:S(2)}, u32[]{:S(2)}) collective-permute-start(bf16[64,2176]{1,0:T(8,128)(2,1)S(1)} %get-tuple-element.59), channel_id=1, source_target_pairs={{0,2},{32,46},{1,3},{33,47},{2,4},{34,32},{3,5},{35,33},{4,6},{36,... | collective-permute-start | bytes 835592 | tf_op jit(solution)/shard_map/ppermute | solution.py:58
  46.7 26.5 %collective-permute-start.3 = (bf16[16,2176]{1,0:T(8,128)(2,1)S(1)}, bf16[16,2176]{1,0:T(8,128)(2,1)S(1)}, u32[]{:S(2)}, u32[]{:S(2)}) collective-permute-start(bf16[16,2176]{1,0:T(8,128)(2,1)S(1)} %slice.54), channel_id=1, source_target_pairs={{0,12},{32,36},{1,13},{33,37},{2,14},{34,38},{3,15},{35,39},{4,0},... | collective-permute-start | bytes 208904 | tf_op jit(solution)/shard_map/ppermute | solution.py:58
  54.0 24.2 %collective-permute-start.2 = (bf16[16,2176]{1,0:T(8,128)(2,1)S(1)}, bf16[16,2176]{1,0:T(8,128)(2,1)S(1)}, u32[]{:S(2)}, u32[]{:S(2)}) collective-permute-start(bf16[16,2176]{1,0:T(8,128)(2,1)S(1)} %slice.53), channel_id=1, source_target_pairs={{0,4},{32,44},{1,5},{33,45},{2,6},{34,46},{3,7},{35,47},{4,8},{36,... | collective-permute-start | bytes 208904 | tf_op jit(solution)/shard_map/ppermute | solution.py:58
  60.9 17.3 %copy-start.12 = (bf16[64,2176]{1,0:T(8,128)(2,1)}, bf16[64,2176]{1,0:T(8,128)(2,1)S(1)}, u32[]{:S(2)}) copy-start(bf16[64,2176]{1,0:T(8,128)(2,1)S(1)} %collective-permute-done.5.refs_6_) | copy-start | bytes 835588
  73.2 5.0 %copy-start.13 = (bf16[64,2176]{1,0:T(8,128)(2,1)}, bf16[64,2176]{1,0:T(8,128)(2,1)S(1)}, u32[]{:S(2)}) copy-start(bf16[64,2176]{1,0:T(8,128)(2,1)S(1)} %collective-permute-done.4.refs_5_) | copy-start | bytes 835588
  73.2 5.0 %copy-start.14 = (bf16[16,2176]{1,0:T(8,128)(2,1)}, bf16[16,2176]{1,0:T(8,128)(2,1)S(1)}, u32[]{:S(2)}) copy-start(bf16[16,2176]{1,0:T(8,128)(2,1)S(1)} %collective-permute-done.3.refs_4_) | copy-start | bytes 208900
  82.9 10.1 %copy-start.10 = (bf16[1,192,2048]{2,1,0:T(8,128)(2,1)S(1)}, bf16[1,192,2048]{2,1,0:T(8,128)(2,1)}, u32[]{:S(2)}) copy-start(bf16[1,192,2048]{2,1,0:T(8,128)(2,1)} %param.8) | copy-start | bytes 2359300
  82.9 47.9 %all-to-all-start.1 = ((bf16[32,16,2432]{2,1,0:T(8,128)(2,1)}), bf16[32,16,2432]{2,1,0:T(8,128)(2,1)S(1)}, u32[]{:S(2)}, u32[]{:S(2)}) async-start(bf16[32,16,2432]{2,1,0:T(8,128)(2,1)} %bitcast.17), calls=%async_computation.1 | async-start | bytes 4980736 | tf_op jit(solution)/shard_map/all_to_all | solution.py:66
  93.0 20.8 %collective-permute-start.6 = (bf16[192,2048]{1,0:T(8,128)(2,1)S(1)}, bf16[192,2048]{1,0:T(8,128)(2,1)S(1)}, u32[]{:S(2)}, u32[]{:S(2)}) collective-permute-start(bf16[192,2048]{1,0:T(8,128)(2,1)S(1)} %bitcast.21), channel_id=1, source_target_pairs={{0,1},{1,0},{2,3},{3,2},{4,5},{5,4},{6,7},{7,6},{8,9},{9,8},{10,11... | collective-permute-start | bytes 2359304 | tf_op jit(solution)/shard_map/ppermute | solution.py:62
  94.9 35.8 %collective-permute-start.7 = (bf16[192,2048]{1,0:T(8,128)(2,1)}, bf16[192,2048]{1,0:T(8,128)(2,1)}, u32[]{:S(2)}, u32[]{:S(2)}) collective-permute-start(bf16[192,2048]{1,0:T(8,128)(2,1)} %bitcast.22), channel_id=1, source_target_pairs={{0,1},{1,0},{2,3},{3,2},{4,5},{5,4},{6,7},{7,6},{8,9},{9,8},{10,11... | collective-permute-start | bytes 2359304 | tf_op jit(solution)/shard_map/ppermute | solution.py:62
  130.8 1.5 copy-start
  140.6 43.5 %all-to-all-start.2 = ((bf16[32,16,2432]{2,1,0:T(8,128)(2,1)}), bf16[32,16,2432]{2,1,0:T(8,128)(2,1)S(1)}, u32[]{:S(2)}, u32[]{:S(2)}) async-start(bf16[32,16,2432]{2,1,0:T(8,128)(2,1)} %bitcast.18), calls=%async_computation.2 | async-start | bytes 4980736 | tf_op jit(solution)/shard_map/all_to_all | solution.py:66
  154.1 42.9 %collective-permute-start.8 = (bf16[192,2048]{1,0:T(8,128)(2,1)}, bf16[192,2048]{1,0:T(8,128)(2,1)S(1)}, u32[]{:S(2)}, u32[]{:S(2)}) collective-permute-start(bf16[192,2048]{1,0:T(8,128)(2,1)} %get-tuple-element.41), channel_id=1, source_target_pairs={{0,1},{1,0},{2,3},{3,2},{4,5},{5,4},{6,7},{7,6},{8,9},{9,8},{10,11... | collective-permute-start | bytes 2359304 | tf_op jit(solution)/shard_map/ppermute | solution.py:62
  156.0 41.0 %collective-permute-start.9 = (bf16[192,2048]{1,0:T(8,128)(2,1)}, bf16[192,2048]{1,0:T(8,128)(2,1)}, u32[]{:S(2)}, u32[]{:S(2)}) collective-permute-start(bf16[192,2048]{1,0:T(8,128)(2,1)} %get-tuple-element.42), channel_id=1, source_target_pairs={{0,1},{1,0},{2,3},{3,2},{4,5},{5,4},{6,7},{7,6},{8,9},{9,8},{10,11... | collective-permute-start | bytes 2359304 | tf_op jit(solution)/shard_map/ppermute | solution.py:62
  184.1 1.4 copy-start.1
  189.7 15.8 %copy-start.7 = (bf16[256,2048]{1,0:T(8,128)(2,1)S(1)}, bf16[256,2048]{1,0:T(8,128)(2,1)}, u32[]{:S(2)}) copy-start(bf16[256,2048]{1,0:T(8,128)(2,1)} %get-tuple-element.44) | copy-start | bytes 3145732
  189.7 54.4 %all-to-all-start.3 = ((bf16[8,64,384]{2,1,0:T(8,128)(2,1)}), bf16[8,64,384]{2,1,0:T(8,128)(2,1)S(1)}, u32[]{:S(2)}, u32[]{:S(2)}) async-start(bf16[8,64,384]{2,1,0:T(8,128)(2,1)} %bitcast.24), calls=%async_computation.3 | async-start | bytes 786432 | tf_op jit(solution)/shard_map/all_to_all | solution.py:66
  198.1 33.5 %collective-permute-start.13 = (bf16[64,2048]{1,0:T(8,128)(2,1)S(1)}, bf16[64,2048]{1,0:T(8,128)(2,1)S(1)}, u32[]{:S(2)}, u32[]{:S(2)}) collective-permute-start(bf16[64,2048]{1,0:T(8,128)(2,1)S(1)} %get-tuple-element.56), channel_id=1, source_target_pairs={{0,2},{32,46},{1,3},{33,47},{2,4},{34,32},{3,5},{35,33},{4,6},{36,... | collective-permute-start | bytes 786440 | tf_op jit(solution)/shard_map/ppermute | solution.py:58
  203.5 28.1 %collective-permute-start.10 = (bf16[64,2048]{1,0:T(8,128)(2,1)S(1)}, bf16[64,2048]{1,0:T(8,128)(2,1)S(1)}, u32[]{:S(2)}, u32[]{:S(2)}) collective-permute-start(bf16[64,2048]{1,0:T(8,128)(2,1)S(1)} %get-tuple-element.57), channel_id=1, source_target_pairs={{0,14},{32,34},{1,15},{33,35},{2,0},{34,36},{3,1},{35,37},{4,2},{3... | collective-permute-start | bytes 786440 | tf_op jit(solution)/shard_map/ppermute | solution.py:58
  205.5 33.3 %collective-permute-start.14 = (bf16[16,2048]{1,0:T(8,128)(2,1)S(1)}, bf16[16,2048]{1,0:T(8,128)(2,1)S(1)}, u32[]{:S(2)}, u32[]{:S(2)}) collective-permute-start(bf16[16,2048]{1,0:T(8,128)(2,1)S(1)} %get-tuple-element.52), channel_id=1, source_target_pairs={{0,4},{32,44},{1,5},{33,45},{2,6},{34,46},{3,7},{35,47},{4,8},{36,... | collective-permute-start | bytes 196616 | tf_op jit(solution)/shard_map/ppermute | solution.py:58
  212.5 19.2 %collective-permute-start.11 = (bf16[16,2048]{1,0:T(8,128)(2,1)S(1)}, bf16[16,2048]{1,0:T(8,128)(2,1)S(1)}, u32[]{:S(2)}, u32[]{:S(2)}) collective-permute-start(bf16[16,2048]{1,0:T(8,128)(2,1)S(1)} %get-tuple-element.53), channel_id=1, source_target_pairs={{0,12},{32,36},{1,13},{33,37},{2,14},{34,38},{3,15},{35,39},{4,0},... | collective-permute-start | bytes 196616 | tf_op jit(solution)/shard_map/ppermute | solution.py:58
  231.6 9.6 %copy-start.4 = (f32[192,2048]{1,0:T(8,128)S(1)}, f32[192,2048]{1,0:T(8,128)}, u32[]{:S(2)}) copy-start(f32[192,2048]{1,0:T(8,128)} %get-tuple-element.48) | copy-start | bytes 4718596
  231.6 9.6 %copy-start.5 = (f32[192,2048]{1,0:T(8,128)S(1)}, f32[192,2048]{1,0:T(8,128)}, u32[]{:S(2)}) copy-start(f32[192,2048]{1,0:T(8,128)} %get-tuple-element.50) | copy-start | bytes 4718596
  231.8 16.6 %collective-permute-start.12 = (bf16[32,2048]{1,0:T(8,128)(2,1)S(1)}, bf16[32,2048]{1,0:T(8,128)(2,1)}, u32[]{:S(2)}, u32[]{:S(2)}) collective-permute-start(bf16[32,2048]{1,0:T(8,128)(2,1)S(1)} %pad_maximum_fusion.2), channel_id=1, source_target_pairs={{0,12},{32,36},{1,13},{33,37},{2,14},{34,38},{3,15},{35,39},{4,0},... | collective-permute-start | bytes 393224 | tf_op jit(solution)/shard_map/ppermute | solution.py:58
  238.8 17.4 %collective-permute-start.15 = (bf16[32,2048]{1,0:T(8,128)(2,1)S(1)}, bf16[32,2048]{1,0:T(8,128)(2,1)}, u32[]{:S(2)}, u32[]{:S(2)}) collective-permute-start(bf16[32,2048]{1,0:T(8,128)(2,1)S(1)} %pad_maximum_fusion.3), channel_id=1, source_target_pairs={{0,4},{32,44},{1,5},{33,45},{2,6},{34,46},{3,7},{35,47},{4,8},{36,... | collective-permute-start | bytes 393224 | tf_op jit(solution)/shard_map/ppermute | solution.py:58
  (4 other events, 3.0 us)

commit v4 on v3

--- a/solution.py
+++ b/solution.py
@@ -105,7 +105,7 @@
 
 
 def select_kernel(place, *refs):
-    pieces, dh, out, codes_out, held = refs[:7], refs[7], refs[8], refs[9], refs[10]
+    pieces, dh, out, codes_out, held = refs[:6], refs[6], refs[7], refs[8], refs[9]
     tile = out.shape[0]
 
     @pl.when(pl.program_id(0) == 0)
@@ -197,7 +197,6 @@
     ).astype(BF16)
     block = jnp.concatenate([tokens, codes], axis=1)
 
-    half = TOK // 2
     below, above = shift(block, 4), shift(block, -4)
 
     row_of = (expert_ids & 3) * SENT + (expert_ids >> 2) * CAP + rank
@@ -213,14 +212,14 @@
     dh = exchange(dh_send, EVEN).reshape(ROWS, PAIR)
     near_below = shift(jnp.concatenate([block, below]), 2)
     near_above = shift(jnp.concatenate([block, above]), -2)
-    far_below, far_above = shift(below[:half], 4), shift(above[half:], -4)
+    far = shift(above, -4)
 
     gate_own, up_own = gate_blocks[0], up_blocks[0]
     near_below, near_above, gate_out, up_out = lax.optimization_barrier(
         (near_below, near_above, gate_own, up_own)
     )
     gate_other, up_other = swap(gate_out), swap(up_out)
-    pieces = (block, below, above, far_below, far_above, near_below, near_above)
+    pieces = (block, below, above, far, near_below, near_above)
 
     tile = 256
     x_send, codes_all = pl.pallas_call(
@@ -308,16 +307,13 @@
 
     own, to_below, to_above = (part[i * TOK : (i + 1) * TOK].astype(F32) for i in range(3))
     at = 3 * TOK
-    far_up = shift(part[at : at + half], -4).astype(F32)
-    far_down = shift(part[at + half : at + TOK], 4).astype(F32)
+    far_down = shift(part[at : at + TOK], 4).astype(F32)
     at += TOK
     near_up, near_down = shift(part[at : at + 2 * TOK], -2), shift(part[at + 2 * TOK :], 2)
     near_up, near_down = near_up.astype(F32), near_down.astype(F32)
     own = own + near_up[:TOK] + near_down[:TOK]
     to_below = to_below + near_up[TOK:]
-    to_above = to_above + near_down[TOK:]
-    to_below = jnp.concatenate([to_below[:half] + far_up, to_below[half:]])
-    to_above = jnp.concatenate([to_above[:half], to_above[half:] + far_down])
+    to_above = to_above + near_down[TOK:] + far_down
     h_slots = exchange(h_send.reshape(HALF, SENT, PAIR), EVEN)
     hidden = pl.pallas_call(
         unpack_kernel,

time: 259 us -> 259 us (level)
  waiting for transfers between devices: 107 us -> 101 us
  local copies, waits for them, and re-layouts: 12.2 us -> 14.9 us
    ppermute x12 -> x10, waiting for transfers between devices: 51.6 us -> 45.1 us  [shift(): return lax.ppermute(block, ('core',) + COLUMN, route)]
    all_to_all x4, starting transfers between devices: 36.3 us -> 40.9 us  [exchange(): return lax.all_to_all(values, axes, split_axis=0, concat_axis=0, tiled=True)]
    ppermute x12 -> x10, starting transfers between devices: 57.7 us -> 53.6 us  [shift(): return lax.ppermute(block, ('core',) + COLUMN, route)]
    unnamed x32 -> x30, local copies, waits for them, and re-layouts: 5.32 us -> 5.44 us
  transfers between devices with their start and end apart: 20 -> 18, of which waited for: 9 -> 9; matrix products, arithmetic and copies ran while one was open for 4% -> 6% of each run, Pallas kernels for 5% -> 5%
where the time goes in v4:
time: 259 us; the launch traced here: 257 us
  starting transfers between devices  105 us (41%)
  waiting for transfers between devices  101 us (39%)
  Pallas kernels  25.8 us (10%)
  local copies, waits for them, and re-layouts  14.9 us (6%)
  other arithmetic  9.39 us (4%)
    ppermute x10, starting transfers between devices, shift(): return lax.ppermute(block, ('core',) + COLUMN, route)  53.6 us
    ppermute x10, waiting for transfers between devices, shift(): return lax.ppermute(block, ('core',) + COLUMN, route)  45.1 us
    all_to_all x4, starting transfers between devices, exchange(): return lax.all_to_all(values, axes, split_axis=0, concat_axis=0, tiled=True)  40.9 us
    ppermute x4, waiting for transfers between devices, swap(): return lax.ppermute(block, COLUMN, [(i, i ^ 1) for i in range(NZ)])  31.6 us
    all_to_all x4, waiting for transfers between devices, exchange(): return lax.all_to_all(values, axes, split_axis=0, concat_axis=0, tiled=True)  24.7 us
    ppermute x4, starting transfers between devices, swap(): return lax.ppermute(block, COLUMN, [(i, i ^ 1) for i in range(NZ)])  10.6 us
    pallas_call x1, Pallas kernels, on_device(): pl.pallas_call(expert_kernel, out_shape=(jax.ShapeDtypeStruct((ROWS, WIDE...  8.34 us
    pallas_call x1, Pallas kernels, on_device(): pl.pallas_call(weights_kernel, out_shape=(jax.ShapeDtypeStruct((BLK, D),...  5.44 us
  transfers between devices with their start and end apart: 18, of which 9 were waited for; matrix products, arithmetic and copies ran while one was open for 6% of the time, Pallas kernels for 5%

profile of v4, /device:TPU:1, one launch (start us, length us, event | category | flops | bytes accessed | tf_op | source)
XLA Modules:
  0.0 257.5 jit_solution(6096062364675822482)
XLA Ops:
  3.5 9.6 %collective-permute-start.1 = (bf16[32,2176]{1,0:T(8,128)(2,1)S(1)}, bf16[32,2176]{1,0:T(8,128)(2,1)S(1)}, u32[]{:S(2)}, u32[]{:S(2)}) collective-permute-start(bf16[32,2176]{1,0:T(8,128)(2,1)S(1)} %concatenate.12.refs_0_), channel_id=1, source_target_pairs={{0,12},{32,36},{1,13},{33,37},{2,14},{34,38},{3,15},{35,39},{4,0},... | collective-permute-start | bytes 417800 | tf_op jit(solution)/shard_map/ppermute | solution.py:58
  13.1 5.6 %collective-permute-start = (bf16[32,2176]{1,0:T(8,128)(2,1)S(1)}, bf16[32,2176]{1,0:T(8,128)(2,1)S(1)}, u32[]{:S(2)}, u32[]{:S(2)}) collective-permute-start(bf16[32,2176]{1,0:T(8,128)(2,1)S(1)} %concatenate.12.refs_0_), channel_id=1, source_target_pairs={{0,4},{32,44},{1,5},{33,45},{2,6},{34,46},{3,7},{35,47},{4,8},{36,... | collective-permute-start | bytes 417800 | tf_op jit(solution)/shard_map/ppermute | solution.py:58
  21.0 1.9 pack.1
  23.0 5.3 %collective-permute-done.refs_1_ = bf16[32,2176]{1,0:T(8,128)(2,1)S(1)} collective-permute-done((bf16[32,2176]{1,0:T(8,128)(2,1)S(1)}, bf16[32,2176]{1,0:T(8,128)(2,1)S(1)}, u32[]{:S(2)}, u32[]{:S(2)}) %collective-permute-start) | collective-permute-done | bytes 139296 | tf_op jit(solution)/shard_map/ppermute | solution.py:58
  28.3 10.8 %all-to-all-start = ((bf16[8,64,384]{2,1,0:T(8,128)(2,1)}), bf16[8,64,384]{2,1,0:T(8,128)(2,1)S(1)}, u32[]{:S(2)}, u32[]{:S(2)}) async-start(bf16[8,64,384]{2,1,0:T(8,128)(2,1)} %pack.1), calls=%async_computation | async-start | bytes 786432 | tf_op jit(solution)/shard_map/all_to_all | solution.py:66
  39.2 4.3 %collective-permute-start.4 = (bf16[64,2176]{1,0:T(8,128)(2,1)S(1)}, bf16[64,2176]{1,0:T(8,128)(2,1)S(1)}, u32[]{:S(2)}, u32[]{:S(2)}) collective-permute-start(bf16[64,2176]{1,0:T(8,128)(2,1)S(1)} %get-tuple-element.56), channel_id=1, source_target_pairs={{0,14},{32,34},{1,15},{33,35},{2,0},{34,36},{3,1},{35,37},{4,2},{3... | collective-permute-start | bytes 835592 | tf_op jit(solution)/shard_map/ppermute | solution.py:58
  43.5 3.1 %collective-permute-start.3 = (bf16[64,2176]{1,0:T(8,128)(2,1)S(1)}, bf16[64,2176]{1,0:T(8,128)(2,1)S(1)}, u32[]{:S(2)}, u32[]{:S(2)}) collective-permute-start(bf16[64,2176]{1,0:T(8,128)(2,1)S(1)} %get-tuple-element.57), channel_id=1, source_target_pairs={{0,2},{32,46},{1,3},{33,47},{2,4},{34,32},{3,5},{35,33},{4,6},{36,... | collective-permute-start | bytes 835592 | tf_op jit(solution)/shard_map/ppermute | solution.py:58
  46.6 7.3 %collective-permute-start.2 = (bf16[32,2176]{1,0:T(8,128)(2,1)S(1)}, bf16[32,2176]{1,0:T(8,128)(2,1)S(1)}, u32[]{:S(2)}, u32[]{:S(2)}) collective-permute-start(bf16[32,2176]{1,0:T(8,128)(2,1)S(1)} %collective-permute-done.1.refs_2_), channel_id=1, source_target_pairs={{0,12},{32,36},{1,13},{33,37},{2,14},{34,38},{3,15},{35,39},{4,0},... | collective-permute-start | bytes 417800 | tf_op jit(solution)/shard_map/ppermute | solution.py:58
  54.6 6.3 %collective-permute-done.4.refs_5_ = bf16[64,2176]{1,0:T(8,128)(2,1)S(1)} collective-permute-done((bf16[64,2176]{1,0:T(8,128)(2,1)S(1)}, bf16[64,2176]{1,0:T(8,128)(2,1)S(1)}, u32[]{:S(2)}, u32[]{:S(2)}) %collective-permute-start.4) | collective-permute-done | bytes 278560 | tf_op jit(solution)/shard_map/ppermute | solution.py:58
  60.9 12.4 %collective-permute-done.3.refs_4_ = bf16[64,2176]{1,0:T(8,128)(2,1)S(1)} collective-permute-done((bf16[64,2176]{1,0:T(8,128)(2,1)S(1)}, bf16[64,2176]{1,0:T(8,128)(2,1)S(1)}, u32[]{:S(2)}, u32[]{:S(2)}) %collective-permute-start.3) | collective-permute-done | bytes 278560 | tf_op jit(solution)/shard_map/ppermute | solution.py:58
  74.2 3.9 %select.7 = (bf16[512,2432]{1,0:T(8,128)(2,1)}, bf16[256,128]{1,0:T(8,128)(2,1)}) custom-call(s32[2]{0:T(128)} %pad_add_fusion.place, bf16[32,2176]{1,0:T(8,128)(2,1)} %copy-done.5, bf16[32,2176]{1,0:T(8,128)(2,1)} %copy-done.11, bf16[32,2176]{1,0:T(8,128)(2,1)} %copy-done.10, bf16[32,2176]{1,0:T(8,128)(2,1)} %copy-done.14, bf16[64,2176]{1,0:T(8,128)(2,1)} %copy-done.13, ...), custom_call_target="tpu_custom_call" | custom-call | tf_op jit(solution)/shard_map/select/pallas_call | solution.py:225
  78.1 14.3 %all-to-all-start.1 = ((bf16[32,16,2432]{2,1,0:T(8,128)(2,1)}), bf16[32,16,2432]{2,1,0:T(8,128)(2,1)S(1)}, u32[]{:S(2)}, u32[]{:S(2)}) async-start(bf16[32,16,2432]{2,1,0:T(8,128)(2,1)} %bitcast.17), calls=%async_computation.1 | async-start | bytes 4980736 | tf_op jit(solution)/shard_map/all_to_all | solution.py:66
  92.4 1.9 collective-permute-start.5
  94.4 3.4 %collective-permute-start.6 = (bf16[192,2048]{1,0:T(8,128)(2,1)}, bf16[192,2048]{1,0:T(8,128)(2,1)}, u32[]{:S(2)}, u32[]{:S(2)}) collective-permute-start(bf16[192,2048]{1,0:T(8,128)(2,1)} %bitcast.22), channel_id=1, source_target_pairs={{0,1},{1,0},{2,3},{3,2},{4,5},{5,4},{6,7},{7,6},{8,9},{9,8},{10,11... | collective-permute-start | bytes 2359304 | tf_op jit(solution)/shard_map/ppermute | solution.py:62
  97.7 15.5 %collective-permute-done.5.gate_other = bf16[192,2048]{1,0:T(8,128)(2,1)S(1)} collective-permute-done((bf16[192,2048]{1,0:T(8,128)(2,1)S(1)}, bf16[192,2048]{1,0:T(8,128)(2,1)S(1)}, u32[]{:S(2)}, u32[]{:S(2)}) %collective-permute-start.5) | collective-permute-done | bytes 786464 | tf_op jit(solution)/shard_map/ppermute | solution.py:62
  114.1 16.1 %collective-permute-done.6.up_other = bf16[192,2048]{1,0:T(8,128)(2,1)} collective-permute-done((bf16[192,2048]{1,0:T(8,128)(2,1)}, bf16[192,2048]{1,0:T(8,128)(2,1)}, u32[]{:S(2)}, u32[]{:S(2)}) %collective-permute-start.6) | collective-permute-done | bytes 786464 | tf_op jit(solution)/shard_map/ppermute | solution.py:62
  131.7 8.3 %expert.1 = (bf16[512,2432]{1,0:T(8,128)(2,1)}, bf16[512,384]{1,0:T(8,128)(2,1)}, bf16[512,384]{1,0:T(8,128)(2,1)}) custom-call(s32[2]{0:T(128)} %pad_add_fusion.place, bf16[512,2432]{1,0:T(8,128)(2,1)} %bitcast.14, bf16[192,2048]{1,0:T(8,128)(2,1)} %bitcast.20, bf16[192,2048]{1,0:T(8,128)(2,1)} %copy-done.9, bf16[192,2048]{1,0:T(8,128)(2,1)} %bitcast.23, ...), custom_call_target="tpu_custom_call" | custom-call | tf_op jit(solution)/shard_map/expert/pallas_call | solution.py:245
  140.1 8.1 %all-to-all-start.2 = ((bf16[32,16,2432]{2,1,0:T(8,128)(2,1)}), bf16[32,16,2432]{2,1,0:T(8,128)(2,1)S(1)}, u32[]{:S(2)}, u32[]{:S(2)}) async-start(bf16[32,16,2432]{2,1,0:T(8,128)(2,1)} %bitcast.18), calls=%async_computation.2 | async-start | bytes 4980736 | tf_op jit(solution)/shard_map/all_to_all | solution.py:66
  148.1 5.4 %weights.1 = (f32[192,2048]{1,0:T(8,128)}, f32[192,2048]{1,0:T(8,128)}, bf16[192,2048]{1,0:T(8,128)(2,1)}, bf16[192,2048]{1,0:T(8,128)(2,1)}) custom-call(s32[2]{0:T(128)} %pad_add_fusion.place, bf16[512,2432]{1,0:T(8,128)(2,1)} %bitcast.15, bf16[512,384]{1,0:T(8,128)(2,1)} %get-tuple-element.39.d_gate, bf16[512,384]{1,0:T(8,128)(2,1)} %get-tuple-element.40.d_up), custom_call_target="tpu_custom_call" | custom-call | flops 1610612736 | bytes 7340032 | tf_op jit(solution)/shard_map/weights/pallas_call | solution.py:264
  155.5 3.4 %collective-permute-start.8 = (bf16[192,2048]{1,0:T(8,128)(2,1)}, bf16[192,2048]{1,0:T(8,128)(2,1)}, u32[]{:S(2)}, u32[]{:S(2)}) collective-permute-start(bf16[192,2048]{1,0:T(8,128)(2,1)} %get-tuple-element.42), channel_id=1, source_target_pairs={{0,1},{1,0},{2,3},{3,2},{4,5},{5,4},{6,7},{7,6},{8,9},{9,8},{10,11... | collective-permute-start | bytes 2359304 | tf_op jit(solution)/shard_map/ppermute | solution.py:62
  158.9 24.7 %all-to-all-done.2 = bf16[32,16,2432]{2,1,0:T(8,128)(2,1)S(1)} async-done(((bf16[32,16,2432]{2,1,0:T(8,128)(2,1)}), bf16[32,16,2432]{2,1,0:T(8,128)(2,1)S(1)}, u32[]{:S(2)}, u32[]{:S(2)}) %all-to-all-start.2) | async-done | bytes 2490400 | tf_op jit(solution)/shard_map/all_to_all | solution.py:66
  185.0 4.2 %combine.1 = (bf16[256,2048]{1,0:T(8,128)(2,1)}, bf16[512,384]{1,0:T(8,128)(2,1)}) custom-call(s32[2]{0:T(128)} %pad_add_fusion.place, bf16[256,128]{1,0:T(8,128)(2,1)} %get-tuple-element.33.codes, bf16[512,2432]{1,0:T(8,128)(2,1)} %bitcast.16), custom_call_target="tpu_custom_call" | custom-call | tf_op jit(solution)/shard_map/combine/pallas_call | solution.py:284
  189.1 7.7 %all-to-all-start.3 = ((bf16[8,64,384]{2,1,0:T(8,128)(2,1)}), bf16[8,64,384]{2,1,0:T(8,128)(2,1)S(1)}, u32[]{:S(2)}, u32[]{:S(2)}) async-start(bf16[8,64,384]{2,1,0:T(8,128)(2,1)} %bitcast.24), calls=%async_computation.3 | async-start | bytes 786432 | tf_op jit(solution)/shard_map/all_to_all | solution.py:66
  196.9 2.1 fusion.8
  198.9 5.6 %collective-permute-start.11 = (bf16[64,2048]{1,0:T(8,128)(2,1)S(1)}, bf16[64,2048]{1,0:T(8,128)(2,1)}, u32[]{:S(2)}, u32[]{:S(2)}) collective-permute-start(bf16[64,2048]{1,0:T(8,128)(2,1)S(1)} %get-tuple-element.54), channel_id=1, source_target_pairs={{0,2},{32,46},{1,3},{33,47},{2,4},{34,32},{3,5},{35,33},{4,6},{36,... | collective-permute-start | bytes 786440 | tf_op jit(solution)/shard_map/ppermute | solution.py:58
  208.0 7.0 %collective-permute-start.12 = (bf16[32,2048]{1,0:T(8,128)(2,1)}, bf16[32,2048]{1,0:T(8,128)(2,1)}, u32[]{:S(2)}, u32[]{:S(2)}) collective-permute-start(bf16[32,2048]{1,0:T(8,128)(2,1)} %slice.36), channel_id=1, source_target_pairs={{0,4},{32,44},{1,5},{33,45},{2,6},{34,46},{3,7},{35,47},{4,8},{36,... | collective-permute-start | bytes 393224 | tf_op jit(solution)/shard_map/ppermute | solution.py:58
  215.8 15.6 %collective-permute-done.11 = bf16[64,2048]{1,0:T(8,128)(2,1)} collective-permute-done((bf16[64,2048]{1,0:T(8,128)(2,1)S(1)}, bf16[64,2048]{1,0:T(8,128)(2,1)}, u32[]{:S(2)}, u32[]{:S(2)}) %collective-permute-start.11) | collective-permute-done | bytes 262176 | tf_op jit(solution)/shard_map/ppermute | solution.py:58
  232.4 3.3 %collective-permute-done.12 = bf16[32,2048]{1,0:T(8,128)(2,1)} collective-permute-done((bf16[32,2048]{1,0:T(8,128)(2,1)}, bf16[32,2048]{1,0:T(8,128)(2,1)}, u32[]{:S(2)}, u32[]{:S(2)}) %collective-permute-start.12) | collective-permute-done | bytes 131104 | tf_op jit(solution)/shard_map/ppermute | solution.py:58
  238.7 7.3 %collective-permute-start.10 = (bf16[32,2048]{1,0:T(8,128)(2,1)S(1)}, bf16[32,2048]{1,0:T(8,128)(2,1)S(1)}, u32[]{:S(2)}, u32[]{:S(2)}) collective-permute-start(bf16[32,2048]{1,0:T(8,128)(2,1)S(1)} %get-tuple-element.53), channel_id=1, source_target_pairs={{0,12},{32,36},{1,13},{33,37},{2,14},{34,38},{3,15},{35,39},{4,0},... | collective-permute-start | bytes 393224 | tf_op jit(solution)/shard_map/ppermute | solution.py:58
  246.0 3.3 %fusion = (bf16[1,192,2048]{2,1,0:T(8,128)(2,1)}, bf16[1,192,2048]{2,1,0:T(8,128)(2,1)}) fusion(f32[192,2048]{1,0:T(8,128)S(1)} %copy-done.4, bf16[192,2048]{1,0:T(8,128)(2,1)S(1)} %copy-done.7, f32[192,2048]{1,0:T(8,128)} %get-tuple-element.50, bf16[192,2048]{1,0:T(8,128)(2,1)} %collective-permute-done.8), kind=kLoop, calls=%fused_computation.2 | loop fusion | flops 2359296 | bytes 6291456 | tf_op jit(solution)/shard_map/broadcast_in_dim | solution.py:331
  250.0 2.0 unpack.1
  253.6 2.2 collective-permute-done.10
  (62 shorter events, 24.7 us)
Async XLA Ops:
  3.5 69.9 %copy-start.5 = (bf16[32,2176]{1,0:T(8,128)(2,1)}, bf16[32,2176]{1,0:T(8,128)(2,1)S(1)}, u32[]{:S(2)}) copy-start(bf16[32,2176]{1,0:T(8,128)(2,1)S(1)} %concatenate.12.refs_0_) | copy-start | bytes 417796
  3.5 19.5 %collective-permute-start.1 = (bf16[32,2176]{1,0:T(8,128)(2,1)S(1)}, bf16[32,2176]{1,0:T(8,128)(2,1)S(1)}, u32[]{:S(2)}, u32[]{:S(2)}) collective-permute-start(bf16[32,2176]{1,0:T(8,128)(2,1)S(1)} %concatenate.12.refs_0_), channel_id=1, source_target_pairs={{0,12},{32,36},{1,13},{33,37},{2,14},{34,38},{3,15},{35,39},{4,0},... | collective-permute-start | bytes 417800 | tf_op jit(solution)/shard_map/ppermute | solution.py:58
  13.1 15.2 %collective-permute-start = (bf16[32,2176]{1,0:T(8,128)(2,1)S(1)}, bf16[32,2176]{1,0:T(8,128)(2,1)S(1)}, u32[]{:S(2)}, u32[]{:S(2)}) collective-permute-start(bf16[32,2176]{1,0:T(8,128)(2,1)S(1)} %concatenate.12.refs_0_), channel_id=1, source_target_pairs={{0,4},{32,44},{1,5},{33,45},{2,6},{34,46},{3,7},{35,47},{4,8},{36,... | collective-permute-start | bytes 417800 | tf_op jit(solution)/shard_map/ppermute | solution.py:58
  23.0 50.4 %copy-start.10 = (bf16[32,2176]{1,0:T(8,128)(2,1)}, bf16[32,2176]{1,0:T(8,128)(2,1)S(1)}, u32[]{:S(2)}) copy-start(bf16[32,2176]{1,0:T(8,128)(2,1)S(1)} %collective-permute-done.1.refs_2_) | copy-start | bytes 417796
  28.3 45.0 %copy-start.11 = (bf16[32,2176]{1,0:T(8,128)(2,1)}, bf16[32,2176]{1,0:T(8,128)(2,1)S(1)}, u32[]{:S(2)}) copy-start(bf16[32,2176]{1,0:T(8,128)(2,1)S(1)} %collective-permute-done.refs_1_) | copy-start | bytes 417796
  28.3 45.0 %all-to-all-start = ((bf16[8,64,384]{2,1,0:T(8,128)(2,1)}), bf16[8,64,384]{2,1,0:T(8,128)(2,1)S(1)}, u32[]{:S(2)}, u32[]{:S(2)}) async-start(bf16[8,64,384]{2,1,0:T(8,128)(2,1)} %pack.1), calls=%async_computation | async-start | bytes 786432 | tf_op jit(solution)/shard_map/all_to_all | solution.py:66
  39.2 21.7 %collective-permute-start.4 = (bf16[64,2176]{1,0:T(8,128)(2,1)S(1)}, bf16[64,2176]{1,0:T(8,128)(2,1)S(1)}, u32[]{:S(2)}, u32[]{:S(2)}) collective-permute-start(bf16[64,2176]{1,0:T(8,128)(2,1)S(1)} %get-tuple-element.56), channel_id=1, source_target_pairs={{0,14},{32,34},{1,15},{33,35},{2,0},{34,36},{3,1},{35,37},{4,2},{3... | collective-permute-start | bytes 835592 | tf_op jit(solution)/shard_map/ppermute | solution.py:58
  43.5 29.8 %collective-permute-start.3 = (bf16[64,2176]{1,0:T(8,128)(2,1)S(1)}, bf16[64,2176]{1,0:T(8,128)(2,1)S(1)}, u32[]{:S(2)}, u32[]{:S(2)}) collective-permute-start(bf16[64,2176]{1,0:T(8,128)(2,1)S(1)} %get-tuple-element.57), channel_id=1, source_target_pairs={{0,2},{32,46},{1,3},{33,47},{2,4},{34,32},{3,5},{35,33},{4,6},{36,... | collective-permute-start | bytes 835592 | tf_op jit(solution)/shard_map/ppermute | solution.py:58
  46.6 26.7 %collective-permute-start.2 = (bf16[32,2176]{1,0:T(8,128)(2,1)S(1)}, bf16[32,2176]{1,0:T(8,128)(2,1)S(1)}, u32[]{:S(2)}, u32[]{:S(2)}) collective-permute-start(bf16[32,2176]{1,0:T(8,128)(2,1)S(1)} %collective-permute-done.1.refs_2_), channel_id=1, source_target_pairs={{0,12},{32,36},{1,13},{33,37},{2,14},{34,38},{3,15},{35,39},{4,0},... | collective-permute-start | bytes 417800 | tf_op jit(solution)/shard_map/ppermute | solution.py:58
  60.9 12.4 %copy-start.12 = (bf16[64,2176]{1,0:T(8,128)(2,1)}, bf16[64,2176]{1,0:T(8,128)(2,1)S(1)}, u32[]{:S(2)}) copy-start(bf16[64,2176]{1,0:T(8,128)(2,1)S(1)} %collective-permute-done.4.refs_5_) | copy-start | bytes 835588
  73.3 0.8 copy-start.14
  73.3 0.9 copy-start.3
  78.1 14.3 %copy-start.8 = (bf16[1,192,2048]{2,1,0:T(8,128)(2,1)S(1)}, bf16[1,192,2048]{2,1,0:T(8,128)(2,1)}, u32[]{:S(2)}) copy-start(bf16[1,192,2048]{2,1,0:T(8,128)(2,1)} %param.8) | copy-start | bytes 2359300
  78.1 52.1 %all-to-all-start.1 = ((bf16[32,16,2432]{2,1,0:T(8,128)(2,1)}), bf16[32,16,2432]{2,1,0:T(8,128)(2,1)S(1)}, u32[]{:S(2)}, u32[]{:S(2)}) async-start(bf16[32,16,2432]{2,1,0:T(8,128)(2,1)} %bitcast.17), calls=%async_computation.1 | async-start | bytes 4980736 | tf_op jit(solution)/shard_map/all_to_all | solution.py:66
  92.4 20.8 %collective-permute-start.5 = (bf16[192,2048]{1,0:T(8,128)(2,1)S(1)}, bf16[192,2048]{1,0:T(8,128)(2,1)S(1)}, u32[]{:S(2)}, u32[]{:S(2)}) collective-permute-start(bf16[192,2048]{1,0:T(8,128)(2,1)S(1)} %bitcast.21), channel_id=1, source_target_pairs={{0,1},{1,0},{2,3},{3,2},{4,5},{5,4},{6,7},{7,6},{8,9},{9,8},{10,11... | collective-permute-start | bytes 2359304 | tf_op jit(solution)/shard_map/ppermute | solution.py:62
  94.4 35.8 %collective-permute-start.6 = (bf16[192,2048]{1,0:T(8,128)(2,1)}, bf16[192,2048]{1,0:T(8,128)(2,1)}, u32[]{:S(2)}, u32[]{:S(2)}) collective-permute-start(bf16[192,2048]{1,0:T(8,128)(2,1)} %bitcast.22), channel_id=1, source_target_pairs={{0,1},{1,0},{2,3},{3,2},{4,5},{5,4},{6,7},{7,6},{8,9},{9,8},{10,11... | collective-permute-start | bytes 2359304 | tf_op jit(solution)/shard_map/ppermute | solution.py:62
  113.2 0.9 copy-start.9
  130.2 1.5 copy-start
  140.1 43.5 %all-to-all-start.2 = ((bf16[32,16,2432]{2,1,0:T(8,128)(2,1)}), bf16[32,16,2432]{2,1,0:T(8,128)(2,1)S(1)}, u32[]{:S(2)}, u32[]{:S(2)}) async-start(bf16[32,16,2432]{2,1,0:T(8,128)(2,1)} %bitcast.18), calls=%async_computation.2 | async-start | bytes 4980736 | tf_op jit(solution)/shard_map/all_to_all | solution.py:66
  153.6 43.3 %collective-permute-start.7 = (bf16[192,2048]{1,0:T(8,128)(2,1)}, bf16[192,2048]{1,0:T(8,128)(2,1)S(1)}, u32[]{:S(2)}, u32[]{:S(2)}) collective-permute-start(bf16[192,2048]{1,0:T(8,128)(2,1)} %get-tuple-element.41), channel_id=1, source_target_pairs={{0,1},{1,0},{2,3},{3,2},{4,5},{5,4},{6,7},{7,6},{8,9},{9,8},{10,11... | collective-permute-start | bytes 2359304 | tf_op jit(solution)/shard_map/ppermute | solution.py:62
  155.5 41.4 %collective-permute-start.8 = (bf16[192,2048]{1,0:T(8,128)(2,1)}, bf16[192,2048]{1,0:T(8,128)(2,1)}, u32[]{:S(2)}, u32[]{:S(2)}) collective-permute-start(bf16[192,2048]{1,0:T(8,128)(2,1)} %get-tuple-element.42), channel_id=1, source_target_pairs={{0,1},{1,0},{2,3},{3,2},{4,5},{5,4},{6,7},{7,6},{8,9},{9,8},{10,11... | collective-permute-start | bytes 2359304 | tf_op jit(solution)/shard_map/ppermute | solution.py:62
  183.5 1.5 copy-start.1
  189.1 60.1 %all-to-all-start.3 = ((bf16[8,64,384]{2,1,0:T(8,128)(2,1)}), bf16[8,64,384]{2,1,0:T(8,128)(2,1)S(1)}, u32[]{:S(2)}, u32[]{:S(2)}) async-start(bf16[8,64,384]{2,1,0:T(8,128)(2,1)} %bitcast.24), calls=%async_computation.3 | async-start | bytes 786432 | tf_op jit(solution)/shard_map/all_to_all | solution.py:66
  196.9 35.5 %copy-start.6 = (bf16[192,2048]{1,0:T(8,128)(2,1)}, bf16[192,2048]{1,0:T(8,128)(2,1)S(1)}, u32[]{:S(2)}) copy-start(bf16[192,2048]{1,0:T(8,128)(2,1)S(1)} %collective-permute-done.7) | copy-start | bytes 2359300
  198.9 47.0 %copy-start.4 = (f32[192,2048]{1,0:T(8,128)S(1)}, f32[192,2048]{1,0:T(8,128)}, u32[]{:S(2)}) copy-start(f32[192,2048]{1,0:T(8,128)} %get-tuple-element.48) | copy-start | bytes 4718596
  198.9 32.4 %collective-permute-start.11 = (bf16[64,2048]{1,0:T(8,128)(2,1)S(1)}, bf16[64,2048]{1,0:T(8,128)(2,1)}, u32[]{:S(2)}, u32[]{:S(2)}) collective-permute-start(bf16[64,2048]{1,0:T(8,128)(2,1)S(1)} %get-tuple-element.54), channel_id=1, source_target_pairs={{0,2},{32,46},{1,3},{33,47},{2,4},{34,32},{3,5},{35,33},{4,6},{36,... | collective-permute-start | bytes 786440 | tf_op jit(solution)/shard_map/ppermute | solution.py:58
  204.6 27.8 %collective-permute-start.9 = (bf16[64,2048]{1,0:T(8,128)(2,1)}, bf16[64,2048]{1,0:T(8,128)(2,1)S(1)}, u32[]{:S(2)}, u32[]{:S(2)}) collective-permute-start(bf16[64,2048]{1,0:T(8,128)(2,1)} %get-tuple-element.55), channel_id=1, source_target_pairs={{0,14},{32,34},{1,15},{33,35},{2,0},{34,36},{3,1},{35,37},{4,2},{3... | collective-permute-start | bytes 786440 | tf_op jit(solution)/shard_map/ppermute | solution.py:58
  208.0 27.6 %collective-permute-start.12 = (bf16[32,2048]{1,0:T(8,128)(2,1)}, bf16[32,2048]{1,0:T(8,128)(2,1)}, u32[]{:S(2)}, u32[]{:S(2)}) collective-permute-start(bf16[32,2048]{1,0:T(8,128)(2,1)} %slice.36), channel_id=1, source_target_pairs={{0,4},{32,44},{1,5},{33,45},{2,6},{34,46},{3,7},{35,47},{4,8},{36,... | collective-permute-start | bytes 393224 | tf_op jit(solution)/shard_map/ppermute | solution.py:58
  232.4 13.6 %copy-start.7 = (bf16[192,2048]{1,0:T(8,128)(2,1)S(1)}, bf16[192,2048]{1,0:T(8,128)(2,1)}, u32[]{:S(2)}) copy-start(bf16[192,2048]{1,0:T(8,128)(2,1)} %copy-done.6) | copy-start | bytes 2359300
  236.8 16.8 %collective-permute-start.13 = (bf16[32,2048]{1,0:T(8,128)(2,1)S(1)}, bf16[32,2048]{1,0:T(8,128)(2,1)S(1)}, u32[]{:S(2)}, u32[]{:S(2)}) collective-permute-start(bf16[32,2048]{1,0:T(8,128)(2,1)S(1)} %get-tuple-element.52), channel_id=1, source_target_pairs={{0,4},{32,44},{1,5},{33,45},{2,6},{34,46},{3,7},{35,47},{4,8},{36,... | collective-permute-start | bytes 393224 | tf_op jit(solution)/shard_map/ppermute | solution.py:58
  238.7 17.1 %collective-permute-start.10 = (bf16[32,2048]{1,0:T(8,128)(2,1)S(1)}, bf16[32,2048]{1,0:T(8,128)(2,1)S(1)}, u32[]{:S(2)}, u32[]{:S(2)}) collective-permute-start(bf16[32,2048]{1,0:T(8,128)(2,1)S(1)} %get-tuple-element.53), channel_id=1, source_target_pairs={{0,12},{32,36},{1,13},{33,37},{2,14},{34,38},{3,15},{35,39},{4,0},... | collective-permute-start | bytes 393224 | tf_op jit(solution)/shard_map/ppermute | solution.py:58
  249.3 0.7 copy-start.2
  (1 other events, 0.7 us)

commit v5 on v4

--- a/solution.py
+++ b/solution.py
@@ -215,10 +215,10 @@
     far = shift(above, -4)
 
     gate_own, up_own = gate_blocks[0], up_blocks[0]
-    near_below, near_above, gate_out, up_out = lax.optimization_barrier(
-        (near_below, near_above, gate_own, up_own)
+    near_below, near_above, w_out = lax.optimization_barrier(
+        (near_below, near_above, jnp.concatenate([gate_own, up_own]))
     )
-    gate_other, up_other = swap(gate_out), swap(up_out)
+    w_other = swap(w_out)
     pieces = (block, below, above, far, near_below, near_above)
 
     tile = 256
@@ -250,12 +250,13 @@
             jax.ShapeDtypeStruct((ROWS, PAIR), BF16),
         ),
         grid=(ROWS // tile,),
-        in_specs=[smem(), by_rows] + [pl.BlockSpec((BLK, D), whole)] * 4,
+        in_specs=[smem(), by_rows] + [pl.BlockSpec((BLK, D), whole), pl.BlockSpec((BLK, D), whole)]
+        + [pl.BlockSpec((BLK, D), whole), pl.BlockSpec((BLK, D), lambda i: (1, 0))],
         out_specs=(by_rows, by_rows_d, by_rows_d),
         scratch_shapes=[pltpu.VMEM((PAIR, D), BF16)] * 2,
         compiler_params=params(),
         name="expert",
-    )(place, x_all, gate_own, gate_other, up_own, up_other)
+    )(place, x_all, gate_own, w_other, up_own, w_other)
 
     returned = exchange(back.reshape(NQ, PER, WIDE), PLANE).reshape(ROWS, WIDE)
 

time: 259 us -> 258 us (level)
  starting transfers between devices: 105 us -> 99 us
  waiting for transfers between devices: 101 us -> 106 us
    ppermute x4 -> x3, waiting for transfers between devices: 31.6 us -> 36 us  [swap(): return lax.ppermute(block, COLUMN, [(i, i ^ 1) for i in range(NZ)])]
    ppermute x4 -> x3, starting transfers between devices: 10.6 us -> 7.19 us  [swap(): return lax.ppermute(block, COLUMN, [(i, i ^ 1) for i in range(NZ)])]
    all_to_all x4, starting transfers between devices: 40.9 us -> 38.1 us  [exchange(): return lax.all_to_all(values, axes, split_axis=0, concat_axis=0, tiled=True)]
    unnamed x30 -> x28, local copies, waits for them, and re-layouts: 5.44 us -> 5.43 us
  transfers between devices with their start and end apart: 18 -> 17, of which waited for: 9 -> 7; matrix products, arithmetic and copies ran while one was open for 6% -> 5% of each run, Pallas kernels for 5% -> 5%
where the time goes in v5:
time: 258 us; the launch traced here: 255 us
  waiting for transfers between devices  106 us (41%)
  starting transfers between devices  99 us (38%)
  Pallas kernels  25.7 us (10%)
  local copies, waits for them, and re-layouts  14 us (5%)
  other arithmetic  9.57 us (4%)
    ppermute x10, starting transfers between devices, shift(): return lax.ppermute(block, ('core',) + COLUMN, route)  53.7 us
    ppermute x10, waiting for transfers between devices, shift(): return lax.ppermute(block, ('core',) + COLUMN, route)  45.6 us
    all_to_all x4, starting transfers between devices, exchange(): return lax.all_to_all(values, axes, split_axis=0, concat_axis=0, tiled=True)  38.1 us
    ppermute x3, waiting for transfers between devices, swap(): return lax.ppermute(block, COLUMN, [(i, i ^ 1) for i in range(NZ)])  36 us
    all_to_all x4, waiting for transfers between devices, exchange(): return lax.all_to_all(values, axes, split_axis=0, concat_axis=0, tiled=True)  24.7 us
    pallas_call x1, Pallas kernels, on_device(): pl.pallas_call(expert_kernel, out_shape=(jax.ShapeDtypeStruct((ROWS, WIDE...  8.33 us
    ppermute x3, starting transfers between devices, swap(): return lax.ppermute(block, COLUMN, [(i, i ^ 1) for i in range(NZ)])  7.19 us
    unnamed x28, local copies, waits for them, and re-layouts  5.43 us
  transfers between devices with their start and end apart: 17, of which 7 were waited for; matrix products, arithmetic and copies ran while one was open for 5% of the time, Pallas kernels for 5%

profile of v5, /device:TPU:1, one launch (start us, length us, event | category | flops | bytes accessed | tf_op | source)
XLA Modules:
  0.0 255.5 jit_solution(15938918616837007063)
XLA Ops:
  3.6 9.6 %collective-permute-start.1 = (bf16[32,2176]{1,0:T(8,128)(2,1)S(1)}, bf16[32,2176]{1,0:T(8,128)(2,1)S(1)}, u32[]{:S(2)}, u32[]{:S(2)}) collective-permute-start(bf16[32,2176]{1,0:T(8,128)(2,1)S(1)} %concatenate.15.refs_0_), channel_id=1, source_target_pairs={{0,12},{32,36},{1,13},{33,37},{2,14},{34,38},{3,15},{35,39},{4,0},... | collective-permute-start | bytes 417800 | tf_op jit(solution)/shard_map/ppermute | solution.py:58
  13.2 5.6 %collective-permute-start = (bf16[32,2176]{1,0:T(8,128)(2,1)S(1)}, bf16[32,2176]{1,0:T(8,128)(2,1)S(1)}, u32[]{:S(2)}, u32[]{:S(2)}) collective-permute-start(bf16[32,2176]{1,0:T(8,128)(2,1)S(1)} %concatenate.15.refs_0_), channel_id=1, source_target_pairs={{0,4},{32,44},{1,5},{33,45},{2,6},{34,46},{3,7},{35,47},{4,8},{36,... | collective-permute-start | bytes 417800 | tf_op jit(solution)/shard_map/ppermute | solution.py:58
  21.1 1.9 pack.1
  23.1 5.3 %collective-permute-done.refs_1_ = bf16[32,2176]{1,0:T(8,128)(2,1)S(1)} collective-permute-done((bf16[32,2176]{1,0:T(8,128)(2,1)S(1)}, bf16[32,2176]{1,0:T(8,128)(2,1)S(1)}, u32[]{:S(2)}, u32[]{:S(2)}) %collective-permute-start) | collective-permute-done | bytes 139296 | tf_op jit(solution)/shard_map/ppermute | solution.py:58
  28.4 10.8 %all-to-all-start = ((bf16[8,64,384]{2,1,0:T(8,128)(2,1)}), bf16[8,64,384]{2,1,0:T(8,128)(2,1)S(1)}, u32[]{:S(2)}, u32[]{:S(2)}) async-start(bf16[8,64,384]{2,1,0:T(8,128)(2,1)} %pack.1), calls=%async_computation | async-start | bytes 786432 | tf_op jit(solution)/shard_map/all_to_all | solution.py:66
  39.3 7.3 %collective-permute-start.2 = (bf16[32,2176]{1,0:T(8,128)(2,1)S(1)}, bf16[32,2176]{1,0:T(8,128)(2,1)}, u32[]{:S(2)}, u32[]{:S(2)}) collective-permute-start(bf16[32,2176]{1,0:T(8,128)(2,1)S(1)} %collective-permute-done.1.refs_2_), channel_id=1, source_target_pairs={{0,12},{32,36},{1,13},{33,37},{2,14},{34,38},{3,15},{35,39},{4,0},... | collective-permute-start | bytes 417800 | tf_op jit(solution)/shard_map/ppermute | solution.py:58
  46.6 4.0 %collective-permute-start.4 = (bf16[64,2176]{1,0:T(8,128)(2,1)S(1)}, bf16[64,2176]{1,0:T(8,128)(2,1)S(1)}, u32[]{:S(2)}, u32[]{:S(2)}) collective-permute-start(bf16[64,2176]{1,0:T(8,128)(2,1)S(1)} %get-tuple-element.54), channel_id=1, source_target_pairs={{0,14},{32,34},{1,15},{33,35},{2,0},{34,36},{3,1},{35,37},{4,2},{3... | collective-permute-start | bytes 835592 | tf_op jit(solution)/shard_map/ppermute | solution.py:58
  50.6 3.4 %collective-permute-start.3 = (bf16[64,2176]{1,0:T(8,128)(2,1)S(1)}, bf16[64,2176]{1,0:T(8,128)(2,1)S(1)}, u32[]{:S(2)}, u32[]{:S(2)}) collective-permute-start(bf16[64,2176]{1,0:T(8,128)(2,1)S(1)} %get-tuple-element.55), channel_id=1, source_target_pairs={{0,2},{32,46},{1,3},{33,47},{2,4},{34,32},{3,5},{35,33},{4,6},{36,... | collective-permute-start | bytes 835592 | tf_op jit(solution)/shard_map/ppermute | solution.py:58
  55.9 8.1 %collective-permute-done.4.refs_5_ = bf16[64,2176]{1,0:T(8,128)(2,1)S(1)} collective-permute-done((bf16[64,2176]{1,0:T(8,128)(2,1)S(1)}, bf16[64,2176]{1,0:T(8,128)(2,1)S(1)}, u32[]{:S(2)}, u32[]{:S(2)}) %collective-permute-start.4) | collective-permute-done | bytes 278560 | tf_op jit(solution)/shard_map/ppermute | solution.py:58
  64.0 12.1 %collective-permute-done.3.refs_4_ = bf16[64,2176]{1,0:T(8,128)(2,1)S(1)} collective-permute-done((bf16[64,2176]{1,0:T(8,128)(2,1)S(1)}, bf16[64,2176]{1,0:T(8,128)(2,1)S(1)}, u32[]{:S(2)}, u32[]{:S(2)}) %collective-permute-start.3) | collective-permute-done | bytes 278560 | tf_op jit(solution)/shard_map/ppermute | solution.py:58
  76.9 3.9 %select.7 = (bf16[512,2432]{1,0:T(8,128)(2,1)}, bf16[256,128]{1,0:T(8,128)(2,1)}) custom-call(s32[2]{0:T(128)} %pad_add_fusion.place, bf16[32,2176]{1,0:T(8,128)(2,1)} %copy-done.7, bf16[32,2176]{1,0:T(8,128)(2,1)} %copy-done.11, bf16[32,2176]{1,0:T(8,128)(2,1)} %copy-done.10, bf16[32,2176]{1,0:T(8,128)(2,1)} %collective-permute-done.2.refs_3_, ...), custom_call_target="tpu_custom_call" | custom-call | tf_op jit(solution)/shard_map/select/pallas_call | solution.py:225
  80.9 11.4 %all-to-all-start.1 = ((bf16[32,16,2432]{2,1,0:T(8,128)(2,1)}), bf16[32,16,2432]{2,1,0:T(8,128)(2,1)S(1)}, u32[]{:S(2)}, u32[]{:S(2)}) async-start(bf16[32,16,2432]{2,1,0:T(8,128)(2,1)} %bitcast.22), calls=%async_computation.1 | async-start | bytes 4980736 | tf_op jit(solution)/shard_map/all_to_all | solution.py:66
  92.2 1.9 collective-permute-start.5
  94.1 36.0 %collective-permute-done.5.gate_other.up_other = bf16[384,2048]{1,0:T(8,128)(2,1)} collective-permute-done((bf16[384,2048]{1,0:T(8,128)(2,1)}, bf16[384,2048]{1,0:T(8,128)(2,1)}, u32[]{:S(2)}, u32[]{:S(2)}) %collective-permute-start.5) | collective-permute-done | bytes 1572896 | tf_op jit(solution)/shard_map/ppermute | solution.py:62
  131.7 8.3 %expert.1 = (bf16[512,2432]{1,0:T(8,128)(2,1)}, bf16[512,384]{1,0:T(8,128)(2,1)}, bf16[512,384]{1,0:T(8,128)(2,1)}) custom-call(s32[2]{0:T(128)} %pad_add_fusion.place, bf16[512,2432]{1,0:T(8,128)(2,1)} %bitcast.14, bf16[192,2048]{1,0:T(8,128)(2,1)} %bitcast.17, bf16[384,2048]{1,0:T(8,128)(2,1)} %collective-permute-done.5.gate_other.up_other, ...), custom_call_target="tpu_custom_call" | custom-call | tf_op jit(solution)/shard_map/expert/pallas_call | solution.py:245
  140.0 8.1 %all-to-all-start.2 = ((bf16[32,16,2432]{2,1,0:T(8,128)(2,1)}), bf16[32,16,2432]{2,1,0:T(8,128)(2,1)S(1)}, u32[]{:S(2)}, u32[]{:S(2)}) async-start(bf16[32,16,2432]{2,1,0:T(8,128)(2,1)} %bitcast.21), calls=%async_computation.2 | async-start | bytes 4980736 | tf_op jit(solution)/shard_map/all_to_all | solution.py:66
  148.1 5.4 %weights.1 = (f32[192,2048]{1,0:T(8,128)}, f32[192,2048]{1,0:T(8,128)}, bf16[192,2048]{1,0:T(8,128)(2,1)}, bf16[192,2048]{1,0:T(8,128)(2,1)}) custom-call(s32[2]{0:T(128)} %pad_add_fusion.place, bf16[512,2432]{1,0:T(8,128)(2,1)} %bitcast.15, bf16[512,384]{1,0:T(8,128)(2,1)} %get-tuple-element.37.d_gate, bf16[512,384]{1,0:T(8,128)(2,1)} %get-tuple-element.38.d_up), custom_call_target="tpu_custom_call" | custom-call | flops 1610612736 | bytes 7340032 | tf_op jit(solution)/shard_map/weights/pallas_call | solution.py:265
  153.6 1.9 collective-permute-start.6
  155.5 3.4 %collective-permute-start.7 = (bf16[192,2048]{1,0:T(8,128)(2,1)}, bf16[192,2048]{1,0:T(8,128)(2,1)}, u32[]{:S(2)}, u32[]{:S(2)}) collective-permute-start(bf16[192,2048]{1,0:T(8,128)(2,1)} %get-tuple-element.40), channel_id=1, source_target_pairs={{0,1},{1,0},{2,3},{3,2},{4,5},{5,4},{6,7},{7,6},{8,9},{9,8},{10,11... | collective-permute-start | bytes 2359304 | tf_op jit(solution)/shard_map/ppermute | solution.py:62
  158.8 24.7 %all-to-all-done.2 = bf16[32,16,2432]{2,1,0:T(8,128)(2,1)S(1)} async-done(((bf16[32,16,2432]{2,1,0:T(8,128)(2,1)}), bf16[32,16,2432]{2,1,0:T(8,128)(2,1)S(1)}, u32[]{:S(2)}, u32[]{:S(2)}) %all-to-all-start.2) | async-done | bytes 2490400 | tf_op jit(solution)/shard_map/all_to_all | solution.py:66
  185.0 4.1 %combine.1 = (bf16[256,2048]{1,0:T(8,128)(2,1)}, bf16[512,384]{1,0:T(8,128)(2,1)}) custom-call(s32[2]{0:T(128)} %pad_add_fusion.place, bf16[256,128]{1,0:T(8,128)(2,1)} %get-tuple-element.32.codes, bf16[512,2432]{1,0:T(8,128)(2,1)} %bitcast.16), custom_call_target="tpu_custom_call" | custom-call | tf_op jit(solution)/shard_map/combine/pallas_call | solution.py:285
  189.1 7.8 %all-to-all-start.3 = ((bf16[8,64,384]{2,1,0:T(8,128)(2,1)}), bf16[8,64,384]{2,1,0:T(8,128)(2,1)S(1)}, u32[]{:S(2)}, u32[]{:S(2)}) async-start(bf16[8,64,384]{2,1,0:T(8,128)(2,1)} %bitcast.24), calls=%async_computation.3 | async-start | bytes 786432 | tf_op jit(solution)/shard_map/all_to_all | solution.py:66
  198.9 5.6 %collective-permute-start.10 = (bf16[64,2048]{1,0:T(8,128)(2,1)S(1)}, bf16[64,2048]{1,0:T(8,128)(2,1)S(1)}, u32[]{:S(2)}, u32[]{:S(2)}) collective-permute-start(bf16[64,2048]{1,0:T(8,128)(2,1)S(1)} %get-tuple-element.52), channel_id=1, source_target_pairs={{0,2},{32,46},{1,3},{33,47},{2,4},{34,32},{3,5},{35,33},{4,6},{36,... | collective-permute-start | bytes 786440 | tf_op jit(solution)/shard_map/ppermute | solution.py:58
  204.5 1.9 collective-permute-start.8
  208.0 7.0 %collective-permute-start.11 = (bf16[32,2048]{1,0:T(8,128)(2,1)}, bf16[32,2048]{1,0:T(8,128)(2,1)S(1)}, u32[]{:S(2)}, u32[]{:S(2)}) collective-permute-start(bf16[32,2048]{1,0:T(8,128)(2,1)} %slice.36), channel_id=1, source_target_pairs={{0,4},{32,44},{1,5},{33,45},{2,6},{34,46},{3,7},{35,47},{4,8},{36,... | collective-permute-start | bytes 393224 | tf_op jit(solution)/shard_map/ppermute | solution.py:58
  215.7 15.5 %collective-permute-done.10 = bf16[64,2048]{1,0:T(8,128)(2,1)S(1)} collective-permute-done((bf16[64,2048]{1,0:T(8,128)(2,1)S(1)}, bf16[64,2048]{1,0:T(8,128)(2,1)S(1)}, u32[]{:S(2)}, u32[]{:S(2)}) %collective-permute-start.10) | collective-permute-done | bytes 262176 | tf_op jit(solution)/shard_map/ppermute | solution.py:58
  231.3 4.5 %collective-permute-done.11 = bf16[32,2048]{1,0:T(8,128)(2,1)S(1)} collective-permute-done((bf16[32,2048]{1,0:T(8,128)(2,1)}, bf16[32,2048]{1,0:T(8,128)(2,1)S(1)}, u32[]{:S(2)}, u32[]{:S(2)}) %collective-permute-start.11) | collective-permute-done | bytes 131104 | tf_op jit(solution)/shard_map/ppermute | solution.py:58
  236.9 1.9 collective-permute-start.12
  238.8 7.4 %collective-permute-start.9 = (bf16[32,2048]{1,0:T(8,128)(2,1)S(1)}, bf16[32,2048]{1,0:T(8,128)(2,1)S(1)}, u32[]{:S(2)}, u32[]{:S(2)}) collective-permute-start(bf16[32,2048]{1,0:T(8,128)(2,1)S(1)} %get-tuple-element.51), channel_id=1, source_target_pairs={{0,12},{32,36},{1,13},{33,37},{2,14},{34,38},{3,15},{35,39},{4,0},... | collective-permute-start | bytes 393224 | tf_op jit(solution)/shard_map/ppermute | solution.py:58
  246.2 3.3 %fusion = (bf16[1,192,2048]{2,1,0:T(8,128)(2,1)}, bf16[1,192,2048]{2,1,0:T(8,128)(2,1)}) fusion(f32[192,2048]{1,0:T(8,128)S(1)} %copy-done.6, bf16[192,2048]{1,0:T(8,128)(2,1)S(1)} %copy-done.9, f32[192,2048]{1,0:T(8,128)} %get-tuple-element.48, bf16[192,2048]{1,0:T(8,128)(2,1)} %collective-permute-done.7), kind=kLoop, calls=%fused_computation.3 | loop fusion | flops 2359296 | bytes 6291456 | tf_op jit(solution)/shard_map/broadcast_in_dim | solution.py:332
  250.2 2.0 unpack.1
  252.2 1.7 reshape.64
  (59 shorter events, 18.7 us)
Async XLA Ops:
  2.3 51.7 %copy-start.2 = (bf16[1,192,2048]{2,1,0:T(8,128)(2,1)S(1)}, bf16[1,192,2048]{2,1,0:T(8,128)(2,1)}, u32[]{:S(2)}) copy-start(bf16[1,192,2048]{2,1,0:T(8,128)(2,1)} %param.8) | copy-start | bytes 2359300
  2.4 51.7 %copy-start.3 = (bf16[1,192,2048]{2,1,0:T(8,128)(2,1)S(1)}, bf16[1,192,2048]{2,1,0:T(8,128)(2,1)}, u32[]{:S(2)}) copy-start(bf16[1,192,2048]{2,1,0:T(8,128)(2,1)} %param.9) | copy-start | bytes 2359300
  3.6 51.7 %copy-start.7 = (bf16[32,2176]{1,0:T(8,128)(2,1)}, bf16[32,2176]{1,0:T(8,128)(2,1)S(1)}, u32[]{:S(2)}) copy-start(bf16[32,2176]{1,0:T(8,128)(2,1)S(1)} %concatenate.15.refs_0_) | copy-start | bytes 417796
  3.6 19.5 %collective-permute-start.1 = (bf16[32,2176]{1,0:T(8,128)(2,1)S(1)}, bf16[32,2176]{1,0:T(8,128)(2,1)S(1)}, u32[]{:S(2)}, u32[]{:S(2)}) collective-permute-start(bf16[32,2176]{1,0:T(8,128)(2,1)S(1)} %concatenate.15.refs_0_), channel_id=1, source_target_pairs={{0,12},{32,36},{1,13},{33,37},{2,14},{34,38},{3,15},{35,39},{4,0},... | collective-permute-start | bytes 417800 | tf_op jit(solution)/shard_map/ppermute | solution.py:58
  13.2 15.2 %collective-permute-start = (bf16[32,2176]{1,0:T(8,128)(2,1)S(1)}, bf16[32,2176]{1,0:T(8,128)(2,1)S(1)}, u32[]{:S(2)}, u32[]{:S(2)}) collective-permute-start(bf16[32,2176]{1,0:T(8,128)(2,1)S(1)} %concatenate.15.refs_0_), channel_id=1, source_target_pairs={{0,4},{32,44},{1,5},{33,45},{2,6},{34,46},{3,7},{35,47},{4,8},{36,... | collective-permute-start | bytes 417800 | tf_op jit(solution)/shard_map/ppermute | solution.py:58
  23.1 32.2 %copy-start.10 = (bf16[32,2176]{1,0:T(8,128)(2,1)}, bf16[32,2176]{1,0:T(8,128)(2,1)S(1)}, u32[]{:S(2)}) copy-start(bf16[32,2176]{1,0:T(8,128)(2,1)S(1)} %collective-permute-done.1.refs_2_) | copy-start | bytes 417796
  28.4 26.9 %copy-start.11 = (bf16[32,2176]{1,0:T(8,128)(2,1)}, bf16[32,2176]{1,0:T(8,128)(2,1)S(1)}, u32[]{:S(2)}) copy-start(bf16[32,2176]{1,0:T(8,128)(2,1)S(1)} %collective-permute-done.refs_1_) | copy-start | bytes 417796
  28.4 47.7 %all-to-all-start = ((bf16[8,64,384]{2,1,0:T(8,128)(2,1)}), bf16[8,64,384]{2,1,0:T(8,128)(2,1)S(1)}, u32[]{:S(2)}, u32[]{:S(2)}) async-start(bf16[8,64,384]{2,1,0:T(8,128)(2,1)} %pack.1), calls=%async_computation | async-start | bytes 786432 | tf_op jit(solution)/shard_map/all_to_all | solution.py:66
  39.3 36.8 %collective-permute-start.2 = (bf16[32,2176]{1,0:T(8,128)(2,1)S(1)}, bf16[32,2176]{1,0:T(8,128)(2,1)}, u32[]{:S(2)}, u32[]{:S(2)}) collective-permute-start(bf16[32,2176]{1,0:T(8,128)(2,1)S(1)} %collective-permute-done.1.refs_2_), channel_id=1, source_target_pairs={{0,12},{32,36},{1,13},{33,37},{2,14},{34,38},{3,15},{35,39},{4,0},... | collective-permute-start | bytes 417800 | tf_op jit(solution)/shard_map/ppermute | solution.py:58
  46.6 17.4 %collective-permute-start.4 = (bf16[64,2176]{1,0:T(8,128)(2,1)S(1)}, bf16[64,2176]{1,0:T(8,128)(2,1)S(1)}, u32[]{:S(2)}, u32[]{:S(2)}) collective-permute-start(bf16[64,2176]{1,0:T(8,128)(2,1)S(1)} %get-tuple-element.54), channel_id=1, source_target_pairs={{0,14},{32,34},{1,15},{33,35},{2,0},{34,36},{3,1},{35,37},{4,2},{3... | collective-permute-start | bytes 835592 | tf_op jit(solution)/shard_map/ppermute | solution.py:58
  50.6 25.5 %collective-permute-start.3 = (bf16[64,2176]{1,0:T(8,128)(2,1)S(1)}, bf16[64,2176]{1,0:T(8,128)(2,1)S(1)}, u32[]{:S(2)}, u32[]{:S(2)}) collective-permute-start(bf16[64,2176]{1,0:T(8,128)(2,1)S(1)} %get-tuple-element.55), channel_id=1, source_target_pairs={{0,2},{32,46},{1,3},{33,47},{2,4},{34,32},{3,5},{35,33},{4,6},{36,... | collective-permute-start | bytes 835592 | tf_op jit(solution)/shard_map/ppermute | solution.py:58
  64.0 12.1 %copy-start.12 = (bf16[64,2176]{1,0:T(8,128)(2,1)}, bf16[64,2176]{1,0:T(8,128)(2,1)S(1)}, u32[]{:S(2)}) copy-start(bf16[64,2176]{1,0:T(8,128)(2,1)S(1)} %collective-permute-done.4.refs_5_) | copy-start | bytes 835588
  76.1 0.7 copy-start.13
  76.1 0.8 copy-start.5
  80.9 49.3 %all-to-all-start.1 = ((bf16[32,16,2432]{2,1,0:T(8,128)(2,1)}), bf16[32,16,2432]{2,1,0:T(8,128)(2,1)S(1)}, u32[]{:S(2)}, u32[]{:S(2)}) async-start(bf16[32,16,2432]{2,1,0:T(8,128)(2,1)} %bitcast.22), calls=%async_computation.1 | async-start | bytes 4980736 | tf_op jit(solution)/shard_map/all_to_all | solution.py:66
  92.2 38.0 %collective-permute-start.5 = (bf16[384,2048]{1,0:T(8,128)(2,1)}, bf16[384,2048]{1,0:T(8,128)(2,1)}, u32[]{:S(2)}, u32[]{:S(2)}) collective-permute-start(bf16[384,2048]{1,0:T(8,128)(2,1)} %pad_maximum_fusion), channel_id=1, source_target_pairs={{0,1},{1,0},{2,3},{3,2},{4,5},{5,4},{6,7},{7,6},{8,9},{9,8},{10,11... | collective-permute-start | bytes 4718600 | tf_op jit(solution)/shard_map/ppermute | solution.py:62
  130.2 1.5 copy-start
  140.0 43.5 %all-to-all-start.2 = ((bf16[32,16,2432]{2,1,0:T(8,128)(2,1)}), bf16[32,16,2432]{2,1,0:T(8,128)(2,1)S(1)}, u32[]{:S(2)}, u32[]{:S(2)}) async-start(bf16[32,16,2432]{2,1,0:T(8,128)(2,1)} %bitcast.21), calls=%async_computation.2 | async-start | bytes 4980736 | tf_op jit(solution)/shard_map/all_to_all | solution.py:66
  153.6 43.4 %collective-permute-start.6 = (bf16[192,2048]{1,0:T(8,128)(2,1)}, bf16[192,2048]{1,0:T(8,128)(2,1)S(1)}, u32[]{:S(2)}, u32[]{:S(2)}) collective-permute-start(bf16[192,2048]{1,0:T(8,128)(2,1)} %get-tuple-element.39), channel_id=1, source_target_pairs={{0,1},{1,0},{2,3},{3,2},{4,5},{5,4},{6,7},{7,6},{8,9},{9,8},{10,11... | collective-permute-start | bytes 2359304 | tf_op jit(solution)/shard_map/ppermute | solution.py:62
  155.5 41.5 %collective-permute-start.7 = (bf16[192,2048]{1,0:T(8,128)(2,1)}, bf16[192,2048]{1,0:T(8,128)(2,1)}, u32[]{:S(2)}, u32[]{:S(2)}) collective-permute-start(bf16[192,2048]{1,0:T(8,128)(2,1)} %get-tuple-element.40), channel_id=1, source_target_pairs={{0,1},{1,0},{2,3},{3,2},{4,5},{5,4},{6,7},{7,6},{8,9},{9,8},{10,11... | collective-permute-start | bytes 2359304 | tf_op jit(solution)/shard_map/ppermute | solution.py:62
  183.5 1.5 copy-start.1
  189.1 60.4 %all-to-all-start.3 = ((bf16[8,64,384]{2,1,0:T(8,128)(2,1)}), bf16[8,64,384]{2,1,0:T(8,128)(2,1)S(1)}, u32[]{:S(2)}, u32[]{:S(2)}) async-start(bf16[8,64,384]{2,1,0:T(8,128)(2,1)} %bitcast.24), calls=%async_computation.3 | async-start | bytes 786432 | tf_op jit(solution)/shard_map/all_to_all | solution.py:66
  197.0 0.9 copy-start.8
  198.9 47.3 %copy-start.6 = (f32[192,2048]{1,0:T(8,128)S(1)}, f32[192,2048]{1,0:T(8,128)}, u32[]{:S(2)}) copy-start(f32[192,2048]{1,0:T(8,128)} %get-tuple-element.46) | copy-start | bytes 4718596
  198.9 32.3 %collective-permute-start.10 = (bf16[64,2048]{1,0:T(8,128)(2,1)S(1)}, bf16[64,2048]{1,0:T(8,128)(2,1)S(1)}, u32[]{:S(2)}, u32[]{:S(2)}) collective-permute-start(bf16[64,2048]{1,0:T(8,128)(2,1)S(1)} %get-tuple-element.52), channel_id=1, source_target_pairs={{0,2},{32,46},{1,3},{33,47},{2,4},{34,32},{3,5},{35,33},{4,6},{36,... | collective-permute-start | bytes 786440 | tf_op jit(solution)/shard_map/ppermute | solution.py:58
  204.5 26.7 %collective-permute-start.8 = (bf16[64,2048]{1,0:T(8,128)(2,1)S(1)}, bf16[64,2048]{1,0:T(8,128)(2,1)S(1)}, u32[]{:S(2)}, u32[]{:S(2)}) collective-permute-start(bf16[64,2048]{1,0:T(8,128)(2,1)S(1)} %get-tuple-element.53), channel_id=1, source_target_pairs={{0,14},{32,34},{1,15},{33,35},{2,0},{34,36},{3,1},{35,37},{4,2},{3... | collective-permute-start | bytes 786440 | tf_op jit(solution)/shard_map/ppermute | solution.py:58
  208.0 27.8 %collective-permute-start.11 = (bf16[32,2048]{1,0:T(8,128)(2,1)}, bf16[32,2048]{1,0:T(8,128)(2,1)S(1)}, u32[]{:S(2)}, u32[]{:S(2)}) collective-permute-start(bf16[32,2048]{1,0:T(8,128)(2,1)} %slice.36), channel_id=1, source_target_pairs={{0,4},{32,44},{1,5},{33,45},{2,6},{34,46},{3,7},{35,47},{4,8},{36,... | collective-permute-start | bytes 393224 | tf_op jit(solution)/shard_map/ppermute | solution.py:58
  215.7 30.5 %copy-start.9 = (bf16[192,2048]{1,0:T(8,128)(2,1)S(1)}, bf16[192,2048]{1,0:T(8,128)(2,1)}, u32[]{:S(2)}) copy-start(bf16[192,2048]{1,0:T(8,128)(2,1)} %copy-done.8) | copy-start | bytes 2359300
  236.9 17.0 %collective-permute-start.12 = (bf16[32,2048]{1,0:T(8,128)(2,1)S(1)}, bf16[32,2048]{1,0:T(8,128)(2,1)S(1)}, u32[]{:S(2)}, u32[]{:S(2)}) collective-permute-start(bf16[32,2048]{1,0:T(8,128)(2,1)S(1)} %get-tuple-element.50), channel_id=1, source_target_pairs={{0,4},{32,44},{1,5},{33,45},{2,6},{34,46},{3,7},{35,47},{4,8},{36,... | collective-permute-start | bytes 393224 | tf_op jit(solution)/shard_map/ppermute | solution.py:58
  238.8 15.0 %collective-permute-start.9 = (bf16[32,2048]{1,0:T(8,128)(2,1)S(1)}, bf16[32,2048]{1,0:T(8,128)(2,1)S(1)}, u32[]{:S(2)}, u32[]{:S(2)}) collective-permute-start(bf16[32,2048]{1,0:T(8,128)(2,1)S(1)} %get-tuple-element.51), channel_id=1, source_target_pairs={{0,12},{32,36},{1,13},{33,37},{2,14},{34,38},{3,15},{35,39},{4,0},... | collective-permute-start | bytes 393224 | tf_op jit(solution)/shard_map/ppermute | solution.py:58
  249.5 0.7 copy-start.4
